TPU v7x, 256 devices: a whole 4x4x8 slice. The times are simulated.
256 devices in a mesh: batch: 2 (over x_lo), ctx: 32 (over z, y), tp: 4 (over x_hi, core).
Axes of the slice: x: 4 (x_hi: 2, x_lo: 2; x = x_hi * 2 + x_lo), y: 4, z: 8, core: 2. Of those that a mesh axis runs over, the one named last changes fastest.
Arguments:
- frames: bfloat16 [12288, 1536], P(('batch', 'ctx'), 'tp'), parts along dimension 0, may hold values from -6 to 6
- attn_gain: float32 [1536], replicated, may hold values from 0.5 to 1.5
- query_key_value: bfloat16 [3, 1536, 1536], P(None, None, 'tp'), may hold values from -1 to 1
- out_weight: bfloat16 [1536, 1536], P('tp'), may hold values from -6 to 6
- conv_gain: float32 [1536], replicated, may hold values from 0.5 to 1.5
- glu_weight: bfloat16 [2, 1536, 1536], P(None, None, 'tp'), may hold values from -0.15625 to 0.15625
- depth_kernel: bfloat16 [31, 1536], P(None, 'tp'), may hold values from -1 to 1
- depth_bias: float32 [1536], P('tp'), may hold values from -4 to 4
- proj_weight: bfloat16 [1536, 1536], P('tp'), may hold values from -0.15625 to 0.15625
Outputs:
- layer_out: bfloat16 [12288, 1536], P(('batch', 'ctx'), 'tp'), parts along dimension 0
There are 2 independent parts, one for each index of `batch`. A program takes and returns all parts, laid end to end along the dimension named above; an argument that names none is the same for every part. Nothing has to cross between parts.
All inputs are finite; a program needn't handle non-finite values.
Results may differ from a plain program's by a relative error of at most 0.019.
Values may be sent and summed in bfloat16 or wider, within the bound.
No kernel may reach another device: no remote copies, remote signals or barrier semaphores. Data moves between devices by JAX's collectives and lax.ppermute only.
A program may use at most 128 MiB of HBM per device.

v0:
```python
import math

import jax
import jax.numpy as jnp
from jax import lax
from jax.sharding import PartitionSpec as P

HEAD = 96


def layer_norm(inputs, gain):
    inputs = inputs.astype(jnp.float32)
    average = jnp.mean(inputs, axis=-1, keepdims=True)
    centered = inputs - average
    variance = jnp.mean(centered * centered, axis=-1, keepdims=True)
    return (centered * lax.rsqrt(variance + 1e-05) * gain).astype(jnp.bfloat16)


def depthwise(padded, kernel, bias, count):
    convolved = jnp.zeros((count, padded.shape[1]), jnp.float32)
    for kernel_tap in range(kernel.shape[0]):
        convolved = convolved + padded[kernel_tap : kernel_tap + count].astype(
            jnp.float32
        ) * kernel[kernel_tap].astype(jnp.float32)
    return jax.nn.silu(convolved + bias).astype(jnp.bfloat16)


def per_device(
    frames,
    attn_gain,
    query_key_value,
    out_weight,
    conv_gain,
    glu_weight,
    depth_kernel,
    depth_bias,
    proj_weight,
):
    frame_rows = frames.shape[0]
    local_cols = frames.shape[1]
    heads_here = query_key_value.shape[2] // HEAD
    whole_rows = lax.all_gather(frames, "tp", axis=1, tiled=True)
    normed = layer_norm(whole_rows, attn_gain)
    projected = jnp.einsum(
        "td,gdc->gtc", normed, query_key_value, preferred_element_type=jnp.float32
    ).astype(jnp.bfloat16)
    score_scale = 1.0 / math.sqrt(HEAD)
    query_heads = projected[0].reshape(frame_rows, heads_here, HEAD)
    initial = (
        jnp.full((heads_here, frame_rows), -1e30, jnp.float32),
        jnp.zeros((heads_here, frame_rows), jnp.float32),
        jnp.zeros((frame_rows, heads_here, HEAD), jnp.float32),
    )
    pieces = (
        lax.all_gather(projected[1], "ctx", axis=0, tiled=True),
        lax.all_gather(projected[2], "ctx", axis=0, tiled=True),
    )
    key_count = pieces[0].shape[0]
    block_len = 1024
    key_blocks = pieces[0].reshape(key_count // block_len, block_len, heads_here, HEAD)
    value_blocks = pieces[1].reshape(key_count // block_len, block_len, heads_here, HEAD)

    def one_block(running, pieces_now):
        running_max, denominator, weighted = running
        key_block, value_block = pieces_now
        scores = (
            jnp.einsum("qhd,khd->hqk", query_heads, key_block, preferred_element_type=jnp.float32)
            * score_scale
        )
        new_max = jnp.maximum(running_max, jnp.max(scores, axis=-1))
        weights = jnp.exp(scores - new_max[:, :, None])
        rescale = jnp.exp(running_max - new_max)
        denominator = denominator * rescale + jnp.sum(weights, axis=-1)
        added = jnp.einsum(
            "hqk,khd->qhd",
            weights.astype(jnp.bfloat16),
            value_block,
            preferred_element_type=jnp.float32,
        )
        weighted = weighted * jnp.transpose(rescale)[:, :, None] + added
        return ((new_max, denominator, weighted), None)

    result, _ = lax.scan(one_block, initial, (key_blocks, value_blocks))
    running_max, denominator, weighted = result
    context = (
        (weighted / jnp.transpose(denominator)[:, :, None])
        .reshape(frame_rows, local_cols)
        .astype(jnp.bfloat16)
    )
    attn_terms = jnp.dot(context, out_weight, preferred_element_type=jnp.float32)
    summed = lax.psum(attn_terms.astype(jnp.bfloat16), "tp").astype(jnp.float32)
    middle_whole = (whole_rows.astype(jnp.float32) + summed).astype(jnp.bfloat16)
    middle = lax.dynamic_slice_in_dim(
        middle_whole, lax.axis_index("tp") * local_cols, local_cols, 1
    )
    normed_conv = layer_norm(middle_whole, conv_gain)
    halves = jnp.einsum("td,gdc->gtc", normed_conv, glu_weight, preferred_element_type=jnp.float32)
    glu = (halves[0] * jax.nn.sigmoid(halves[1])).astype(jnp.bfloat16)
    reach = depth_kernel.shape[0] // 2
    regrouped = lax.all_to_all(glu, "ctx", split_axis=1, concat_axis=0, tiled=True)
    group_cols = regrouped.shape[1]
    offset_cols = lax.axis_index("ctx") * group_cols
    kernel_part = lax.dynamic_slice_in_dim(depth_kernel, offset_cols, group_cols, 1)
    bias_part = lax.dynamic_slice_in_dim(depth_bias, offset_cols, group_cols, 0)
    padded = jnp.pad(regrouped, ((reach, reach), (0, 0)))
    activated_part = depthwise(padded, kernel_part, bias_part, regrouped.shape[0])
    activated = lax.all_to_all(activated_part, "ctx", split_axis=0, concat_axis=1, tiled=True)
    conv_terms = jnp.dot(activated, proj_weight, preferred_element_type=jnp.float32)
    conv_sum = lax.psum_scatter(
        conv_terms.astype(jnp.bfloat16), "tp", scatter_dimension=1, tiled=True
    ).astype(jnp.float32)
    return (middle.astype(jnp.float32) + conv_sum).astype(jnp.bfloat16)


def solution(mesh):
    in_specs = (
        P(("batch", "ctx"), "tp"),
        P(),
        P(None, None, "tp"),
        P("tp", None),
        P(),
        P(None, None, "tp"),
        P(None, "tp"),
        P("tp"),
        P("tp", None),
    )
    out_specs = P(("batch", "ctx"), "tp")
    return jax.shard_map(
        per_device, mesh=mesh, in_specs=in_specs, out_specs=out_specs, check_vma=False
    )
```

profile of v0, /device:TPU:56, one launch (start us, length us, event | category | flops | bytes accessed | tf_op | source)
XLA Modules:
  0.0 414.8 jit_solution(18295216857343930924)
XLA Ops:
  6.5 9.4 %all_gather.9 = bf16[192,1536]{1,0:T(8,128)(2,1)S(1)} all-gather(bf16[192,384]{1,0:T(8,128)(2,1)} %param.11), channel_id=1, replica_groups=mesh['batch'=2,'ctx'=32,'tp'=4] {'tp'}, dimensions={1}, use_global_device_ids=true | all-gather | bytes 737280 | tf_op jit(solution)/shard_map/all_gather | solution.py:42
  22.4 79.6 %all-gather.5.cloned.1.call-done = bf16[1,6144,384]{2,1,0:T(8,128)(2,1)} async-done(((bf16[1,192,384]{2,1,0:T(8,128)(2,1)}), bf16[1,6144,384]{2,1,0:T(8,128)(2,1)}) %all-gather.5.cloned.1.call-update) | async-done | bytes 4718608 | tf_op jit(solution)/shard_map/all_gather | solution.py:55
  102.0 12.4 %reshape.93 = bf16[6,1024,4,96]{3,2,1,0:T(4,128)(2,1)} reshape(bf16[1,6144,384]{2,1,0:T(8,128)(2,1)} %all-gather.5.cloned.1.call-done) | data formatting | bytes 9437184 | tf_op jit(solution)/shard_map/reshape | solution.py:60
  114.4 10.2 %copy.23 = bf16[6,1024,4,96]{1,3,2,0:T(8,128)(2,1)} copy(bf16[6,1024,4,96]{3,2,1,0:T(4,128)(2,1)} %reshape.93) | data formatting | bytes 9437184
  124.6 60.8 %all-gather.7.cloned.1.call-done = bf16[1,6144,384]{2,1,0:T(8,128)(2,1)} async-done(((bf16[1,192,384]{2,1,0:T(8,128)(2,1)}), bf16[1,6144,384]{2,1,0:T(8,128)(2,1)}) %all-gather.7.cloned.1.call-update) | async-done | bytes 4718608 | tf_op jit(solution)/shard_map/all_gather | solution.py:56
  185.4 12.4 %reshape.94 = bf16[6,1024,4,96]{3,2,1,0:T(4,128)(2,1)} reshape(bf16[1,6144,384]{2,1,0:T(8,128)(2,1)} %all-gather.7.cloned.1.call-done) | data formatting | bytes 9437184 | tf_op jit(solution)/shard_map/reshape | solution.py:61
  197.8 10.2 %copy.25 = bf16[6,1024,4,96]{1,3,2,0:T(8,128)(2,1)} copy(bf16[6,1024,4,96]{3,2,1,0:T(4,128)(2,1)} %reshape.94) | data formatting | bytes 9437184
  208.0 48.8 %while.15 = (s32[]{:T(128)}, f32[4,192]{1,0:T(4,128)S(1)}, f32[4,192]{1,0:T(4,128)S(1)}, f32[192,4,96]{0,2,1:T(8,128)}, bf16[6,1024,4,96]{1,3,2,0:T(8,128)(2,1)}...) while((s32[]{:T(128)}, f32[4,192]{1,0:T(4,128)S(1)}, ...), condition=%wide.region_5.6_spmd.clone, body=%wide.region_2.5_spmd.clone.sunk | while | flops 308507136 | bytes 24528004 | solution.py:83
  211.4 3.8 fusion.103
  216.0 3.5 bitcast_reduce_fusion.2
  219.5 3.9 fusion.103
  224.2 3.4 bitcast_reduce_fusion.2
  227.7 3.9 fusion.103
  232.3 3.4 bitcast_reduce_fusion.2
  235.8 3.9 fusion.103
  243.9 3.9 fusion.103
  248.6 3.4 bitcast_reduce_fusion.2
  252.1 3.9 fusion.103
  260.4 46.8 %all-reduce.3.cloned.1.call-done = bf16[192,1536]{1,0:T(8,128)(2,1)} async-done(((bf16[192,1536]{1,0:T(8,128)(2,1)}), bf16[192,1536]{1,0:T(8,128)(2,1)}) %all-reduce.3.cloned.1.call-update) | async-done | bytes 589840 | tf_op jit(solution)/shard_map/psum | solution.py:91
  314.1 10.1 %all-to-all-start = ((bf16[192,32,12]{0,2,1:T(8,128)(2,1)}), bf16[192,32,12]{0,2,1:T(8,128)(2,1)}, u32[]{:S(2)}, u32[]{:S(2)}) async-start(bf16[192,32,12]{0,2,1:T(8,128)(2,1)} %reshape.86), calls=%async_computation | async-start | bytes 524288 | tf_op jit(solution)/shard_map/all_to_all | solution.py:100
  329.2 6.2 %all-to-all-done = bf16[192,32,12]{0,2,1:T(8,128)(2,1)} async-done(((bf16[192,32,12]{0,2,1:T(8,128)(2,1)}), bf16[192,32,12]{0,2,1:T(8,128)(2,1)}, u32[]{:S(2)}, u32[]{:S(2)}) %all-to-all-start) | async-done | bytes 147488 | tf_op jit(solution)/shard_map/all_to_all | solution.py:100
  338.9 9.3 %multiply_convert_fusion = bf16[6144,12]{0,1:T(8,128)(2,1)} fusion(bf16[6144,12]{0,1:T(8,128)(2,1)} %all_to_all.28, f32[12]{0:T(128)} %dynamic_slice.18, f32[12]{0:T(128)} %get-tuple-element.143, f32[12]{0:T(128)S(1)} %get-tuple-element.114, f32[12]{0:T(128)S(1)} %get-tuple-element.115, f32[12]{0:T(128)S(1)} %get-tuple-element.116, ...), kind=kLoop, calls=%fused_computation.53 | loop fusion | flops 7225344 | bytes 296448 | tf_op jit(solution)/shard_map/convert_element_type | solution.py:25
  351.1 16.1 %all_to_all.35 = bf16[32,192,12]{1,2,0:T(8,128)(2,1)} all-to-all(bf16[32,192,12]{1,2,0:T(8,128)(2,1)S(1)} %copy.28), channel_id=1, replica_groups=mesh['batch'=2,'ctx'=32,'tp'=4] {'ctx'}, dimensions={0} | all-to-all | bytes 294912 | tf_op jit(solution)/shard_map/all_to_all | solution.py:107
  373.9 31.0 %reduce-scatter.4.cloned.1.call-done = bf16[384,192]{1,0:T(8,128)(2,1)} async-done(((bf16[1536,192]{1,0:T(8,128)(2,1)}), bf16[384,192]{1,0:T(8,128)(2,1)}) %reduce-scatter.4.cloned.1.call-update) | async-done | bytes 147472
  (91 shorter events, 49.8 us)
Async XLA Ops:
  6.5 9.9 %copy-start = (bf16[3,1536,384]{2,1,0:T(8,128)(2,1)S(1)}, bf16[3,1536,384]{2,1,0:T(8,128)(2,1)}, u32[]{:S(2)}) copy-start(bf16[3,1536,384]{2,1,0:T(8,128)(2,1)} %param.13) | copy-start | bytes 10616836
  6.5 9.9 %copy-start.5 = (f32[1536]{0:T(1024)S(1)}, f32[1536]{0:T(1024)}, u32[]{:S(2)}) copy-start(f32[1536]{0:T(1024)} %param.12) | copy-start | bytes 18436
  6.5 95.5 %all-gather.5.cloned.1.call-start = ((), (), s32[]{:S(2)}) async-start(), calls=%async_computation.4 | async-start | bytes 4866048 | tf_op jit(solution)/shard_map/all_gather | solution.py:55
  15.9 1.5 copy-start.2
  18.2 167.2 %all-gather.7.cloned.1.call-start = ((), (), s32[]{:S(2)}) async-start(), calls=%async_computation.5 | async-start | bytes 4866048 | tf_op jit(solution)/shard_map/all_gather | solution.py:56
  19.0 288.2 %all-reduce.3.cloned.1.call-start = ((), (), s32[]{:S(2)}) async-start(), calls=%async_computation.3 | async-start | bytes 1179648 | tf_op jit(solution)/shard_map/psum | solution.py:91
  211.4 3.9 copy-start.1
  219.5 3.9 copy-start.1
  227.7 3.9 copy-start.1
  235.8 3.9 copy-start.1
  243.9 3.9 copy-start.1
  252.1 3.9 copy-start.1
  260.4 48.8 %copy-start.6 = (f32[1536]{0:T(1024)S(1)}, f32[1536]{0:T(1024)}, u32[]{:S(2)}) copy-start(f32[1536]{0:T(1024)} %param.15) | copy-start | bytes 18436
  307.2 2.0 copy-start.4
  308.9 1.1 copy-start.3
  314.1 21.3 %all-to-all-start = ((bf16[192,32,12]{0,2,1:T(8,128)(2,1)}), bf16[192,32,12]{0,2,1:T(8,128)(2,1)}, u32[]{:S(2)}, u32[]{:S(2)}) async-start(bf16[192,32,12]{0,2,1:T(8,128)(2,1)} %reshape.86), calls=%async_computation | async-start | bytes 524288 | tf_op jit(solution)/shard_map/all_to_all | solution.py:100
  324.2 80.7 %reduce-scatter.4.cloned.1.call-start = ((), (), s32[]{:S(2)}) async-start(), calls=%async_computation.6 | async-start | bytes 983040
Sparse Core Ops, SparseCore 0:
  18.4 83.6 all-gather.4
  104.6 80.7 all-gather.6
  260.5 46.6 all-reduce.2
  374.1 30.8 reduce-scatter.3
where the time goes:
time: 418 us; the launch traced here: 415 us
  waiting for transfers between devices  225 us (54%)
  local copies, waits for them, and re-layouts  66.1 us (16%)
  matrix products  51 us (12%)
  blocking collectives  25.5 us (6%)
  other arithmetic  23.2 us (6%)
  between operations  13.3 us (3%)
  starting transfers between devices  10.4 us (2%)
    all_gather x1, waiting for transfers between devices, per_device(): lax.all_gather(projected[1], 'ctx', axis=0, tiled=True)  79.6 us
    all_gather x1, waiting for transfers between devices, per_device(): lax.all_gather(projected[2], 'ctx', axis=0, tiled=True)  60.8 us
    psum x1, waiting for transfers between devices, per_device(): summed = lax.psum(attn_terms.astype(jnp.bfloat16), 'tp').astype(jnp.float32)  46.8 us
    unnamed x5, waiting for transfers between devices  31.7 us
    unnamed x17, local copies, waits for them, and re-layouts  26 us
    dot_general x6, matrix products, one_block(): jnp.einsum('hqk,khd->qhd', weights.astype(jnp.bfloat16), value_block, pre...  23.3 us
    dot_general x6, matrix products, one_block(): jnp.einsum('qhd,khd->hqk', query_heads, key_block, preferred_element_type...  20.7 us
    all_to_all x1, blocking collectives, per_device(): lax.all_to_all(activated_part, 'ctx', split_axis=0, concat_axis=1, tiled=...  16.1 us
  transfers between devices with their start and end apart: 5, of which 5 were waited for; matrix products, arithmetic and copies ran while one was open for 7% of the time, Pallas kernels for 0%

commit v1 on v0

v1 whole, which is shorter than its diff:
```python
import functools
import math

import jax
import jax.numpy as jnp
from jax import lax
from jax.experimental import pallas as pl
from jax.experimental.pallas import tpu as pltpu
from jax.sharding import Mesh
from jax.sharding import PartitionSpec as P

D = 1536
HEAD = 96
HEADS_HERE = 4
COLS = 384
ROWS = 192
REACH = 15
HALO = 16
EXT = 512
TP = ("xh", "core")
CTX = ("z", "y")
Q_SCALE = math.log2(math.e) / math.sqrt(HEAD)
VMEM_LIMIT = 40 * 2**20


def layer_norm(inputs, gain):
    inputs = inputs.astype(jnp.float32)
    average = jnp.mean(inputs, axis=-1, keepdims=True)
    centered = inputs - average
    variance = jnp.mean(centered * centered, axis=-1, keepdims=True)
    return (centered * lax.rsqrt(variance + 1e-05) * gain).astype(jnp.bfloat16)


def split_three(value):
    high = value.astype(jnp.bfloat16).astype(jnp.float32)
    rest = value - high
    mid = rest.astype(jnp.bfloat16).astype(jnp.float32)
    return high, mid, rest - mid


def head_window(head):
    start = 0 if head < 2 else 128
    lane = lax.broadcasted_iota(jnp.int32, (1, 256), 1) + start
    return start, (lane >= head * HEAD) & (lane < (head + 1) * HEAD)


def attention_kernel(q_ref, k_ref, v_ref, o_ref):
    tile = q_ref.shape[0]
    total = jnp.zeros((tile, COLS), jnp.float32)
    lane = lax.broadcasted_iota(jnp.int32, (1, 128), 1)
    stats = jnp.zeros((tile, 128), jnp.float32)
    for head in range(HEADS_HERE):
        start, inside = head_window(head)
        queries = jnp.where(inside, q_ref[:, start : start + 256], 0)
        scores = lax.dot_general(
            queries,
            k_ref[:, start : start + 256],
            (((1,), (1,)), ((), ())),
            preferred_element_type=jnp.float32,
        )
        top = jnp.max(scores, axis=1, keepdims=True)
        weights = jnp.exp2(scores - top)
        denominator = jnp.sum(weights, axis=1, keepdims=True)
        summed = jnp.dot(
            weights.astype(jnp.bfloat16),
            v_ref[:, start : start + 256],
            preferred_element_type=jnp.float32,
        )
        part = jnp.where(inside, summed * (1.0 / denominator), 0.0)
        blank = jnp.zeros((tile, 128), jnp.float32)
        total = total + jnp.concatenate([part, blank] if start == 0 else [blank, part], 1)
        for place, piece in enumerate(split_three(top + jnp.log2(denominator))):
            stats = jnp.where(lane == place * HEADS_HERE + head, piece, stats)
    o_ref[:, :COLS] = total.astype(jnp.bfloat16)
    o_ref[:, COLS:] = stats.astype(jnp.bfloat16)


def attention(queries, keys_values, tile):
    count = queries.shape[0]
    key_count = keys_values.shape[0]
    return pl.pallas_call(
        attention_kernel,
        grid=(count // tile,),
        in_specs=[
            pl.BlockSpec((tile, COLS), lambda i: (i, 0)),
            pl.BlockSpec((key_count, COLS), lambda i: (0, 0)),
            pl.BlockSpec((key_count, COLS), lambda i: (0, 1)),
        ],
        out_specs=pl.BlockSpec((tile, EXT), lambda i: (i, 0)),
        out_shape=jax.ShapeDtypeStruct((count, EXT), jnp.bfloat16),
        compiler_params=pltpu.CompilerParams(vmem_limit_bytes=VMEM_LIMIT),
        name="attention",
    )(queries, keys_values, keys_values)


def combine_kernel(parts_ref, o_ref):
    count = parts_ref.shape[0]
    lane = lax.broadcasted_iota(jnp.int32, (1, COLS), 1)
    logs = []
    for part in range(count):
        stats = parts_ref[part, :, COLS:].astype(jnp.float32)
        logs.append(stats[:, 0:4] + stats[:, 4:8] + stats[:, 8:12])
    top = functools.reduce(jnp.maximum, logs)
    shares = [jnp.exp2(log - top) for log in logs]
    inverse = 1.0 / functools.reduce(jnp.add, shares)
    total = jnp.zeros((parts_ref.shape[1], COLS), jnp.float32)
    for part in range(count):
        share = shares[part] * inverse
        spread = jnp.zeros((parts_ref.shape[1], COLS), jnp.float32)
        for head in range(HEADS_HERE):
            inside = (lane >= head * HEAD) & (lane < (head + 1) * HEAD)
            spread = jnp.where(inside, share[:, head : head + 1], spread)
        total = total + spread * parts_ref[part, :, :COLS].astype(jnp.float32)
    o_ref[...] = total.astype(jnp.bfloat16)


def combine(parts):
    return pl.pallas_call(
        combine_kernel,
        out_shape=jax.ShapeDtypeStruct((parts.shape[1], COLS), jnp.bfloat16),
        compiler_params=pltpu.CompilerParams(vmem_limit_bytes=VMEM_LIMIT),
        name="combine",
    )(parts)


def middle_kernel(place_ref, rows_ref, context_ref, w0, w1, w2, w3, gain_ref, glu_ref, m_ref, g_ref):
    place = place_ref[0]
    total = rows_ref[...].astype(jnp.float32)
    for offset, weight in enumerate((w0, w1, w2, w3)):
        total = total + jnp.dot(
            context_ref[place ^ offset], weight[...], preferred_element_type=jnp.float32
        )
    middle = total.astype(jnp.bfloat16)
    for position in range(4):

        @pl.when(place == position)
        def _():
            m_ref[...] = middle[:, position * COLS : (position + 1) * COLS]

    normed = layer_norm(middle, gain_ref[...])
    value = jnp.dot(normed, glu_ref[0], preferred_element_type=jnp.float32)
    gate = jnp.dot(normed, glu_ref[1], preferred_element_type=jnp.float32)
    g_ref[...] = (value * (1.0 / (1.0 + jnp.exp(-gate)))).astype(jnp.bfloat16)


def middle_and_glu(place, rows, context, weights, gain, glu_weight):
    count = rows.shape[0]
    vmem = pl.BlockSpec(memory_space=pltpu.VMEM)
    return pl.pallas_call(
        middle_kernel,
        in_specs=[pl.BlockSpec(memory_space=pltpu.SMEM)] + [vmem] * 8,
        out_specs=[vmem] * 2,
        out_shape=[jax.ShapeDtypeStruct((count, COLS), jnp.bfloat16)] * 2,
        compiler_params=pltpu.CompilerParams(vmem_limit_bytes=VMEM_LIMIT),
        name="middle",
    )(place, rows, context, *weights, gain.reshape(1, D), glu_weight)


def depthwise_kernel(before_ref, glu_ref, after_ref, taps_ref, bias_ref, o_ref, held):
    held[:HALO] = before_ref[...].astype(jnp.float32)
    held[HALO : HALO + ROWS] = glu_ref[...].astype(jnp.float32)
    held[HALO + ROWS :] = after_ref[...].astype(jnp.float32)
    taps = taps_ref[...].astype(jnp.float32)
    for column in range(COLS // 128):
        here = slice(column * 128, (column + 1) * 128)
        total = jnp.zeros((ROWS, 128), jnp.float32) + bias_ref[:, here]
        for tap in range(2 * REACH + 1):
            begin = HALO - REACH + tap
            total = total + held[begin : begin + ROWS, here] * taps[tap : tap + 1, here]
        o_ref[:, here] = (total / (1.0 + jnp.exp(-total))).astype(jnp.bfloat16)


def depthwise(before, glu, after, taps, bias):
    return pl.pallas_call(
        depthwise_kernel,
        out_shape=jax.ShapeDtypeStruct((ROWS, COLS), jnp.bfloat16),
        scratch_shapes=[pltpu.VMEM((ROWS + 2 * HALO, COLS), jnp.float32)],
        compiler_params=pltpu.CompilerParams(vmem_limit_bytes=VMEM_LIMIT),
        name="depthwise",
    )(before, glu, after, taps, bias.reshape(1, COLS))


def per_device(
    frames,
    attn_gain,
    query_key_value,
    out_weight,
    conv_gain,
    glu_weight,
    depth_kernel,
    depth_bias,
    proj_weight,
):
    place = lax.axis_index(TP)
    whole_rows = lax.all_gather(frames, TP, axis=1, tiled=True)
    normed = layer_norm(whole_rows, attn_gain)

    def project(index):
        return jnp.dot(normed, query_key_value[index], preferred_element_type=jnp.float32)

    keys_values = jnp.concatenate(
        [project(1).astype(jnp.bfloat16), project(2).astype(jnp.bfloat16)], axis=1
    )
    queries = (project(0) * Q_SCALE).astype(jnp.bfloat16)
    keys_values = lax.all_gather(keys_values, "z", axis=0, tiled=True)
    queries = lax.all_gather(queries, "y", axis=0, tiled=True)

    out_here, proj_here, queries = lax.optimization_barrier((out_weight, proj_weight, queries))
    swap = [(0, 1), (1, 0)]
    out_far = lax.ppermute(out_here, "xh", swap)
    out_core = lax.ppermute(out_here, "core", swap)
    out_far_core = lax.ppermute(out_far, "core", swap)
    out_pieces = (out_here, out_core, out_far, out_far_core)
    proj_split = proj_here.reshape(COLS, 4, COLS)
    proj_pieces = [lax.dynamic_index_in_dim(proj_split, place, 1, False)]
    for offset in range(1, 4):
        piece = lax.dynamic_index_in_dim(proj_split, place ^ offset, 1, False)
        proj_pieces.append(lax.ppermute(piece, TP, [(i, i ^ offset) for i in range(4)]))

    partial = attention(queries, keys_values, 256)
    parts = lax.all_to_all(partial, "y", split_axis=0, concat_axis=0, tiled=True)
    context = combine(parts.reshape(4, ROWS, EXT))
    context = lax.all_gather(context, TP, axis=0, tiled=False)
    middle, glu = middle_and_glu(
        place.reshape(1), whole_rows, context, out_pieces, conv_gain, glu_weight
    )
    before = lax.ppermute(glu[ROWS - HALO :], CTX, [(i, i + 1) for i in range(31)])
    after = lax.ppermute(glu[:HALO], CTX, [(i + 1, i) for i in range(31)])
    activated = depthwise(before, glu, after, depth_kernel, depth_bias)
    activated = lax.all_gather(activated, TP, axis=0, tiled=False)
    conv_sum = jnp.zeros((ROWS, COLS), jnp.float32)
    for offset in range(4):
        piece = lax.dynamic_index_in_dim(activated, place ^ offset, 0, False)
        conv_sum = conv_sum + jnp.dot(
            piece, proj_pieces[offset], preferred_element_type=jnp.float32
        )
    return (middle.astype(jnp.float32) + conv_sum).astype(jnp.bfloat16)


def solution(mesh):
    parted = Mesh(mesh.devices.reshape(2, 8, 4, 2, 2), ("batch", "z", "y", "xh", "core"))
    in_specs = (
        P(("batch",) + CTX, TP),
        P(),
        P(None, None, TP),
        P(TP, None),
        P(),
        P(None, None, TP),
        P(None, TP),
        P(TP),
        P(TP, None),
    )
    out_specs = P(("batch",) + CTX, TP)
    return jax.shard_map(
        per_device, mesh=parted, in_specs=in_specs, out_specs=out_specs, check_vma=False
    )
```

time: 418 us -> 143 us (0.34)
  the two profiles are of different devices: /device:TPU:56 before, /device:TPU:129 now
where the time goes in v1:
time: 143 us
  blocking collectives  42.1 us (29%)
  waiting for transfers between devices  28.3 us (20%)
  starting transfers between devices  24.9 us (17%)
  Pallas kernels  16 us (11%)
  between operations  13.6 us (10%)
  local copies, waits for them, and re-layouts  8.31 us (6%)
  matrix products  7.43 us (5%)
  other arithmetic  1.9 us (1%)
    ppermute x1, waiting for transfers between devices, per_device(): out_far = lax.ppermute(out_here, 'xh', swap)  22.5 us
    all_gather x1, blocking collectives, per_device(): queries = lax.all_gather(queries, 'y', axis=0, tiled=True)  11.8 us
    all_gather x1, blocking collectives, per_device(): activated = lax.all_gather(activated, TP, axis=0, tiled=False)  11.2 us
    all_gather x1, blocking collectives, per_device(): whole_rows = lax.all_gather(frames, TP, axis=1, tiled=True)  9.9 us
    pallas_call x1, Pallas kernels, attention(): pl.pallas_call(attention_kernel, grid=(count // tile,), in_specs=[pl.Bloc...  9.37 us
    all_gather x1, blocking collectives, per_device(): context = lax.all_gather(context, TP, axis=0, tiled=False)  9.15 us
    ppermute x1, starting transfers between devices, per_device(): after = lax.ppermute(glu[:HALO], CTX, [(i + 1, i) for i in range(31)])  6.41 us
    all_to_all x1, waiting for transfers between devices, per_device(): lax.all_to_all(partial, 'y', split_axis=0, concat_axis=0, tiled=True)  5.81 us
  transfers between devices with their start and end apart: 10, of which 2 were waited for; matrix products, arithmetic and copies ran while one was open for 6% of the time, Pallas kernels for 11%

profile of v1, /device:TPU:129, one launch (start us, length us, event | category | flops | bytes accessed | tf_op | source)
XLA Modules:
  0.0 142.5 jit_solution(1930973819950971283)
XLA Ops:
  6.5 9.9 %all_gather.21.rows_ref = bf16[192,1536]{1,0:T(8,128)(2,1)S(1)} all-gather(bf16[192,384]{1,0:T(8,128)(2,1)} %param.9), channel_id=1, replica_groups=mesh['batch'=2,'z'=8,'y'=4,'xh'=2,'core'=2] {'xh','core'}, dimensions={1}, use_global_device_ids=true | all-gather | bytes 737280 | tf_op jit(solution)/shard_map/all_gather | solution.py:195
  16.9 1.8 %fusion.21 = bf16[192,384]{1,0:T(8,128)(2,1)S(1)} fusion(bf16[3,1536,384]{2,1,0:T(8,128)(2,1)} %param.11, bf16[192,1536]{1,0:T(8,128)(2,1)S(1)} %all_gather.21.rows_ref, f32[1536]{0:T(1024)S(1)} %copy-done.6, f32[192]{0:T(256)S(1)} %add_rsqrt_fusion, f32[192]{0:T(256)S(1)} %broadcast_multiply_fusion), kind=kOutput, calls=%fused_computation.21 | convolution fusion | flops 228040704 | bytes 1924608 | tf_op jit(solution)/shard_map/dot_general | solution.py:199
  18.7 1.8 %fusion.24 = bf16[192,384]{1,0:T(8,128)(2,1)S(1)} fusion(bf16[3,1536,384]{2,1,0:T(8,128)(2,1)} %param.11, bf16[192,1536]{1,0:T(8,128)(2,1)S(1)} %all_gather.21.rows_ref, f32[1536]{0:T(1024)S(1)} %copy-done.6, f32[192]{0:T(256)S(1)} %add_rsqrt_fusion, f32[192]{0:T(256)S(1)} %broadcast_multiply_fusion), kind=kOutput, calls=%fused_computation.22 | convolution fusion | flops 228040704 | bytes 1924608 | tf_op jit(solution)/shard_map/dot_general | solution.py:199
  21.3 1.9 %fusion.18 = bf16[192,384]{1,0:T(8,128)(2,1)S(1)} fusion(bf16[3,1536,384]{2,1,0:T(8,128)(2,1)} %param.11, bf16[192,1536]{1,0:T(8,128)(2,1)S(1)} %all_gather.21.rows_ref, f32[1536]{0:T(1024)S(1)} %copy-done.6, f32[192]{0:T(256)S(1)} %add_rsqrt_fusion, f32[192]{0:T(256)S(1)} %broadcast_multiply_fusion), kind=kOutput, calls=%fused_computation.20 | convolution fusion | flops 228114432 | bytes 1924608 | tf_op jit(solution)/shard_map/dot_general | solution.py:199
  23.2 11.8 %all_gather.22.q_ref = bf16[768,384]{1,0:T(8,128)(2,1)S(1)} all-gather(bf16[192,384]{1,0:T(8,128)(2,1)S(1)} %fusion.18), channel_id=1, replica_groups=mesh['batch'=2,'z'=8,'y'=4,'xh'=2,'core'=2] {'y'}, dimensions={0}, use_global_device_ids=true | all-gather | bytes 737280 | tf_op jit(solution)/shard_map/all_gather | solution.py:206
  35.0 2.2 %collective-permute-start.1 = (bf16[384,1536]{1,0:T(8,128)(2,1)S(1)}, bf16[384,1536]{1,0:T(8,128)(2,1)}, u32[]{:S(2)}, u32[]{:S(2)}) collective-permute-start(bf16[384,1536]{1,0:T(8,128)(2,1)S(1)} %copy-done.2), channel_id=1, source_target_pairs={{0,2},{2,0},{1,3},{3,1},{4,6},{6,4},{5,7},{7,5},{8,10},{10,8},{9,1... | collective-permute-start | bytes 3538952 | tf_op jit(solution)/shard_map/ppermute | solution.py:210
  37.1 2.4 %collective-permute-start = (bf16[384,1536]{1,0:T(8,128)(2,1)S(1)}, bf16[384,1536]{1,0:T(8,128)(2,1)}, u32[]{:S(2)}, u32[]{:S(2)}) collective-permute-start(bf16[384,1536]{1,0:T(8,128)(2,1)S(1)} %copy-done.2), channel_id=1, source_target_pairs={{0,1},{1,0},{2,3},{3,2},{4,5},{5,4},{6,7},{7,6},{8,9},{9,8},{10,11... | collective-permute-start | bytes 3538952 | tf_op jit(solution)/shard_map/ppermute | solution.py:211
  39.6 22.5 %collective-permute-done.1.w2 = bf16[384,1536]{1,0:T(8,128)(2,1)} collective-permute-done((bf16[384,1536]{1,0:T(8,128)(2,1)S(1)}, bf16[384,1536]{1,0:T(8,128)(2,1)}, u32[]{:S(2)}, u32[]{:S(2)}) %collective-permute-start.1) | collective-permute-done | bytes 1179680 | tf_op jit(solution)/shard_map/ppermute | solution.py:210
  62.0 2.9 %collective-permute-start.2 = (bf16[384,1536]{1,0:T(8,128)(2,1)}, bf16[384,1536]{1,0:T(8,128)(2,1)}, u32[]{:S(2)}, u32[]{:S(2)}) collective-permute-start(bf16[384,1536]{1,0:T(8,128)(2,1)} %collective-permute-done.1.w2), channel_id=1, source_target_pairs={{0,1},{1,0},{2,3},{3,2},{4,5},{5,4},{6,7},{7,6},{8,9},{9,8},{10,11... | collective-permute-start | bytes 3538952 | tf_op jit(solution)/shard_map/ppermute | solution.py:212
  65.0 1.7 %copy-done = bf16[1536,768]{1,0:T(8,128)(2,1)S(1)} copy-done((bf16[1536,768]{1,0:T(8,128)(2,1)S(1)}, bf16[1536,768]{1,0:T(8,128)(2,1)}, u32[]{:S(2)}) %copy-start) | copy-done | bytes 2359320
  66.6 9.4 %attention.1 = bf16[768,512]{1,0:T(8,128)(2,1)} custom-call(bf16[768,384]{1,0:T(8,128)(2,1)S(1)} %all_gather.22.q_ref, bf16[1536,768]{1,0:T(8,128)(2,1)S(1)} %copy-done, bf16[1536,768]{1,0:T(8,128)(2,1)S(1)} %copy-done), custom_call_target="tpu_custom_call" | custom-call | tf_op jit(solution)/shard_map/attention/pallas_call | solution.py:81
  76.0 3.5 %all-to-all-start = ((bf16[4,192,512]{2,1,0:T(8,128)(2,1)}), bf16[4,192,512]{2,1,0:T(8,128)(2,1)S(1)}, u32[]{:S(2)}, u32[]{:S(2)}) async-start(bf16[4,192,512]{2,1,0:T(8,128)(2,1)} %bitcast.4), calls=%async_computation | async-start | bytes 1572864 | tf_op jit(solution)/shard_map/all_to_all | solution.py:221
  79.5 2.4 %copy.10 = bf16[384,1536]{0,1:T(8,128)(2,1)} copy(bf16[384,1536]{1,0:T(8,128)(2,1)} %param.17) | data formatting | bytes 2359296 | tf_op jit(solution)/shard_map/optimization_barrier | solution.py:208
  81.9 1.2 constant_dynamic-slice_fusion
  84.0 2.1 %collective-permute-start.7 = (bf16[384,384]{1,0:T(8,128)(2,1)}, bf16[384,384]{1,0:T(8,128)(2,1)S(1)}, u32[]{:S(2)}, u32[]{:S(2)}) collective-permute-start(bf16[384,384]{1,0:T(8,128)(2,1)} %bitcast.51), channel_id=1, source_target_pairs={{0,3},{1,2},{2,1},{3,0},{4,7},{5,6},{6,5},{7,4},{8,11},{9,10},{10,... | collective-permute-start | bytes 884744 | tf_op jit(solution)/shard_map/ppermute | solution.py:218
  86.1 5.8 %all-to-all-done.parts_ref = bf16[4,192,512]{2,1,0:T(8,128)(2,1)S(1)} async-done(((bf16[4,192,512]{2,1,0:T(8,128)(2,1)}), bf16[4,192,512]{2,1,0:T(8,128)(2,1)S(1)}, u32[]{:S(2)}, u32[]{:S(2)}) %all-to-all-start) | async-done | bytes 786464 | tf_op jit(solution)/shard_map/all_to_all | solution.py:221
  92.7 9.2 %all-gather = bf16[768,384]{1,0:T(8,128)(2,1)S(1)} all-gather(bf16[192,384]{1,0:T(8,128)(2,1)S(1)} %combine.1), channel_id=2, replica_groups=mesh['batch'=2,'z'=8,'y'=4,'xh'=2,'core'=2] {'xh','core'}, dimensions={0}, use_global_device_ids=true | all-gather | bytes 737280 | tf_op jit(solution)/shard_map/all_gather | solution.py:223
  101.9 1.7 %copy-done.1 = bf16[2,1536,384]{2,1,0:T(8,128)(2,1)S(1)} copy-done((bf16[2,1536,384]{2,1,0:T(8,128)(2,1)S(1)}, bf16[2,1536,384]{2,1,0:T(8,128)(2,1)}, u32[]{:S(2)}) %copy-start.1) | copy-done | bytes 2359320
  103.5 4.5 %middle.1 = (bf16[192,384]{1,0:T(8,128)(2,1)S(1)}, bf16[192,384]{1,0:T(8,128)(2,1)S(1)}) custom-call(s32[1]{0:T(128)} %bitcast.place_ref, bf16[192,1536]{1,0:T(8,128)(2,1)S(1)} %all_gather.21.rows_ref, bf16[4,192,384]{2,1,0:T(8,128)(2,1)S(1)} %bitcast.44, bf16[384,1536]{1,0:T(8,128)(2,1)S(1)} %copy-done.2, bf16[384,1536]{1,0:T(8,128)(2,1)} %collective-permute-done.w1, ...), custom_call_target="tpu_custom_call" | custom-call | tf_op jit(solution)/shard_map/middle/pallas_call | solution.py:149
  108.1 2.2 %collective-permute-start.3 = (bf16[16,384]{1,0:T(8,128)(2,1)S(1)}, bf16[16,384]{1,0:T(8,128)(2,1)S(1)}, u32[]{:S(2)}, u32[]{:S(2)}) collective-permute-start(bf16[16,384]{1,0:T(8,128)(2,1)S(1)} %get-tuple-element.19), channel_id=1, source_target_pairs={{0,4},{4,8},{8,12},{12,16},{16,20},{20,24},{24,28},{28,32},{32,36}... | collective-permute-start | bytes 36872 | tf_op jit(solution)/shard_map/ppermute | solution.py:227
  110.3 6.4 %collective-permute-start.4 = (bf16[16,384]{1,0:T(8,128)(2,1)S(1)}, bf16[16,384]{1,0:T(8,128)(2,1)S(1)}, u32[]{:S(2)}, u32[]{:S(2)}) collective-permute-start(bf16[16,384]{1,0:T(8,128)(2,1)S(1)} %get-tuple-element.18), channel_id=1, source_target_pairs={{4,0},{8,4},{12,8},{16,12},{20,16},{24,20},{28,24},{32,28},{36,32}... | collective-permute-start | bytes 36872 | tf_op jit(solution)/shard_map/ppermute | solution.py:228
  118.1 2.3 %collective-permute-start.6 = (bf16[384,384]{1,0:T(8,128)(2,1)S(1)}, bf16[384,384]{1,0:T(8,128)(2,1)S(1)}, u32[]{:S(2)}, u32[]{:S(2)}) collective-permute-start(bf16[384,384]{1,0:T(8,128)(2,1)S(1)} %bitcast.52), channel_id=1, source_target_pairs={{0,2},{1,3},{2,0},{3,1},{4,6},{5,7},{6,4},{7,5},{8,10},{9,11},{10,... | collective-permute-start | bytes 884744 | tf_op jit(solution)/shard_map/ppermute | solution.py:218
  120.4 1.3 depthwise.1
  121.8 11.2 %all-gather.1 = bf16[768,384]{1,0:T(8,128)(2,1)S(1)} all-gather(bf16[192,384]{1,0:T(8,128)(2,1)S(1)} %depthwise.1), channel_id=3, replica_groups=mesh['batch'=2,'z'=8,'y'=4,'xh'=2,'core'=2] {'xh','core'}, dimensions={0}, use_global_device_ids=true | all-gather | bytes 737280 | tf_op jit(solution)/shard_map/all_gather | solution.py:230
  (40 shorter events, 7.0 us)
Async XLA Ops:
  6.5 10.4 %copy-start.6 = (f32[1536]{0:T(1024)S(1)}, f32[1536]{0:T(1024)}, u32[]{:S(2)}) copy-start(f32[1536]{0:T(1024)} %param.10) | copy-start | bytes 18436
  6.5 58.4 %all-gather.4.cloned.1.call-start = ((), (), s32[]{:S(2)}) async-start(), calls=%async_computation.1 | async-start | bytes 2654208 | tf_op jit(solution)/shard_map/all_gather | solution.py:205
  21.3 13.7 %copy-start.2 = (bf16[384,1536]{1,0:T(8,128)(2,1)S(1)}, bf16[384,1536]{1,0:T(8,128)(2,1)}, u32[]{:S(2)}) copy-start(bf16[384,1536]{1,0:T(8,128)(2,1)} %w0) | copy-start | bytes 3538948
  35.0 27.1 %collective-permute-start.1 = (bf16[384,1536]{1,0:T(8,128)(2,1)S(1)}, bf16[384,1536]{1,0:T(8,128)(2,1)}, u32[]{:S(2)}, u32[]{:S(2)}) collective-permute-start(bf16[384,1536]{1,0:T(8,128)(2,1)S(1)} %copy-done.2), channel_id=1, source_target_pairs={{0,2},{2,0},{1,3},{3,1},{4,6},{6,4},{5,7},{7,5},{8,10},{10,8},{9,1... | collective-permute-start | bytes 3538952 | tf_op jit(solution)/shard_map/ppermute | solution.py:210
  37.1 64.7 %collective-permute-start = (bf16[384,1536]{1,0:T(8,128)(2,1)S(1)}, bf16[384,1536]{1,0:T(8,128)(2,1)}, u32[]{:S(2)}, u32[]{:S(2)}) collective-permute-start(bf16[384,1536]{1,0:T(8,128)(2,1)S(1)} %copy-done.2), channel_id=1, source_target_pairs={{0,1},{1,0},{2,3},{3,2},{4,5},{5,4},{6,7},{7,6},{8,9},{9,8},{10,11... | collective-permute-start | bytes 3538952 | tf_op jit(solution)/shard_map/ppermute | solution.py:211
  62.0 39.8 %collective-permute-start.2 = (bf16[384,1536]{1,0:T(8,128)(2,1)}, bf16[384,1536]{1,0:T(8,128)(2,1)}, u32[]{:S(2)}, u32[]{:S(2)}) collective-permute-start(bf16[384,1536]{1,0:T(8,128)(2,1)} %collective-permute-done.1.w2), channel_id=1, source_target_pairs={{0,1},{1,0},{2,3},{3,2},{4,5},{5,4},{6,7},{7,6},{8,9},{9,8},{10,11... | collective-permute-start | bytes 3538952 | tf_op jit(solution)/shard_map/ppermute | solution.py:212
  65.0 1.7 %copy-start = (bf16[1536,768]{1,0:T(8,128)(2,1)S(1)}, bf16[1536,768]{1,0:T(8,128)(2,1)}, u32[]{:S(2)}) copy-start(bf16[1536,768]{1,0:T(8,128)(2,1)} %all-gather.4.cloned.1.call-done.k_ref.v_ref) | copy-start | bytes 7077892
  76.0 15.9 %all-to-all-start = ((bf16[4,192,512]{2,1,0:T(8,128)(2,1)}), bf16[4,192,512]{2,1,0:T(8,128)(2,1)S(1)}, u32[]{:S(2)}, u32[]{:S(2)}) async-start(bf16[4,192,512]{2,1,0:T(8,128)(2,1)} %bitcast.4), calls=%async_computation | async-start | bytes 1572864 | tf_op jit(solution)/shard_map/all_to_all | solution.py:221
  81.9 4.2 %copy-start.4 = (f32[1536]{0:T(1024)S(1)}, f32[1536]{0:T(1024)}, u32[]{:S(2)}) copy-start(f32[1536]{0:T(1024)} %param.13) | copy-start | bytes 18436
  84.0 49.0 %collective-permute-start.7 = (bf16[384,384]{1,0:T(8,128)(2,1)}, bf16[384,384]{1,0:T(8,128)(2,1)S(1)}, u32[]{:S(2)}, u32[]{:S(2)}) collective-permute-start(bf16[384,384]{1,0:T(8,128)(2,1)} %bitcast.51), channel_id=1, source_target_pairs={{0,3},{1,2},{2,1},{3,0},{4,7},{5,6},{6,5},{7,4},{8,11},{9,10},{10,... | collective-permute-start | bytes 884744 | tf_op jit(solution)/shard_map/ppermute | solution.py:218
  101.9 1.7 %copy-start.1 = (bf16[2,1536,384]{2,1,0:T(8,128)(2,1)S(1)}, bf16[2,1536,384]{2,1,0:T(8,128)(2,1)}, u32[]{:S(2)}) copy-start(bf16[2,1536,384]{2,1,0:T(8,128)(2,1)} %glu_ref.1) | copy-start | bytes 7077892
  108.0 12.3 %copy-start.5 = (f32[384]{0:T(512)S(1)}, f32[384]{0:T(512)}, u32[]{:S(2)}) copy-start(f32[384]{0:T(512)} %param.16) | copy-start | bytes 4612
  108.1 12.4 %copy-start.3 = (bf16[31,384]{1,0:T(8,128)(2,1)S(1)}, bf16[31,384]{1,0:T(8,128)(2,1)}, u32[]{:S(2)}) copy-start(bf16[31,384]{1,0:T(8,128)(2,1)} %taps_ref.1) | copy-start | bytes 71428
  108.1 12.3 %collective-permute-start.3 = (bf16[16,384]{1,0:T(8,128)(2,1)S(1)}, bf16[16,384]{1,0:T(8,128)(2,1)S(1)}, u32[]{:S(2)}, u32[]{:S(2)}) collective-permute-start(bf16[16,384]{1,0:T(8,128)(2,1)S(1)} %get-tuple-element.19), channel_id=1, source_target_pairs={{0,4},{4,8},{8,12},{12,16},{16,20},{20,24},{24,28},{28,32},{32,36}... | collective-permute-start | bytes 36872 | tf_op jit(solution)/shard_map/ppermute | solution.py:227
  110.3 10.1 %collective-permute-start.4 = (bf16[16,384]{1,0:T(8,128)(2,1)S(1)}, bf16[16,384]{1,0:T(8,128)(2,1)S(1)}, u32[]{:S(2)}, u32[]{:S(2)}) collective-permute-start(bf16[16,384]{1,0:T(8,128)(2,1)S(1)} %get-tuple-element.18), channel_id=1, source_target_pairs={{4,0},{8,4},{12,8},{16,12},{20,16},{24,20},{28,24},{32,28},{36,32}... | collective-permute-start | bytes 36872 | tf_op jit(solution)/shard_map/ppermute | solution.py:228
  116.9 17.6 %collective-permute-start.5 = (bf16[384,384]{1,0:T(8,128)(2,1)S(1)}, bf16[384,384]{1,0:T(8,128)(2,1)S(1)}, u32[]{:S(2)}, u32[]{:S(2)}) collective-permute-start(bf16[384,384]{1,0:T(8,128)(2,1)S(1)} %bitcast.53), channel_id=1, source_target_pairs={{0,1},{1,0},{2,3},{3,2},{4,5},{5,4},{6,7},{7,6},{8,9},{9,8},{10,11... | collective-permute-start | bytes 884744 | tf_op jit(solution)/shard_map/ppermute | solution.py:218
  118.1 16.6 %collective-permute-start.6 = (bf16[384,384]{1,0:T(8,128)(2,1)S(1)}, bf16[384,384]{1,0:T(8,128)(2,1)S(1)}, u32[]{:S(2)}, u32[]{:S(2)}) collective-permute-start(bf16[384,384]{1,0:T(8,128)(2,1)S(1)} %bitcast.52), channel_id=1, source_target_pairs={{0,2},{1,3},{2,0},{3,1},{4,6},{5,7},{6,4},{7,5},{8,10},{9,11},{10,... | collective-permute-start | bytes 884744 | tf_op jit(solution)/shard_map/ppermute | solution.py:218
Sparse Core Ops, SparseCore 0:
  21.4 36.3 all-gather.3

commit v2 on v1

v2 whole, which is shorter than its diff:
```python
import functools
import math

import jax
import jax.numpy as jnp
from jax import lax
from jax.experimental import pallas as pl
from jax.experimental.pallas import tpu as pltpu
from jax.sharding import Mesh
from jax.sharding import PartitionSpec as P

D = 1536
HEAD = 96
HEADS_HERE = 4
COLS = 384
ROWS = 192
REACH = 15
HALO = 16
EXT = 512
TP = ("xh", "core")
CTX = ("z", "y")
Q_SCALE = math.log2(math.e) / math.sqrt(HEAD)
VMEM_LIMIT = 24 * 2**20
VMEM_WHOLE = 60 * 2**20


def layer_norm(inputs, gain):
    inputs = inputs.astype(jnp.float32)
    average = jnp.mean(inputs, axis=-1, keepdims=True)
    centered = inputs - average
    variance = jnp.mean(centered * centered, axis=-1, keepdims=True)
    return (centered * lax.rsqrt(variance + 1e-05) * gain).astype(jnp.bfloat16)


def split_three(value):
    high = value.astype(jnp.bfloat16).astype(jnp.float32)
    rest = value - high
    mid = rest.astype(jnp.bfloat16).astype(jnp.float32)
    return high, mid, rest - mid


def head_window(head):
    start = 0 if head < 2 else 128
    lane = lax.broadcasted_iota(jnp.int32, (1, 256), 1) + start
    return start, (lane >= head * HEAD) & (lane < (head + 1) * HEAD)


def attend(queries, keys, values, head):
    start, inside = head_window(head)
    masked = jnp.where(inside, queries[:, start : start + 256], 0)
    window = jnp.concatenate([block[:, start : start + 256] for block in keys], 0)
    scores = lax.dot_general(
        masked, window, (((1,), (1,)), ((), ())), preferred_element_type=jnp.float32
    )
    top = jnp.max(scores, axis=1, keepdims=True)
    weights = jnp.exp2(scores - top)
    denominator = jnp.sum(weights, axis=1, keepdims=True)
    window = jnp.concatenate([block[:, start : start + 256] for block in values], 0)
    summed = jnp.dot(weights.astype(jnp.bfloat16), window, preferred_element_type=jnp.float32)
    return inside, summed, top, denominator


def widen(part, head):
    blank = jnp.zeros((part.shape[0], 128), jnp.float32)
    return jnp.concatenate([part, blank] if head < 2 else [blank, part], 1)


def split_refs(refs, count):
    keys = [ref.at[:, :COLS] for ref in refs[:count]]
    values = [ref.at[:, COLS:] for ref in refs[:count]]
    return keys, values, refs[count:]


def first_attention_kernel(blocks, *refs):
    pieces, refs = refs[: -blocks - 3], refs[-blocks - 3 :]
    keys, values, rest = split_refs(refs, blocks)
    o_ref, top_ref, sum_ref = rest
    lane = lax.broadcasted_iota(jnp.int32, (1, 128), 1)
    queries = jnp.concatenate([ref[...] for ref in pieces], 0)
    total = jnp.zeros((2 * ROWS, COLS), jnp.float32)
    tops = jnp.zeros((2 * ROWS, 128), jnp.float32)
    sums = jnp.ones((2 * ROWS, 128), jnp.float32)
    for head in range(HEADS_HERE):
        inside, summed, top, denominator = attend(queries, keys, values, head)
        total = total + widen(jnp.where(inside, summed, 0.0), head)
        tops = jnp.where(lane == head, top, tops)
        sums = jnp.where(lane == head, denominator, sums)
    o_ref[...] = total
    top_ref[...] = tops
    sum_ref[...] = sums


def last_attention_kernel(blocks, *refs):
    pieces, refs = refs[: -blocks - 5], refs[-blocks - 5 :]
    keys, values, rest = split_refs(refs, blocks)
    prior_ref, top_ref, sum_ref, *outs = rest
    lane = lax.broadcasted_iota(jnp.int32, (1, 128), 1)
    queries = jnp.concatenate([ref[...] for ref in pieces], 0)
    tops = jnp.zeros((2 * ROWS, 128), jnp.float32)
    sums = jnp.zeros((2 * ROWS, 128), jnp.float32)
    products = []
    for head in range(HEADS_HERE):
        inside, summed, top, denominator = attend(queries, keys, values, head)
        products.append((inside, summed))
        tops = jnp.where(lane == head, top, tops)
        sums = jnp.where(lane == head, denominator, sums)
    joint = jnp.maximum(tops, top_ref[...])
    rescale = jnp.exp2(tops - joint)
    prior_rescale = jnp.exp2(top_ref[...] - joint)
    denominator = sums * rescale + sum_ref[...] * prior_rescale
    inverse = 1.0 / denominator
    rescale = rescale * inverse
    prior_rescale = prior_rescale * inverse
    total = jnp.zeros((2 * ROWS, COLS), jnp.float32)
    for head, (inside, summed) in enumerate(products):
        start = 0 if head < 2 else 128
        part = (
            summed * rescale[:, head : head + 1]
            + prior_ref[:, start : start + 256] * prior_rescale[:, head : head + 1]
        )
        total = total + widen(jnp.where(inside, part, 0.0), head)
    high, mid, low = split_three(joint + jnp.log2(denominator))
    stats = jnp.where(
        lane < 4, high, jnp.where(lane < 8, pltpu.roll(mid, 4, 1), pltpu.roll(low, 8, 1))
    )
    for side in range(2):
        rows = slice(side * ROWS, (side + 1) * ROWS)
        outs[side][:, :COLS] = total[rows].astype(jnp.bfloat16)
        outs[side][:, COLS:] = stats[rows].astype(jnp.bfloat16)


def attention_cost(rows, blocks):
    flops = 2 * 2 * rows * ROWS * blocks * 256 * HEADS_HERE
    return pl.CostEstimate(flops=flops, bytes_accessed=4 * 2**20, transcendentals=0)


def first_attention(queries, blocks):
    rows = 2 * ROWS
    return pl.pallas_call(
        functools.partial(first_attention_kernel, len(blocks)),
        out_shape=[
            jax.ShapeDtypeStruct((rows, COLS), jnp.float32),
            jax.ShapeDtypeStruct((rows, 128), jnp.float32),
            jax.ShapeDtypeStruct((rows, 128), jnp.float32),
        ],
        compiler_params=pltpu.CompilerParams(vmem_limit_bytes=VMEM_LIMIT),
        cost_estimate=attention_cost(rows, len(blocks)),
        name="first_attention",
    )(*queries, *blocks)


def last_attention(queries, blocks, prior):
    return pl.pallas_call(
        functools.partial(last_attention_kernel, len(blocks)),
        out_shape=[jax.ShapeDtypeStruct((ROWS, EXT), jnp.bfloat16)] * 2,
        compiler_params=pltpu.CompilerParams(vmem_limit_bytes=VMEM_LIMIT),
        cost_estimate=attention_cost(2 * ROWS, len(blocks)),
        name="last_attention",
    )(*queries, *blocks, *prior)


def combine_kernel(*refs):
    parts, o_ref = refs[:-1], refs[-1]
    count = len(parts)
    lane = lax.broadcasted_iota(jnp.int32, (1, COLS), 1)
    logs = []
    for part in range(count):
        stats = parts[part][:, COLS:].astype(jnp.float32)
        logs.append(stats[:, 0:4] + stats[:, 4:8] + stats[:, 8:12])
    top = functools.reduce(jnp.maximum, logs)
    shares = [jnp.exp2(log - top) for log in logs]
    inverse = 1.0 / functools.reduce(jnp.add, shares)
    total = jnp.zeros((ROWS, COLS), jnp.float32)
    for part in range(count):
        share = shares[part] * inverse
        spread = jnp.zeros((ROWS, COLS), jnp.float32)
        for head in range(HEADS_HERE):
            inside = (lane >= head * HEAD) & (lane < (head + 1) * HEAD)
            spread = jnp.where(inside, share[:, head : head + 1], spread)
        total = total + spread * parts[part][:, :COLS].astype(jnp.float32)
    o_ref[...] = total.astype(jnp.bfloat16)


def combine(parts):
    return pl.pallas_call(
        combine_kernel,
        out_shape=jax.ShapeDtypeStruct((ROWS, COLS), jnp.bfloat16),
        compiler_params=pltpu.CompilerParams(vmem_limit_bytes=VMEM_LIMIT),
        name="combine",
    )(*parts)


def middle_kernel(
    place_ref, rows_ref, context_ref, w0, w1, w2, w3, gain_ref, glu_ref, m_ref, g_ref,
    weights, gain, glu, sems,
):
    copies = [
        pltpu.make_async_copy(weight, weights.at[index], sems.at[index])
        for index, weight in enumerate((w0, w1, w2, w3))
    ]
    copies.append(pltpu.make_async_copy(gain_ref, gain, sems.at[4]))
    for index in range(2):
        copies.append(pltpu.make_async_copy(glu_ref.at[index], glu.at[index], sems.at[5 + index]))
    for copy in copies:
        copy.start()
    place = place_ref[0]
    total = rows_ref[...].astype(jnp.float32)
    for offset in range(4):
        copies[offset].wait()
        total = total + jnp.dot(
            context_ref[place ^ offset], weights[offset], preferred_element_type=jnp.float32
        )
    middle = total.astype(jnp.bfloat16)
    for position in range(4):

        @pl.when(place == position)
        def _():
            m_ref[...] = middle[:, position * COLS : (position + 1) * COLS]

    copies[4].wait()
    normed = layer_norm(middle, gain[...].reshape(1, D))
    copies[5].wait()
    value = jnp.dot(normed, glu[0], preferred_element_type=jnp.float32)
    copies[6].wait()
    gate = jnp.dot(normed, glu[1], preferred_element_type=jnp.float32)
    g_ref[...] = (value * (1.0 / (1.0 + jnp.exp(-gate)))).astype(jnp.bfloat16)


def middle_and_glu(place, rows, context, weights, gain, glu_weight):
    count = rows.shape[0]
    vmem = pl.BlockSpec(memory_space=pltpu.VMEM)
    hbm = pl.BlockSpec(memory_space=pltpu.HBM)
    return pl.pallas_call(
        middle_kernel,
        in_specs=[pl.BlockSpec(memory_space=pltpu.SMEM), vmem, vmem] + [hbm] * 6,
        out_specs=[vmem] * 2,
        out_shape=[jax.ShapeDtypeStruct((count, COLS), jnp.bfloat16)] * 2,
        scratch_shapes=[
            pltpu.VMEM((4, COLS, D), jnp.bfloat16),
            pltpu.VMEM((D,), jnp.float32),
            pltpu.VMEM((2, D, COLS), jnp.bfloat16),
            pltpu.SemaphoreType.DMA((7,)),
        ],
        compiler_params=pltpu.CompilerParams(vmem_limit_bytes=VMEM_WHOLE),
        name="middle",
    )(place, rows, context, *weights, gain, glu_weight)


def depthwise_kernel(before_ref, glu_ref, after_ref, taps_ref, bias_ref, o_ref, held):
    held[:HALO] = before_ref[...].astype(jnp.float32)
    held[HALO : HALO + ROWS] = glu_ref[...].astype(jnp.float32)
    held[HALO + ROWS :] = after_ref[...].astype(jnp.float32)
    taps = taps_ref[...].astype(jnp.float32)
    for column in range(COLS // 128):
        here = slice(column * 128, (column + 1) * 128)
        total = jnp.zeros((ROWS, 128), jnp.float32) + bias_ref[here].reshape(1, 128)
        for tap in range(2 * REACH + 1):
            begin = HALO - REACH + tap
            total = total + held[begin : begin + ROWS, here] * taps[tap : tap + 1, here]
        o_ref[:, here] = (total / (1.0 + jnp.exp(-total))).astype(jnp.bfloat16)


def depthwise(before, glu, after, taps, bias):
    return pl.pallas_call(
        depthwise_kernel,
        out_shape=jax.ShapeDtypeStruct((ROWS, COLS), jnp.bfloat16),
        scratch_shapes=[pltpu.VMEM((ROWS + 2 * HALO, COLS), jnp.float32)],
        compiler_params=pltpu.CompilerParams(vmem_limit_bytes=VMEM_LIMIT),
        name="depthwise",
    )(before, glu, after, taps, bias)


def project_kernel(rows_ref, gain_ref, w_ref, kv_ref, q_ref, gain, weights, sems):
    copies = [pltpu.make_async_copy(gain_ref, gain, sems.at[3])]
    for index in (1, 2, 0):
        copies.append(pltpu.make_async_copy(w_ref.at[index], weights.at[index], sems.at[index]))
    for copy in copies:
        copy.start()
    rows = rows_ref[...].astype(jnp.float32)
    average = jnp.mean(rows, axis=-1, keepdims=True)
    centered = rows - average
    variance = jnp.mean(centered * centered, axis=-1, keepdims=True)
    scaled = centered * lax.rsqrt(variance + 1e-05)
    copies[0].wait()
    normed = (scaled * gain[...].reshape(1, D)).astype(jnp.bfloat16)
    for half in range(2):
        copies[1 + half].wait()
        kv_ref[:, half * COLS : (half + 1) * COLS] = jnp.dot(
            normed, weights[1 + half], preferred_element_type=jnp.float32
        ).astype(jnp.bfloat16)
    copies[3].wait()
    query = jnp.dot(normed, weights[0], preferred_element_type=jnp.float32)
    q_ref[...] = (query * Q_SCALE).astype(jnp.bfloat16)


def project(rows, gain, weights):
    vmem = pl.BlockSpec(memory_space=pltpu.VMEM)
    hbm = pl.BlockSpec(memory_space=pltpu.HBM)
    return pl.pallas_call(
        project_kernel,
        in_specs=[vmem, hbm, hbm],
        out_specs=[vmem, vmem],
        out_shape=[
            jax.ShapeDtypeStruct((ROWS, 2 * COLS), jnp.bfloat16),
            jax.ShapeDtypeStruct((ROWS, COLS), jnp.bfloat16),
        ],
        scratch_shapes=[
            pltpu.VMEM((D,), jnp.float32),
            pltpu.VMEM((3, D, COLS), jnp.bfloat16),
            pltpu.SemaphoreType.DMA((4,)),
        ],
        compiler_params=pltpu.CompilerParams(vmem_limit_bytes=VMEM_WHOLE),
        name="project",
    )(rows, gain, weights)


def part_kernel(place_ref, own_ref, other_ref, w_own, w_other, *refs):
    o_ref = refs[-1]
    columns = pl.ds(pl.multiple_of(place_ref[0] * COLS, 128), COLS)
    total = jnp.dot(own_ref[...], w_own[:, columns], preferred_element_type=jnp.float32)
    total = total + jnp.dot(
        other_ref[...], w_other[:, columns], preferred_element_type=jnp.float32
    )
    if len(refs) > 1:
        total = total + refs[0][...].astype(jnp.float32)
    o_ref[...] = total.astype(o_ref.dtype)


def part_sum(place, own, other, weights, extra, kind):
    vmem = pl.BlockSpec(memory_space=pltpu.VMEM)
    return pl.pallas_call(
        part_kernel,
        in_specs=[pl.BlockSpec(memory_space=pltpu.SMEM)] + [vmem] * (4 + len(extra)),
        out_specs=vmem,
        out_shape=jax.ShapeDtypeStruct((ROWS, COLS), kind),
        compiler_params=pltpu.CompilerParams(vmem_limit_bytes=VMEM_LIMIT),
        cost_estimate=pl.CostEstimate(
            flops=4 * ROWS * COLS * COLS, bytes_accessed=3 * 2**20, transcendentals=0
        ),
        name="part_sum",
    )(place, own, other, *weights, *extra)


def behind(values, *earlier):
    return lax.optimization_barrier((tuple(values),) + earlier)[0]


def swap(value, axis, count, flip):
    return lax.ppermute(value, axis, [(i, i ^ flip) for i in range(count)])


def shift(value, axis, count, offset):
    return lax.ppermute(value, axis, [(i, (i + offset) % count) for i in range(count)])


def per_device(
    frames,
    attn_gain,
    query_key_value,
    out_weight,
    conv_gain,
    glu_weight,
    depth_kernel,
    depth_bias,
    proj_weight,
):
    place = lax.axis_index(TP)
    out_core = swap(out_weight, "core", 2, 1)
    proj_core = swap(proj_weight, "core", 2, 1)
    whole_rows = lax.all_gather(frames, TP, axis=1, tiled=True)
    mine, query = project(whole_rows, attn_gain, query_key_value)
    lower1, upper1 = shift(mine, "z", 8, 1), shift(mine, "z", 8, -1)
    query1 = swap(query, "y", 4, 1)
    (out_here,) = behind((out_weight,), query1)
    out_far = swap(out_here, "xh", 2, 1)
    lower2, upper2 = shift(lower1, "z", 8, 1), shift(upper1, "z", 8, -1)
    pair2 = swap(jnp.concatenate([query, query1], 0), "y", 4, 2)
    half = ROWS // 2
    second = [
        shift(lower2, "z", 8, 1),
        shift(upper2, "z", 8, -1),
        shift(lower2[:half], "z", 8, 2),
        shift(upper2[half:], "z", 8, -2),
    ]
    blocks = [mine, lower1, upper1, lower2, upper2]
    prior2 = first_attention([pair2], blocks)
    prior0 = first_attention([query, query1], blocks)
    second = behind(second, prior0, prior2)
    partial2, partial3 = last_attention([pair2], second, prior2)
    part2, part3 = swap(partial2, "y", 4, 2), swap(partial3, "y", 4, 3)
    partial0, partial1 = last_attention([query, query1], second, prior0)
    part1 = swap(partial1, "y", 4, 1)
    (out_far_core,) = behind((out_far,), part2, part3, part1)
    out_far_core = swap(out_far_core, "core", 2, 1)
    out_pieces = (out_weight, out_core, out_far, out_far_core)
    parts = [partial0, part1, part2, part3]
    context = combine(parts)
    context = lax.all_gather(context, TP, axis=0, tiled=False)
    middle, glu = middle_and_glu(
        place.reshape(1), whole_rows, context, out_pieces, conv_gain, glu_weight
    )
    before = lax.ppermute(glu[ROWS - HALO :], CTX, [(i, i + 1) for i in range(31)])
    after = lax.ppermute(glu[:HALO], CTX, [(i + 1, i) for i in range(31)])
    activated = depthwise(before, glu, after, depth_kernel, depth_bias)
    other = swap(activated, "core", 2, 1)
    weights = (proj_weight, proj_core)
    theirs = part_sum((place ^ 2).reshape(1), activated, other, weights, (), jnp.bfloat16)
    theirs = swap(theirs, "xh", 2, 1)
    ours = part_sum(place.reshape(1), activated, other, weights, (middle,), jnp.float32)
    return (ours + theirs.astype(jnp.float32)).astype(jnp.bfloat16)


def solution(mesh):
    parted = Mesh(mesh.devices.reshape(2, 8, 4, 2, 2), ("batch", "z", "y", "xh", "core"))
    in_specs = (
        P(("batch",) + CTX, TP),
        P(),
        P(None, None, TP),
        P(TP, None),
        P(),
        P(None, None, TP),
        P(None, TP),
        P(TP),
        P(TP, None),
    )
    out_specs = P(("batch",) + CTX, TP)
    return jax.shard_map(
        per_device, mesh=parted, in_specs=in_specs, out_specs=out_specs, check_vma=False
    )
```

time: 143 us -> 111 us (0.78)
  the two profiles are of different devices: /device:TPU:129 before, /device:TPU:56 now
where the time goes in v2:
time: 111 us
  waiting for transfers between devices  33.7 us (30%)
  starting transfers between devices  30.4 us (27%)
  Pallas kernels  23.1 us (21%)
  blocking collectives  20.2 us (18%)
  local copies, waits for them, and re-layouts  1.69 us (2%)
  other arithmetic  1.63 us (1%)
    ppermute x11, waiting for transfers between devices, swap(): return lax.ppermute(value, axis, [(i, i ^ flip) for i in range(count)])  17.7 us
    ppermute x8, starting transfers between devices, shift(): lax.ppermute(value, axis, [(i, (i + offset) % count) for i in range(count)])  13.2 us
    all_gather x1, blocking collectives, per_device(): whole_rows = lax.all_gather(frames, TP, axis=1, tiled=True)  10.6 us
    ppermute x8, waiting for transfers between devices, shift(): lax.ppermute(value, axis, [(i, (i + offset) % count) for i in range(count)])  10.2 us
    ppermute x11, starting transfers between devices, swap(): return lax.ppermute(value, axis, [(i, i ^ flip) for i in range(count)])  9.57 us
    all_gather x1, blocking collectives, per_device(): context = lax.all_gather(context, TP, axis=0, tiled=False)  9.57 us
    pallas_call x1, Pallas kernels, middle_and_glu(): pl.pallas_call(middle_kernel, in_specs=[pl.BlockSpec(memory_space=pltpu.S...  6.19 us
    ppermute x1, waiting for transfers between devices, per_device(): after = lax.ppermute(glu[:HALO], CTX, [(i + 1, i) for i in range(31)])  5.76 us
  transfers between devices with their start and end apart: 21, of which 10 were waited for; matrix products, arithmetic and copies ran while one was open for 2% of the time, Pallas kernels for 16%

profile of v2, /device:TPU:56, one launch (start us, length us, event | category | flops | bytes accessed | tf_op | source)
XLA Modules:
  0.0 110.8 jit_solution(12016292350177116046)
XLA Ops:
  0.0 10.6 %all_gather.9.rows_ref = bf16[192,1536]{1,0:T(8,128)(2,1)} all-gather(bf16[192,384]{1,0:T(8,128)(2,1)} %param.9), channel_id=1, replica_groups=mesh['batch'=2,'z'=8,'y'=4,'xh'=2,'core'=2] {'xh','core'}, dimensions={1}, use_global_device_ids=true | all-gather | bytes 737280 | tf_op jit(solution)/shard_map/all_gather | solution.py:370
  10.6 4.5 %project.1 = (bf16[192,768]{1,0:T(8,128)(2,1)}, bf16[192,384]{1,0:T(8,128)(2,1)}) custom-call(bf16[192,1536]{1,0:T(8,128)(2,1)} %all_gather.9.rows_ref, f32[1536]{0:T(1024)} %gain_ref.2, bf16[3,1536,384]{2,1,0:T(8,128)(2,1)} %w_ref.1), custom_call_target="tpu_custom_call" | custom-call | tf_op jit(solution)/shard_map/project/pallas_call | solution.py:299
  15.1 2.0 %collective-permute-start.1 = (bf16[192,768]{1,0:T(8,128)(2,1)}, bf16[192,768]{1,0:T(8,128)(2,1)S(1)}, u32[]{:S(2)}, u32[]{:S(2)}) collective-permute-start(bf16[192,768]{1,0:T(8,128)(2,1)} %get-tuple-element.26.refs_2_.refs_1_), channel_id=1, source_target_pairs={{0,16},{16,32},{32,48},{48,64},{64,80},{80,96},{96,112},{112,0},{1... | collective-permute-start | bytes 884744 | tf_op jit(solution)/shard_map/ppermute | solution.py:353
  18.0 5.2 %collective-permute-done.refs_1_ = bf16[192,384]{1,0:T(8,128)(2,1)S(1)} collective-permute-done((bf16[192,384]{1,0:T(8,128)(2,1)}, bf16[192,384]{1,0:T(8,128)(2,1)S(1)}, u32[]{:S(2)}, u32[]{:S(2)}) %collective-permute-start) | collective-permute-done | bytes 147488 | tf_op jit(solution)/shard_map/ppermute | solution.py:349
  23.2 1.7 %collective-permute-start.14 = (bf16[384,1536]{1,0:T(8,128)(2,1)}, bf16[384,1536]{1,0:T(8,128)(2,1)}, u32[]{:S(2)}, u32[]{:S(2)}) collective-permute-start(bf16[384,1536]{1,0:T(8,128)(2,1)} %w0.1), channel_id=1, source_target_pairs={{0,2},{2,0},{1,3},{3,1},{4,6},{6,4},{5,7},{7,5},{8,10},{10,8},{9,1... | collective-permute-start | bytes 3538952 | tf_op jit(solution)/shard_map/ppermute | solution.py:349
  24.8 1.9 %collective-permute-start.2 = (bf16[192,768]{1,0:T(8,128)(2,1)S(1)}, bf16[192,768]{1,0:T(8,128)(2,1)S(1)}, u32[]{:S(2)}, u32[]{:S(2)}) collective-permute-start(bf16[192,768]{1,0:T(8,128)(2,1)S(1)} %collective-permute-done.1.refs_3_.refs_2_), channel_id=1, source_target_pairs={{0,16},{16,32},{32,48},{48,64},{64,80},{80,96},{96,112},{112,0},{1... | collective-permute-start | bytes 884744 | tf_op jit(solution)/shard_map/ppermute | solution.py:353
  26.8 2.3 %collective-permute-start.5 = (bf16[192,768]{1,0:T(8,128)(2,1)S(1)}, bf16[192,768]{1,0:T(8,128)(2,1)S(1)}, u32[]{:S(2)}, u32[]{:S(2)}) collective-permute-start(bf16[192,768]{1,0:T(8,128)(2,1)S(1)} %collective-permute-done.4.refs_4_.refs_3_), channel_id=1, source_target_pairs={{0,112},{16,0},{32,16},{48,32},{64,48},{80,64},{96,80},{112,96},{1... | collective-permute-start | bytes 884744 | tf_op jit(solution)/shard_map/ppermute | solution.py:353
  31.3 4.5 %collective-permute-done.2.refs_5_.refs_4_ = bf16[192,768]{1,0:T(8,128)(2,1)S(1)} collective-permute-done((bf16[192,768]{1,0:T(8,128)(2,1)S(1)}, bf16[192,768]{1,0:T(8,128)(2,1)S(1)}, u32[]{:S(2)}, u32[]{:S(2)}) %collective-permute-start.2) | collective-permute-done | bytes 294944 | tf_op jit(solution)/shard_map/ppermute | solution.py:353
  36.4 2.4 %collective-permute-start.6 = (bf16[192,768]{1,0:T(8,128)(2,1)S(1)}, bf16[192,768]{1,0:T(8,128)(2,1)S(1)}, u32[]{:S(2)}, u32[]{:S(2)}) collective-permute-start(bf16[192,768]{1,0:T(8,128)(2,1)S(1)} %collective-permute-done.5.refs_6_.refs_5_), channel_id=1, source_target_pairs={{0,112},{16,0},{32,16},{48,32},{64,48},{80,64},{96,80},{112,96},{1... | collective-permute-start | bytes 884744 | tf_op jit(solution)/shard_map/ppermute | solution.py:353
  38.8 3.2 %collective-permute-start.7 = (bf16[96,768]{1,0:T(8,128)(2,1)S(1)}, bf16[96,768]{1,0:T(8,128)(2,1)S(1)}, u32[]{:S(2)}, u32[]{:S(2)}) collective-permute-start(bf16[96,768]{1,0:T(8,128)(2,1)S(1)} %slice.16), channel_id=1, source_target_pairs={{0,32},{16,48},{32,64},{48,80},{64,96},{80,112},{96,0},{112,16},{1... | collective-permute-start | bytes 442376 | tf_op jit(solution)/shard_map/ppermute | solution.py:353
  43.3 2.5 %first_attention.2 = (f32[384,384]{1,0:T(8,128)S(1)}, f32[384,128]{1,0:T(8,128)S(1)}, f32[384,128]{1,0:T(8,128)S(1)}) custom-call(bf16[192,384]{1,0:T(8,128)(2,1)S(1)} %copy-done.3, bf16[192,384]{1,0:T(8,128)(2,1)S(1)} %collective-permute-done.refs_1_, bf16[192,768]{1,0:T(8,128)(2,1)S(1)} %copy-done.6, ...), custom_call_target="tpu_custom_call" | custom-call | flops 1509949440 | bytes 4194304 | tf_op jit(solution)/shard_map/first_attention/pallas_call | solution.py:139
  45.9 2.5 %first_attention.3 = (f32[384,384]{1,0:T(8,128)S(1)}, f32[384,128]{1,0:T(8,128)S(1)}, f32[384,128]{1,0:T(8,128)S(1)}) custom-call(bf16[384,384]{1,0:T(8,128)(2,1)S(1)} %collective-permute-done.9.refs_0_, bf16[192,768]{1,0:T(8,128)(2,1)S(1)} %copy-done.6, bf16[192,768]{1,0:T(8,128)(2,1)S(1)} %collective-permute-done.1.refs_3_.refs_2_, ...), custom_call_target="tpu_custom_call" | custom-call | flops 1509949440 | bytes 4194304 | tf_op jit(solution)/shard_map/first_attention/pallas_call | solution.py:139
  48.4 5.2 %collective-permute-done.7.refs_4_.refs_3_ = bf16[96,768]{1,0:T(8,128)(2,1)S(1)} collective-permute-done((bf16[96,768]{1,0:T(8,128)(2,1)S(1)}, bf16[96,768]{1,0:T(8,128)(2,1)S(1)}, u32[]{:S(2)}, u32[]{:S(2)}) %collective-permute-start.7) | collective-permute-done | bytes 147488 | tf_op jit(solution)/shard_map/ppermute | solution.py:353
  53.6 2.3 %last_attention.3 = (bf16[192,512]{1,0:T(8,128)(2,1)S(1)}, bf16[192,512]{1,0:T(8,128)(2,1)S(1)}) custom-call(bf16[384,384]{1,0:T(8,128)(2,1)S(1)} %collective-permute-done.9.refs_0_, bf16[192,768]{1,0:T(8,128)(2,1)S(1)} %collective-permute-done.3.refs_2_.refs_1_, bf16[192,768]{1,0:T(8,128)(2,1)S(1)} %collective-permute-done.6.refs_3_.refs_2_, ...), custom_call_target="tpu_custom_call" | custom-call | flops 1207959552 | bytes 4194304 | tf_op jit(solution)/shard_map/last_attention/pallas_call | solution.py:153
  57.2 2.2 %collective-permute-start.12 = (bf16[192,512]{1,0:T(8,128)(2,1)S(1)}, bf16[192,512]{1,0:T(8,128)(2,1)S(1)}, u32[]{:S(2)}, u32[]{:S(2)}) collective-permute-start(bf16[192,512]{1,0:T(8,128)(2,1)S(1)} %get-tuple-element.40), channel_id=1, source_target_pairs={{0,12},{4,8},{8,4},{12,0},{1,13},{5,9},{9,5},{13,1},{2,14},{6,10},... | collective-permute-start | bytes 589832 | tf_op jit(solution)/shard_map/ppermute | solution.py:349
  59.4 2.3 %last_attention.2 = (bf16[192,512]{1,0:T(8,128)(2,1)S(1)}, bf16[192,512]{1,0:T(8,128)(2,1)S(1)}) custom-call(bf16[192,384]{1,0:T(8,128)(2,1)S(1)} %copy-done.3, bf16[192,384]{1,0:T(8,128)(2,1)S(1)} %collective-permute-done.refs_1_, bf16[192,768]{1,0:T(8,128)(2,1)S(1)} %collective-permute-done.3.refs_2_.refs_1_, ...), custom_call_target="tpu_custom_call" | custom-call | flops 1207959552 | bytes 4194304 | tf_op jit(solution)/shard_map/last_attention/pallas_call | solution.py:153
  61.9 3.1 %collective-permute-done.11.refs_2_ = bf16[192,512]{1,0:T(8,128)(2,1)S(1)} collective-permute-done((bf16[192,512]{1,0:T(8,128)(2,1)S(1)}, bf16[192,512]{1,0:T(8,128)(2,1)S(1)}, u32[]{:S(2)}, u32[]{:S(2)}) %collective-permute-start.11) | collective-permute-done | bytes 196640 | tf_op jit(solution)/shard_map/ppermute | solution.py:349
  65.6 1.8 %collective-permute-done.10.refs_1_ = bf16[192,512]{1,0:T(8,128)(2,1)S(1)} collective-permute-done((bf16[192,512]{1,0:T(8,128)(2,1)S(1)}, bf16[192,512]{1,0:T(8,128)(2,1)S(1)}, u32[]{:S(2)}, u32[]{:S(2)}) %collective-permute-start.10) | collective-permute-done | bytes 196640 | tf_op jit(solution)/shard_map/ppermute | solution.py:349
  68.7 9.6 %all-gather = bf16[768,384]{1,0:T(8,128)(2,1)} all-gather(bf16[192,384]{1,0:T(8,128)(2,1)S(1)} %combine.1), channel_id=2, replica_groups=mesh['batch'=2,'z'=8,'y'=4,'xh'=2,'core'=2] {'xh','core'}, dimensions={0}, use_global_device_ids=true | all-gather | bytes 737280 | tf_op jit(solution)/shard_map/all_gather | solution.py:398
  78.3 6.2 %middle.1 = (bf16[192,384]{1,0:T(8,128)(2,1)}, bf16[192,384]{1,0:T(8,128)(2,1)}) custom-call(s32[1]{0:T(128)} %bitcast.place_ref, bf16[192,1536]{1,0:T(8,128)(2,1)} %all_gather.9.rows_ref, bf16[4,192,384]{2,1,0:T(8,128)(2,1)} %bitcast.3, bf16[384,1536]{1,0:T(8,128)(2,1)} %w0.1, bf16[384,1536]{1,0:T(8,128)(2,1)} %collective-permute-done.13.w1, ...), custom_call_target="tpu_custom_call" | custom-call | tf_op jit(solution)/shard_map/middle/pallas_call | solution.py:233
  85.2 5.6 %collective-permute-start.16 = (bf16[16,384]{1,0:T(8,128)(2,1)S(1)}, bf16[16,384]{1,0:T(8,128)(2,1)S(1)}, u32[]{:S(2)}, u32[]{:S(2)}) collective-permute-start(bf16[16,384]{1,0:T(8,128)(2,1)S(1)} %get-tuple-element.46), channel_id=1, source_target_pairs={{0,4},{4,8},{8,12},{12,16},{16,20},{20,24},{24,28},{28,32},{32,36}... | collective-permute-start | bytes 36872 | tf_op jit(solution)/shard_map/ppermute | solution.py:402
  90.9 1.9 %collective-permute-start.17 = (bf16[16,384]{1,0:T(8,128)(2,1)S(1)}, bf16[16,384]{1,0:T(8,128)(2,1)S(1)}, u32[]{:S(2)}, u32[]{:S(2)}) collective-permute-start(bf16[16,384]{1,0:T(8,128)(2,1)S(1)} %get-tuple-element.45), channel_id=1, source_target_pairs={{4,0},{8,4},{12,8},{16,12},{20,16},{24,20},{28,24},{32,28},{36,32}... | collective-permute-start | bytes 36872 | tf_op jit(solution)/shard_map/ppermute | solution.py:403
  92.8 5.8 %collective-permute-done.17.after_ref = bf16[16,384]{1,0:T(8,128)(2,1)S(1)} collective-permute-done((bf16[16,384]{1,0:T(8,128)(2,1)S(1)}, bf16[16,384]{1,0:T(8,128)(2,1)S(1)}, u32[]{:S(2)}, u32[]{:S(2)}) %collective-permute-start.17) | collective-permute-done | bytes 12320 | tf_op jit(solution)/shard_map/ppermute | solution.py:403
  104.5 5.6 %collective-permute-done.20 = bf16[192,384]{1,0:T(8,128)(2,1)S(1)} collective-permute-done((bf16[192,384]{1,0:T(8,128)(2,1)S(1)}, bf16[192,384]{1,0:T(8,128)(2,1)S(1)}, u32[]{:S(2)}, u32[]{:S(2)}) %collective-permute-start.20) | collective-permute-done | bytes 147488 | tf_op jit(solution)/shard_map/ppermute | solution.py:349
  (49 shorter events, 15.6 us)
Async XLA Ops:
  15.1 28.2 %copy-start.3 = (bf16[192,384]{1,0:T(8,128)(2,1)S(1)}, bf16[192,384]{1,0:T(8,128)(2,1)}, u32[]{:S(2)}) copy-start(bf16[192,384]{1,0:T(8,128)(2,1)} %get-tuple-element.25.refs_0_) | copy-start | bytes 442372
  15.1 28.2 %copy-start.6 = (bf16[192,768]{1,0:T(8,128)(2,1)S(1)}, bf16[192,768]{1,0:T(8,128)(2,1)}, u32[]{:S(2)}) copy-start(bf16[192,768]{1,0:T(8,128)(2,1)} %get-tuple-element.26.refs_2_.refs_1_) | copy-start | bytes 884740
  15.1 9.7 %collective-permute-start.1 = (bf16[192,768]{1,0:T(8,128)(2,1)}, bf16[192,768]{1,0:T(8,128)(2,1)S(1)}, u32[]{:S(2)}, u32[]{:S(2)}) collective-permute-start(bf16[192,768]{1,0:T(8,128)(2,1)} %get-tuple-element.26.refs_2_.refs_1_), channel_id=1, source_target_pairs={{0,16},{16,32},{32,48},{48,64},{64,80},{80,96},{96,112},{112,0},{1... | collective-permute-start | bytes 884744 | tf_op jit(solution)/shard_map/ppermute | solution.py:353
  17.1 9.6 %collective-permute-start.4 = (bf16[192,768]{1,0:T(8,128)(2,1)}, bf16[192,768]{1,0:T(8,128)(2,1)S(1)}, u32[]{:S(2)}, u32[]{:S(2)}) collective-permute-start(bf16[192,768]{1,0:T(8,128)(2,1)} %get-tuple-element.26.refs_2_.refs_1_), channel_id=1, source_target_pairs={{0,112},{16,0},{32,16},{48,32},{64,48},{80,64},{96,80},{112,96},{1... | collective-permute-start | bytes 884744 | tf_op jit(solution)/shard_map/ppermute | solution.py:353
  17.2 5.9 %collective-permute-start = (bf16[192,384]{1,0:T(8,128)(2,1)}, bf16[192,384]{1,0:T(8,128)(2,1)S(1)}, u32[]{:S(2)}, u32[]{:S(2)}) collective-permute-start(bf16[192,384]{1,0:T(8,128)(2,1)} %get-tuple-element.25.refs_0_), channel_id=1, source_target_pairs={{0,4},{4,0},{8,12},{12,8},{1,5},{5,1},{9,13},{13,9},{2,6},{6,2},{1... | collective-permute-start | bytes 442376 | tf_op jit(solution)/shard_map/ppermute | solution.py:349
  23.2 44.3 %collective-permute-start.14 = (bf16[384,1536]{1,0:T(8,128)(2,1)}, bf16[384,1536]{1,0:T(8,128)(2,1)}, u32[]{:S(2)}, u32[]{:S(2)}) collective-permute-start(bf16[384,1536]{1,0:T(8,128)(2,1)} %w0.1), channel_id=1, source_target_pairs={{0,2},{2,0},{1,3},{3,1},{4,6},{6,4},{5,7},{7,5},{8,10},{10,8},{9,1... | collective-permute-start | bytes 3538952 | tf_op jit(solution)/shard_map/ppermute | solution.py:349
  24.8 11.0 %collective-permute-start.2 = (bf16[192,768]{1,0:T(8,128)(2,1)S(1)}, bf16[192,768]{1,0:T(8,128)(2,1)S(1)}, u32[]{:S(2)}, u32[]{:S(2)}) collective-permute-start(bf16[192,768]{1,0:T(8,128)(2,1)S(1)} %collective-permute-done.1.refs_3_.refs_2_), channel_id=1, source_target_pairs={{0,16},{16,32},{32,48},{48,64},{64,80},{80,96},{96,112},{112,0},{1... | collective-permute-start | bytes 884744 | tf_op jit(solution)/shard_map/ppermute | solution.py:353
  26.8 9.6 %collective-permute-start.5 = (bf16[192,768]{1,0:T(8,128)(2,1)S(1)}, bf16[192,768]{1,0:T(8,128)(2,1)S(1)}, u32[]{:S(2)}, u32[]{:S(2)}) collective-permute-start(bf16[192,768]{1,0:T(8,128)(2,1)S(1)} %collective-permute-done.4.refs_4_.refs_3_), channel_id=1, source_target_pairs={{0,112},{16,0},{32,16},{48,32},{64,48},{80,64},{96,80},{112,96},{1... | collective-permute-start | bytes 884744 | tf_op jit(solution)/shard_map/ppermute | solution.py:353
  30.0 12.1 %collective-permute-start.9 = (bf16[384,384]{1,0:T(8,128)(2,1)S(1)}, bf16[384,384]{1,0:T(8,128)(2,1)S(1)}, u32[]{:S(2)}, u32[]{:S(2)}) collective-permute-start(bf16[384,384]{1,0:T(8,128)(2,1)S(1)} %pad_maximum_fusion), channel_id=1, source_target_pairs={{0,8},{4,12},{8,0},{12,4},{1,9},{5,13},{9,1},{13,5},{2,10},{6,14},... | collective-permute-start | bytes 884744 | tf_op jit(solution)/shard_map/ppermute | solution.py:349
  35.8 17.7 %collective-permute-start.3 = (bf16[192,768]{1,0:T(8,128)(2,1)S(1)}, bf16[192,768]{1,0:T(8,128)(2,1)S(1)}, u32[]{:S(2)}, u32[]{:S(2)}) collective-permute-start(bf16[192,768]{1,0:T(8,128)(2,1)S(1)} %collective-permute-done.2.refs_5_.refs_4_), channel_id=1, source_target_pairs={{0,16},{16,32},{32,48},{48,64},{64,80},{80,96},{96,112},{112,0},{1... | collective-permute-start | bytes 884744 | tf_op jit(solution)/shard_map/ppermute | solution.py:353
  36.4 17.2 %collective-permute-start.6 = (bf16[192,768]{1,0:T(8,128)(2,1)S(1)}, bf16[192,768]{1,0:T(8,128)(2,1)S(1)}, u32[]{:S(2)}, u32[]{:S(2)}) collective-permute-start(bf16[192,768]{1,0:T(8,128)(2,1)S(1)} %collective-permute-done.5.refs_6_.refs_5_), channel_id=1, source_target_pairs={{0,112},{16,0},{32,16},{48,32},{64,48},{80,64},{96,80},{112,96},{1... | collective-permute-start | bytes 884744 | tf_op jit(solution)/shard_map/ppermute | solution.py:353
  38.8 14.8 %collective-permute-start.7 = (bf16[96,768]{1,0:T(8,128)(2,1)S(1)}, bf16[96,768]{1,0:T(8,128)(2,1)S(1)}, u32[]{:S(2)}, u32[]{:S(2)}) collective-permute-start(bf16[96,768]{1,0:T(8,128)(2,1)S(1)} %slice.16), channel_id=1, source_target_pairs={{0,32},{16,48},{32,64},{48,80},{64,96},{80,112},{96,0},{112,16},{1... | collective-permute-start | bytes 442376 | tf_op jit(solution)/shard_map/ppermute | solution.py:353
  42.1 11.5 %collective-permute-start.8 = (bf16[96,768]{1,0:T(8,128)(2,1)S(1)}, bf16[96,768]{1,0:T(8,128)(2,1)S(1)}, u32[]{:S(2)}, u32[]{:S(2)}) collective-permute-start(bf16[96,768]{1,0:T(8,128)(2,1)S(1)} %slice.17), channel_id=1, source_target_pairs={{0,96},{16,112},{32,0},{48,16},{64,32},{80,48},{96,64},{112,80},{1... | collective-permute-start | bytes 442376 | tf_op jit(solution)/shard_map/ppermute | solution.py:353
  55.9 9.1 %collective-permute-start.11 = (bf16[192,512]{1,0:T(8,128)(2,1)S(1)}, bf16[192,512]{1,0:T(8,128)(2,1)S(1)}, u32[]{:S(2)}, u32[]{:S(2)}) collective-permute-start(bf16[192,512]{1,0:T(8,128)(2,1)S(1)} %get-tuple-element.39), channel_id=1, source_target_pairs={{0,8},{4,12},{8,0},{12,4},{1,9},{5,13},{9,1},{13,5},{2,10},{6,14},... | collective-permute-start | bytes 589832 | tf_op jit(solution)/shard_map/ppermute | solution.py:349
  57.2 8.4 %collective-permute-start.12 = (bf16[192,512]{1,0:T(8,128)(2,1)S(1)}, bf16[192,512]{1,0:T(8,128)(2,1)S(1)}, u32[]{:S(2)}, u32[]{:S(2)}) collective-permute-start(bf16[192,512]{1,0:T(8,128)(2,1)S(1)} %get-tuple-element.40), channel_id=1, source_target_pairs={{0,12},{4,8},{8,4},{12,0},{1,13},{5,9},{9,5},{13,1},{2,14},{6,10},... | collective-permute-start | bytes 589832 | tf_op jit(solution)/shard_map/ppermute | solution.py:349
  61.7 5.8 %collective-permute-start.10 = (bf16[192,512]{1,0:T(8,128)(2,1)S(1)}, bf16[192,512]{1,0:T(8,128)(2,1)S(1)}, u32[]{:S(2)}, u32[]{:S(2)}) collective-permute-start(bf16[192,512]{1,0:T(8,128)(2,1)S(1)} %get-tuple-element.38), channel_id=1, source_target_pairs={{0,4},{4,0},{8,12},{12,8},{1,5},{5,1},{9,13},{13,9},{2,6},{6,2},{1... | collective-permute-start | bytes 589832 | tf_op jit(solution)/shard_map/ppermute | solution.py:349
  61.8 16.4 %collective-permute-start.13 = (bf16[384,1536]{1,0:T(8,128)(2,1)}, bf16[384,1536]{1,0:T(8,128)(2,1)}, u32[]{:S(2)}, u32[]{:S(2)}) collective-permute-start(bf16[384,1536]{1,0:T(8,128)(2,1)} %w0.1), channel_id=1, source_target_pairs={{0,1},{1,0},{2,3},{3,2},{4,5},{5,4},{6,7},{7,6},{8,9},{9,8},{10,11... | collective-permute-start | bytes 3538952 | tf_op jit(solution)/shard_map/ppermute | solution.py:349
  67.4 10.8 %collective-permute-start.15 = (bf16[384,1536]{1,0:T(8,128)(2,1)}, bf16[384,1536]{1,0:T(8,128)(2,1)}, u32[]{:S(2)}, u32[]{:S(2)}) collective-permute-start(bf16[384,1536]{1,0:T(8,128)(2,1)} %collective-permute-done.14.w2), channel_id=1, source_target_pairs={{0,1},{1,0},{2,3},{3,2},{4,5},{5,4},{6,7},{7,6},{8,9},{9,8},{10,11... | collective-permute-start | bytes 3538952 | tf_op jit(solution)/shard_map/ppermute | solution.py:349
  67.4 33.5 %collective-permute-start.19 = (bf16[384,1536]{1,0:T(8,128)(2,1)S(1)}, bf16[384,1536]{1,0:T(8,128)(2,1)S(1)}, u32[]{:S(2)}, u32[]{:S(2)}) collective-permute-start(bf16[384,1536]{1,0:T(8,128)(2,1)S(1)} %copy-done), channel_id=1, source_target_pairs={{0,1},{1,0},{2,3},{3,2},{4,5},{5,4},{6,7},{7,6},{8,9},{9,8},{10,11... | collective-permute-start | bytes 3538952 | tf_op jit(solution)/shard_map/ppermute | solution.py:349
  78.3 20.3 %copy-start.4 = (bf16[31,384]{1,0:T(8,128)(2,1)S(1)}, bf16[31,384]{1,0:T(8,128)(2,1)}, u32[]{:S(2)}) copy-start(bf16[31,384]{1,0:T(8,128)(2,1)} %taps_ref.1) | copy-start | bytes 71428
  85.2 7.6 %collective-permute-start.16 = (bf16[16,384]{1,0:T(8,128)(2,1)S(1)}, bf16[16,384]{1,0:T(8,128)(2,1)S(1)}, u32[]{:S(2)}, u32[]{:S(2)}) collective-permute-start(bf16[16,384]{1,0:T(8,128)(2,1)S(1)} %get-tuple-element.46), channel_id=1, source_target_pairs={{0,4},{4,8},{8,12},{12,16},{16,20},{20,24},{24,28},{28,32},{32,36}... | collective-permute-start | bytes 36872 | tf_op jit(solution)/shard_map/ppermute | solution.py:402
  90.9 7.7 %collective-permute-start.17 = (bf16[16,384]{1,0:T(8,128)(2,1)S(1)}, bf16[16,384]{1,0:T(8,128)(2,1)S(1)}, u32[]{:S(2)}, u32[]{:S(2)}) collective-permute-start(bf16[16,384]{1,0:T(8,128)(2,1)S(1)} %get-tuple-element.45), channel_id=1, source_target_pairs={{4,0},{8,4},{12,8},{16,12},{20,16},{24,20},{28,24},{32,28},{36,32}... | collective-permute-start | bytes 36872 | tf_op jit(solution)/shard_map/ppermute | solution.py:403
  100.8 1.5 %collective-permute-start.18 = (bf16[192,384]{1,0:T(8,128)(2,1)S(1)}, bf16[192,384]{1,0:T(8,128)(2,1)S(1)}, u32[]{:S(2)}, u32[]{:S(2)}) collective-permute-start(bf16[192,384]{1,0:T(8,128)(2,1)S(1)} %depthwise.1.own_ref), channel_id=1, source_target_pairs={{0,1},{1,0},{2,3},{3,2},{4,5},{5,4},{6,7},{7,6},{8,9},{9,8},{10,11... | collective-permute-start | bytes 442376 | tf_op jit(solution)/shard_map/ppermute | solution.py:349
  102.6 7.5 %collective-permute-start.20 = (bf16[192,384]{1,0:T(8,128)(2,1)S(1)}, bf16[192,384]{1,0:T(8,128)(2,1)S(1)}, u32[]{:S(2)}, u32[]{:S(2)}) collective-permute-start(bf16[192,384]{1,0:T(8,128)(2,1)S(1)} %part_sum.3), channel_id=1, source_target_pairs={{0,2},{2,0},{1,3},{3,1},{4,6},{6,4},{5,7},{7,5},{8,10},{10,8},{9,1... | collective-permute-start | bytes 442376 | tf_op jit(solution)/shard_map/ppermute | solution.py:349
  (4 other events, 33.3 us)

commit v3 on v2

v3 whole, which is shorter than its diff:
```python
import functools
import math

import jax
import jax.numpy as jnp
from jax import lax
from jax.experimental import pallas as pl
from jax.experimental.pallas import tpu as pltpu
from jax.sharding import Mesh
from jax.sharding import PartitionSpec as P

D = 1536
HEAD = 96
HEADS_HERE = 4
COLS = 384
ROWS = 192
REACH = 15
HALO = 16
STATS = 16
TP = ("xh", "core")
CTX = ("z", "y")
Q_SCALE = math.log2(math.e) / math.sqrt(HEAD)
VMEM_LIMIT = 8 * 2**20
OVERLAPPED = pl.CostEstimate(flops=2 * 10**10, bytes_accessed=2**20, transcendentals=0)


def layer_norm(inputs, gain):
    inputs = inputs.astype(jnp.float32)
    average = jnp.mean(inputs, axis=-1, keepdims=True)
    centered = inputs - average
    variance = jnp.mean(centered * centered, axis=-1, keepdims=True)
    return (centered * lax.rsqrt(variance + 1e-05) * gain).astype(jnp.bfloat16)


def split_three(value):
    high = value.astype(jnp.bfloat16).astype(jnp.float32)
    rest = value - high
    mid = rest.astype(jnp.bfloat16).astype(jnp.float32)
    return high, mid, rest - mid


def head_window(head):
    start = 0 if head < 2 else 128
    lane = lax.broadcasted_iota(jnp.int32, (1, 256), 1) + start
    return start, (lane >= head * HEAD) & (lane < (head + 1) * HEAD)


def attend(queries, keys, values, head):
    start, inside = head_window(head)
    masked = jnp.where(inside, queries[:, start : start + 256], 0)
    window = jnp.concatenate([block[:, start : start + 256] for block in keys], 0)
    scores = lax.dot_general(
        masked, window, (((1,), (1,)), ((), ())), preferred_element_type=jnp.float32
    )
    top = jnp.max(scores, axis=1, keepdims=True)
    weights = jnp.exp2(scores - top)
    denominator = jnp.sum(weights, axis=1, keepdims=True)
    window = jnp.concatenate([block[:, start : start + 256] for block in values], 0)
    summed = jnp.dot(weights.astype(jnp.bfloat16), window, preferred_element_type=jnp.float32)
    return inside, summed, top, denominator


def widen(part, head):
    blank = jnp.zeros((part.shape[0], 128), jnp.float32)
    return jnp.concatenate([part, blank] if head < 2 else [blank, part], 1)


def split_refs(refs, count):
    keys = [ref.at[:, :COLS] for ref in refs[:count]]
    values = [ref.at[:, COLS:] for ref in refs[:count]]
    return keys, values, refs[count:]


def first_attention_kernel(places, blocks, *refs):
    pieces, refs = refs[: len(places)], refs[len(places) :]
    keys, values, rest = split_refs(refs, blocks)
    o_ref, top_ref, sum_ref = rest
    lane = lax.broadcasted_iota(jnp.int32, (1, 128), 1)
    queries = [ref[at * ROWS : (at + 1) * ROWS] for ref, at in zip(pieces, places)]
    queries = jnp.concatenate(queries, 0)
    count = queries.shape[0]
    total = jnp.zeros((count, COLS), jnp.float32)
    tops = jnp.zeros((count, 128), jnp.float32)
    sums = jnp.ones((count, 128), jnp.float32)
    for head in range(HEADS_HERE):
        inside, summed, top, denominator = attend(queries, keys, values, head)
        total = total + widen(jnp.where(inside, summed, 0.0), head)
        tops = jnp.where(lane == head, top, tops)
        sums = jnp.where(lane == head, denominator, sums)
    o_ref[...] = total
    top_ref[...] = tops
    sum_ref[...] = sums


def last_attention_kernel(places, blocks, *refs):
    pieces, refs = refs[: len(places)], refs[len(places) :]
    keys, values, rest = split_refs(refs, blocks)
    prior_ref, top_ref, sum_ref, *outs = rest
    lane = lax.broadcasted_iota(jnp.int32, (1, 128), 1)
    queries = [ref[at * ROWS : (at + 1) * ROWS] for ref, at in zip(pieces, places)]
    queries = jnp.concatenate(queries, 0)
    count = queries.shape[0]
    tops = jnp.zeros((count, 128), jnp.float32)
    sums = jnp.zeros((count, 128), jnp.float32)
    products = []
    for head in range(HEADS_HERE):
        inside, summed, top, denominator = attend(queries, keys, values, head)
        products.append((inside, summed))
        tops = jnp.where(lane == head, top, tops)
        sums = jnp.where(lane == head, denominator, sums)
    joint = jnp.maximum(tops, top_ref[...])
    rescale = jnp.exp2(tops - joint)
    prior_rescale = jnp.exp2(top_ref[...] - joint)
    denominator = sums * rescale + sum_ref[...] * prior_rescale
    inverse = 1.0 / denominator
    rescale = rescale * inverse
    prior_rescale = prior_rescale * inverse
    total = jnp.zeros((count, COLS), jnp.float32)
    for head, (inside, summed) in enumerate(products):
        start = 0 if head < 2 else 128
        part = (
            summed * rescale[:, head : head + 1]
            + prior_ref[:, start : start + 256] * prior_rescale[:, head : head + 1]
        )
        total = total + widen(jnp.where(inside, part, 0.0), head)
    high, mid, low = split_three(joint + jnp.log2(denominator))
    stats = jnp.where(
        lane < 4, high, jnp.where(lane < 8, pltpu.roll(mid, 4, 1), pltpu.roll(low, 8, 1))
    )
    for place, out in enumerate(outs):
        rows = slice(place * ROWS, (place + 1) * ROWS)
        out[:ROWS] = total[rows].astype(jnp.bfloat16)
        turned = jnp.concatenate([stats[rows], jnp.zeros((256 - ROWS, 128), jnp.float32)], 0)
        turned = jnp.transpose(turned)[:STATS].astype(jnp.bfloat16)
        blank = jnp.zeros((STATS, COLS - 256), jnp.bfloat16)
        out[ROWS:] = jnp.concatenate([turned, blank], 1)


def attention_cost(rows, blocks):
    flops = 2 * 2 * rows * ROWS * blocks * 256 * HEADS_HERE
    return pl.CostEstimate(flops=flops, bytes_accessed=4 * 2**20, transcendentals=0)


def first_attention(queries, blocks):
    places = tuple(at for _, at in queries)
    rows = len(places) * ROWS
    return pl.pallas_call(
        functools.partial(first_attention_kernel, places, len(blocks)),
        out_shape=[
            jax.ShapeDtypeStruct((rows, COLS), jnp.float32),
            jax.ShapeDtypeStruct((rows, 128), jnp.float32),
            jax.ShapeDtypeStruct((rows, 128), jnp.float32),
        ],
        compiler_params=pltpu.CompilerParams(vmem_limit_bytes=VMEM_LIMIT),
        cost_estimate=attention_cost(rows, len(blocks)),
        name="first_attention",
    )(*[query for query, _ in queries], *blocks)


def last_attention(queries, blocks, prior):
    places = tuple(at for _, at in queries)
    rows = len(places) * ROWS
    return pl.pallas_call(
        functools.partial(last_attention_kernel, places, len(blocks)),
        out_shape=[jax.ShapeDtypeStruct((ROWS + STATS, COLS), jnp.bfloat16)] * (rows // ROWS),
        compiler_params=pltpu.CompilerParams(vmem_limit_bytes=VMEM_LIMIT),
        cost_estimate=attention_cost(rows, len(blocks)),
        name="last_attention",
    )(*[query for query, _ in queries], *blocks, *prior)


def combine_kernel(*refs):
    parts, o_ref = refs[:-1], refs[-1]
    lane = lax.broadcasted_iota(jnp.int32, (1, COLS), 1)
    logs = []
    for part in parts:
        stats = part[ROWS:, :256].astype(jnp.float32)
        logs.append(stats[0:4] + stats[4:8] + stats[8:12])
    top = functools.reduce(jnp.maximum, logs)
    shares = [jnp.exp2(log - top) for log in logs]
    inverse = 1.0 / functools.reduce(jnp.add, shares)
    shares = jnp.concatenate([share * inverse for share in shares], 0)
    blank = jnp.zeros((128 - shares.shape[0], 256), jnp.float32)
    shares = jnp.transpose(jnp.concatenate([shares, blank], 0))[:ROWS]
    total = jnp.zeros((ROWS, COLS), jnp.float32)
    for place, part in enumerate(parts):
        spread = jnp.zeros((ROWS, COLS), jnp.float32)
        for head in range(HEADS_HERE):
            inside = (lane >= head * HEAD) & (lane < (head + 1) * HEAD)
            column = place * HEADS_HERE + head
            spread = jnp.where(inside, shares[:, column : column + 1], spread)
        total = total + spread * part[:ROWS].astype(jnp.float32)
    o_ref[...] = total.astype(jnp.bfloat16)


def combine(parts):
    return pl.pallas_call(
        combine_kernel,
        out_shape=jax.ShapeDtypeStruct((ROWS, COLS), jnp.bfloat16),
        compiler_params=pltpu.CompilerParams(vmem_limit_bytes=VMEM_LIMIT),
        cost_estimate=OVERLAPPED,
        name="combine",
    )(*parts)


def middle_kernel(
    rows_ref, context_ref, w0, w1, w2, w3, gain_ref, glu_ref, m_ref, g_ref, top_ref, end_ref
):
    place = lax.axis_index(TP)
    total = rows_ref[...].astype(jnp.float32)
    for offset, weight in enumerate((w0, w1, w2, w3)):
        total = total + jnp.dot(
            context_ref[place ^ offset], weight[...], preferred_element_type=jnp.float32
        )
    middle = total.astype(jnp.bfloat16)
    for position in range(4):

        @pl.when(place == position)
        def _():
            m_ref[...] = middle[:, position * COLS : (position + 1) * COLS]

    normed = layer_norm(middle, gain_ref[...].reshape(1, D))
    value = jnp.dot(normed, glu_ref[0], preferred_element_type=jnp.float32)
    gate = jnp.dot(normed, glu_ref[1], preferred_element_type=jnp.float32)
    glu = (value * (1.0 / (1.0 + jnp.exp(-gate)))).astype(jnp.bfloat16)
    g_ref[...] = glu
    top_ref[...] = glu[:HALO]
    end_ref[...] = glu[ROWS - HALO :]


def middle_and_glu(rows, context, weights, gain, glu_weight):
    vmem = pl.BlockSpec(memory_space=pltpu.VMEM)
    return pl.pallas_call(
        middle_kernel,
        in_specs=[vmem] * 8,
        out_specs=[vmem] * 4,
        out_shape=[jax.ShapeDtypeStruct((ROWS, COLS), jnp.bfloat16)] * 2
        + [jax.ShapeDtypeStruct((HALO, COLS), jnp.bfloat16)] * 2,
        compiler_params=pltpu.CompilerParams(vmem_limit_bytes=VMEM_LIMIT),
        cost_estimate=OVERLAPPED,
        name="middle",
    )(rows, context, *weights, gain, glu_weight)


def convolve(held, taps_ref, bias_ref, count, store):
    taps = taps_ref[...].astype(jnp.float32)
    for column in range(COLS // 128):
        here = slice(column * 128, (column + 1) * 128)
        total = jnp.zeros((count, 128), jnp.float32) + bias_ref[here].reshape(1, 128)
        for tap in range(2 * REACH + 1):
            begin = HALO - REACH + tap
            total = total + held[begin : begin + count, here] * taps[tap : tap + 1, here]
        store(here, (total / (1.0 + jnp.exp(-total))).astype(jnp.bfloat16))


def inner_kernel(glu_ref, taps_ref, bias_ref, o_ref, held):
    held[...] = glu_ref[...].astype(jnp.float32)

    def store(here, value):
        o_ref[:, here] = value

    convolve(held, taps_ref, bias_ref, ROWS - 2 * HALO, store)


def edges_kernel(before_ref, glu_ref, after_ref, inner_ref, taps_ref, bias_ref, o_ref, held):
    o_ref[HALO : ROWS - HALO] = inner_ref[...]
    for side in range(2):
        if side == 0:
            held[:HALO] = before_ref[...].astype(jnp.float32)
            held[HALO:] = glu_ref[: 2 * HALO].astype(jnp.float32)
        else:
            held[: 2 * HALO] = glu_ref[ROWS - 2 * HALO :].astype(jnp.float32)
            held[2 * HALO :] = after_ref[...].astype(jnp.float32)

        def store(here, value):
            o_ref[side * (ROWS - HALO) : side * (ROWS - HALO) + HALO, here] = value

        convolve(held, taps_ref, bias_ref, HALO, store)


def depthwise(before, glu, after, taps, bias):
    inner = pl.pallas_call(
        inner_kernel,
        out_shape=jax.ShapeDtypeStruct((ROWS - 2 * HALO, COLS), jnp.bfloat16),
        scratch_shapes=[pltpu.VMEM((ROWS, COLS), jnp.float32)],
        compiler_params=pltpu.CompilerParams(vmem_limit_bytes=VMEM_LIMIT),
        name="inner",
    )(glu, taps, bias)
    return pl.pallas_call(
        edges_kernel,
        out_shape=jax.ShapeDtypeStruct((ROWS, COLS), jnp.bfloat16),
        scratch_shapes=[pltpu.VMEM((3 * HALO, COLS), jnp.float32)],
        compiler_params=pltpu.CompilerParams(vmem_limit_bytes=VMEM_LIMIT),
        name="edges",
    )(before, glu, after, inner, taps, bias)


def project_kernel(rows_ref, gain_ref, w_ref, kv_ref, q_ref):
    normed = layer_norm(rows_ref[...], gain_ref[...].reshape(1, D))
    for half in range(2):
        kv_ref[:, half * COLS : (half + 1) * COLS] = jnp.dot(
            normed, w_ref[1 + half], preferred_element_type=jnp.float32
        ).astype(jnp.bfloat16)
    query = jnp.dot(normed, w_ref[0], preferred_element_type=jnp.float32)
    q_ref[...] = (query * Q_SCALE).astype(jnp.bfloat16)


def project(rows, gain, weights):
    return pl.pallas_call(
        project_kernel,
        out_shape=[
            jax.ShapeDtypeStruct((ROWS, 2 * COLS), jnp.bfloat16),
            jax.ShapeDtypeStruct((ROWS, COLS), jnp.bfloat16),
        ],
        compiler_params=pltpu.CompilerParams(vmem_limit_bytes=VMEM_LIMIT),
        name="project",
    )(rows, gain, weights)


def stage_kernel(frames_ref, o_ref):
    o_ref[...] = frames_ref[...]


def stage(frames):
    return pl.pallas_call(
        stage_kernel,
        out_shape=jax.ShapeDtypeStruct(frames.shape, frames.dtype),
        compiler_params=pltpu.CompilerParams(vmem_limit_bytes=VMEM_LIMIT),
        cost_estimate=OVERLAPPED,
        name="stage",
    )(frames)


def join_kernel(a_ref, b_ref, o_ref):
    o_ref[:ROWS] = a_ref[...]
    o_ref[ROWS:] = b_ref[...]


def join(a, b):
    return pl.pallas_call(
        join_kernel,
        out_shape=jax.ShapeDtypeStruct((2 * ROWS, COLS), jnp.bfloat16),
        compiler_params=pltpu.CompilerParams(vmem_limit_bytes=VMEM_LIMIT),
        name="join",
    )(a, b)


def halves_kernel(a_ref, b_ref, a_out, b_out):
    a_out[...] = a_ref[: ROWS // 2]
    b_out[...] = b_ref[ROWS // 2 :]


def halves(a, b):
    return pl.pallas_call(
        halves_kernel,
        out_shape=[jax.ShapeDtypeStruct((ROWS // 2, 2 * COLS), jnp.bfloat16)] * 2,
        compiler_params=pltpu.CompilerParams(vmem_limit_bytes=VMEM_LIMIT),
        name="halves",
    )(a, b)


def part_kernel(flip, own_ref, other_ref, w_own, w_other, *refs):
    o_ref = refs[-1]
    columns = pl.ds(pl.multiple_of((lax.axis_index(TP) ^ flip) * COLS, 128), COLS)
    total = jnp.dot(own_ref[...], w_own[:, columns], preferred_element_type=jnp.float32)
    total = total + jnp.dot(
        other_ref[...], w_other[:, columns], preferred_element_type=jnp.float32
    )
    for extra in refs[:-1]:
        total = total + extra[...].astype(jnp.float32)
    o_ref[...] = total.astype(o_ref.dtype)


def part_sum(flip, own, other, weights, extra):
    vmem = pl.BlockSpec(memory_space=pltpu.VMEM)
    return pl.pallas_call(
        functools.partial(part_kernel, flip),
        in_specs=[vmem] * (4 + len(extra)),
        out_specs=vmem,
        out_shape=jax.ShapeDtypeStruct((ROWS, COLS), jnp.bfloat16),
        compiler_params=pltpu.CompilerParams(vmem_limit_bytes=VMEM_LIMIT),
        cost_estimate=pl.CostEstimate(
            flops=4 * ROWS * COLS * COLS, bytes_accessed=3 * 2**20, transcendentals=0
        ),
        name="part_sum",
    )(own, other, *weights, *extra)


def swap(value, axis, count, flip):
    return lax.ppermute(value, axis, [(i, i ^ flip) for i in range(count)])


def shift(value, axis, count, offset):
    return lax.ppermute(value, axis, [(i, (i + offset) % count) for i in range(count)])


def per_device(
    frames,
    attn_gain,
    query_key_value,
    out_weight,
    conv_gain,
    glu_weight,
    depth_kernel,
    depth_bias,
    proj_weight,
):
    out_core = swap(out_weight, "core", 2, 1)
    out_far = swap(out_weight, "xh", 2, 1)
    whole_rows = lax.all_gather(stage(frames), TP, axis=1, tiled=True)
    mine, query = project(whole_rows, attn_gain, query_key_value)
    lower1, upper1 = shift(mine, "z", 8, 1), shift(mine, "z", 8, -1)
    query1 = swap(query, "y", 4, 1)
    lower2, upper2 = shift(lower1, "z", 8, 1), shift(upper1, "z", 8, -1)
    pair2 = swap(join(query, query1), "y", 4, 2)
    low_half, high_half = halves(lower2, upper2)
    second = [
        shift(lower2, "z", 8, 1),
        shift(upper2, "z", 8, -1),
        shift(low_half, "z", 8, 2),
        shift(high_half, "z", 8, -2),
    ]
    blocks = [mine, lower1, upper1, lower2, upper2]
    groups = ([(pair2, 0)], [(query1, 0), (pair2, 1)], [(query, 0)])
    priors = [first_attention(group, blocks) for group in groups]
    (partial2,) = last_attention(groups[0], second, priors[0])
    part2 = swap(partial2, "y", 4, 2)
    partial1, partial3 = last_attention(groups[1], second, priors[1])
    part1, part3 = swap(partial1, "y", 4, 1), swap(partial3, "y", 4, 3)
    (partial0,) = last_attention(groups[2], second, priors[2])
    out_far_core = swap(out_far, "core", 2, 1)
    out_pieces = (out_weight, out_core, out_far, out_far_core)
    context = combine([partial0, part1, part2, part3])
    proj_core = swap(proj_weight, "core", 2, 1)
    context = lax.all_gather(context, TP, axis=0, tiled=False)
    middle, glu, top, end = middle_and_glu(
        whole_rows, context, out_pieces, conv_gain, glu_weight
    )
    before = lax.ppermute(end, CTX, [(i, i + 1) for i in range(31)])
    after = lax.ppermute(top, CTX, [(i + 1, i) for i in range(31)])
    activated = depthwise(before, glu, after, depth_kernel, depth_bias)
    other = swap(activated, "core", 2, 1)
    weights = (proj_weight, proj_core)
    theirs = swap(part_sum(2, activated, other, weights, ()), "xh", 2, 1)
    return part_sum(0, activated, other, weights, (middle, theirs))


def solution(mesh):
    parted = Mesh(mesh.devices.reshape(2, 8, 4, 2, 2), ("batch", "z", "y", "xh", "core"))
    in_specs = (
        P(("batch",) + CTX, TP),
        P(),
        P(None, None, TP),
        P(TP, None),
        P(),
        P(None, None, TP),
        P(None, TP),
        P(TP),
        P(TP, None),
    )
    out_specs = P(("batch",) + CTX, TP)
    return jax.shard_map(
        per_device, mesh=parted, in_specs=in_specs, out_specs=out_specs, check_vma=False
    )
```

time: 111 us -> 99.7 us (0.90)
  waiting for transfers between devices: 33.7 us -> 27.2 us
  Pallas kernels: 23.1 us -> 20.4 us
  starting transfers between devices: 30.4 us -> 32.4 us
  blocking collectives: 20.2 us -> 18.4 us
  other arithmetic: 1.63 us -> 0 us
    ppermute x11, waiting for transfers between devices: 17.7 us -> 6.63 us  [swap(): return lax.ppermute(value, axis, [(i, i ^ flip) for i in range(count)])]
    ppermute x8, waiting for transfers between devices: 10.2 us -> 16 us  [shift(): lax.ppermute(value, axis, [(i, (i + offset) % count) for i in range(count)])]
    pallas_call x9 -> x15, Pallas kernels: 22.3 us -> 19.7 us  [the longest x3 6.69 us: first_attention(): pl.pallas_call(functools.partial(first_attention_kernel, places, len(bloc...]
    ppermute x11, starting transfers between devices: 9.57 us -> 11.9 us  [swap(): return lax.ppermute(value, axis, [(i, i ^ flip) for i in range(count)])]
    all_gather x1, blocking collectives: 10.6 us -> 9.19 us  [per_device(): whole_rows = lax.all_gather(stage(frames), TP, axis=1, tiled=True)]
    ppermute x2, waiting for transfers between devices: 5.76 us -> 4.62 us  [the longest x1 4.61 us: per_device(): after = lax.ppermute(top, CTX, [(i + 1, i) for i in range(31)])]
  transfers between devices with their start and end apart: 21 -> 21, of which waited for: 10 -> 7; matrix products, arithmetic and copies ran while one was open for 2% -> 0% of each run, Pallas kernels for 16% -> 18%
where the time goes in v3:
time: 99.7 us; the launch traced here: 99.6 us
  starting transfers between devices  32.4 us (32%)
  waiting for transfers between devices  27.2 us (27%)
  Pallas kernels  20.4 us (20%)
  blocking collectives  18.4 us (18%)
    ppermute x8, waiting for transfers between devices, shift(): lax.ppermute(value, axis, [(i, (i + offset) % count) for i in range(count)])  16 us
    ppermute x8, starting transfers between devices, shift(): lax.ppermute(value, axis, [(i, (i + offset) % count) for i in range(count)])  13.1 us
    ppermute x11, starting transfers between devices, swap(): return lax.ppermute(value, axis, [(i, i ^ flip) for i in range(count)])  11.9 us
    all_gather x1, blocking collectives, per_device(): context = lax.all_gather(context, TP, axis=0, tiled=False)  9.24 us
    all_gather x1, blocking collectives, per_device(): whole_rows = lax.all_gather(stage(frames), TP, axis=1, tiled=True)  9.19 us
    pallas_call x3, Pallas kernels, first_attention(): pl.pallas_call(functools.partial(first_attention_kernel, places, len(bloc...  6.69 us
    ppermute x11, waiting for transfers between devices, swap(): return lax.ppermute(value, axis, [(i, i ^ flip) for i in range(count)])  6.63 us
    pallas_call x3, Pallas kernels, last_attention(): pl.pallas_call(functools.partial(last_attention_kernel, places, len(block...  6.19 us
  transfers between devices with their start and end apart: 21, of which 7 were waited for; matrix products, arithmetic and copies ran while one was open for 0% of the time, Pallas kernels for 18%

profile of v3, /device:TPU:56, one launch (start us, length us, event | category | flops | bytes accessed | tf_op | source)
XLA Modules:
  0.0 99.6 jit_solution(9608763036785115626)
XLA Ops:
  0.9 9.2 %all_gather.9.rows_ref = bf16[192,1536]{1,0:T(8,128)(2,1)S(1)} all-gather(bf16[192,384]{1,0:T(8,128)(2,1)S(1)} %stage.1), channel_id=1, replica_groups=mesh['batch'=2,'z'=8,'y'=4,'xh'=2,'core'=2] {'xh','core'}, dimensions={1}, use_global_device_ids=true | all-gather | bytes 737280 | tf_op jit(solution)/shard_map/all_gather | solution.py:410
  11.6 2.0 %collective-permute-start = (bf16[192,768]{1,0:T(8,128)(2,1)S(1)}, bf16[192,768]{1,0:T(8,128)(2,1)S(1)}, u32[]{:S(2)}, u32[]{:S(2)}) collective-permute-start(bf16[192,768]{1,0:T(8,128)(2,1)S(1)} %get-tuple-element.25.refs_1_.refs_2_), channel_id=1, source_target_pairs={{0,16},{16,32},{32,48},{48,64},{64,80},{80,96},{96,112},{112,0},{1... | collective-permute-start | bytes 884744 | tf_op jit(solution)/shard_map/ppermute | solution.py:394
  13.7 2.6 %collective-permute-start.14 = (bf16[384,1536]{1,0:T(8,128)(2,1)S(1)}, bf16[384,1536]{1,0:T(8,128)(2,1)S(1)}, u32[]{:S(2)}, u32[]{:S(2)}) collective-permute-start(bf16[384,1536]{1,0:T(8,128)(2,1)S(1)} %copy-done.6), channel_id=1, source_target_pairs={{0,2},{2,0},{1,3},{3,1},{4,6},{6,4},{5,7},{7,5},{8,10},{10,8},{9,1... | collective-permute-start | bytes 3538952 | tf_op jit(solution)/shard_map/ppermute | solution.py:390
  17.0 3.9 %collective-permute-done.refs_2_.refs_3_ = bf16[192,768]{1,0:T(8,128)(2,1)S(1)} collective-permute-done((bf16[192,768]{1,0:T(8,128)(2,1)S(1)}, bf16[192,768]{1,0:T(8,128)(2,1)S(1)}, u32[]{:S(2)}, u32[]{:S(2)}) %collective-permute-start) | collective-permute-done | bytes 294944 | tf_op jit(solution)/shard_map/ppermute | solution.py:394
  20.9 1.9 %collective-permute-start.1 = (bf16[192,768]{1,0:T(8,128)(2,1)S(1)}, bf16[192,768]{1,0:T(8,128)(2,1)S(1)}, u32[]{:S(2)}, u32[]{:S(2)}) collective-permute-start(bf16[192,768]{1,0:T(8,128)(2,1)S(1)} %collective-permute-done.refs_2_.refs_3_), channel_id=1, source_target_pairs={{0,16},{16,32},{32,48},{48,64},{64,80},{80,96},{96,112},{112,0},{1... | collective-permute-start | bytes 884744 | tf_op jit(solution)/shard_map/ppermute | solution.py:394
  22.9 2.3 %collective-permute-start.4 = (bf16[192,768]{1,0:T(8,128)(2,1)S(1)}, bf16[192,768]{1,0:T(8,128)(2,1)S(1)}, u32[]{:S(2)}, u32[]{:S(2)}) collective-permute-start(bf16[192,768]{1,0:T(8,128)(2,1)S(1)} %collective-permute-done.3.refs_3_.refs_4_), channel_id=1, source_target_pairs={{0,112},{16,0},{32,16},{48,32},{64,48},{80,64},{96,80},{112,96},{1... | collective-permute-start | bytes 884744 | tf_op jit(solution)/shard_map/ppermute | solution.py:394
  26.5 5.7 %collective-permute-done.1.a_ref.refs_4_.refs_5_ = bf16[192,768]{1,0:T(8,128)(2,1)S(1)} collective-permute-done((bf16[192,768]{1,0:T(8,128)(2,1)S(1)}, bf16[192,768]{1,0:T(8,128)(2,1)S(1)}, u32[]{:S(2)}, u32[]{:S(2)}) %collective-permute-start.1) | collective-permute-done | bytes 294944 | tf_op jit(solution)/shard_map/ppermute | solution.py:394
  32.6 2.5 %collective-permute-start.5 = (bf16[192,768]{1,0:T(8,128)(2,1)S(1)}, bf16[192,768]{1,0:T(8,128)(2,1)S(1)}, u32[]{:S(2)}, u32[]{:S(2)}) collective-permute-start(bf16[192,768]{1,0:T(8,128)(2,1)S(1)} %collective-permute-done.4.b_ref.refs_5_.refs_6_), channel_id=1, source_target_pairs={{0,112},{16,0},{32,16},{48,32},{64,48},{80,64},{96,80},{112,96},{1... | collective-permute-start | bytes 884744 | tf_op jit(solution)/shard_map/ppermute | solution.py:394
  35.2 3.2 %collective-permute-start.6 = (bf16[96,768]{1,0:T(8,128)(2,1)S(1)}, bf16[96,768]{1,0:T(8,128)(2,1)S(1)}, u32[]{:S(2)}, u32[]{:S(2)}) collective-permute-start(bf16[96,768]{1,0:T(8,128)(2,1)S(1)} %get-tuple-element.26), channel_id=1, source_target_pairs={{0,32},{16,48},{32,64},{48,80},{64,96},{80,112},{96,0},{112,16},{1... | collective-permute-start | bytes 442376 | tf_op jit(solution)/shard_map/ppermute | solution.py:394
  39.4 2.1 %first_attention.5 = (f32[192,384]{1,0:T(8,128)S(1)}, f32[192,128]{1,0:T(8,128)S(1)}, f32[192,128]{1,0:T(8,128)S(1)}) custom-call(bf16[384,384]{1,0:T(8,128)(2,1)S(1)} %collective-permute-done.9.refs_1_.refs_0_, bf16[192,768]{1,0:T(8,128)(2,1)S(1)} %get-tuple-element.25.refs_1_.refs_2_, bf16[192,768]{1,0:T(8,128)(2,1)S(1)} %collective-permute-done.refs_2_.refs_3_, ...), custom_call_target="tpu_custom_call" | custom-call | flops 754974720 | bytes 4194304 | tf_op jit(solution)/shard_map/first_attention/pallas_call | solution.py:147
  41.5 2.5 %first_attention.4 = (f32[384,384]{1,0:T(8,128)S(1)}, f32[384,128]{1,0:T(8,128)S(1)}, f32[384,128]{1,0:T(8,128)S(1)}) custom-call(bf16[192,384]{1,0:T(8,128)(2,1)S(1)} %collective-permute-done.8.b_ref.refs_0_, bf16[384,384]{1,0:T(8,128)(2,1)S(1)} %collective-permute-done.9.refs_1_.refs_0_, bf16[192,768]{1,0:T(8,128)(2,1)S(1)} %get-tuple-element.25.refs_1_.refs_2_, ...), custom_call_target="tpu_custom_call" | custom-call | flops 1509949440 | bytes 4194304 | tf_op jit(solution)/shard_map/first_attention/pallas_call | solution.py:147
  44.0 6.0 %collective-permute-done.6.refs_3_.refs_4_ = bf16[96,768]{1,0:T(8,128)(2,1)S(1)} collective-permute-done((bf16[96,768]{1,0:T(8,128)(2,1)S(1)}, bf16[96,768]{1,0:T(8,128)(2,1)S(1)}, u32[]{:S(2)}, u32[]{:S(2)}) %collective-permute-start.6) | collective-permute-done | bytes 147488 | tf_op jit(solution)/shard_map/ppermute | solution.py:394
  50.0 1.9 %last_attention.5 = bf16[208,384]{1,0:T(8,128)(2,1)S(1)} custom-call(bf16[384,384]{1,0:T(8,128)(2,1)S(1)} %collective-permute-done.9.refs_1_.refs_0_, bf16[192,768]{1,0:T(8,128)(2,1)S(1)} %collective-permute-done.2.refs_1_.refs_2_, bf16[192,768]{1,0:T(8,128)(2,1)S(1)} %collective-permute-done.5.refs_2_.refs_3_, ...), custom_call_target="tpu_custom_call" | custom-call | flops 603979776 | bytes 4194304 | tf_op jit(solution)/shard_map/last_attention/pallas_call | solution.py:163
  53.1 2.3 %last_attention.4 = (bf16[208,384]{1,0:T(8,128)(2,1)S(1)}, bf16[208,384]{1,0:T(8,128)(2,1)S(1)}) custom-call(bf16[192,384]{1,0:T(8,128)(2,1)S(1)} %collective-permute-done.8.b_ref.refs_0_, bf16[384,384]{1,0:T(8,128)(2,1)S(1)} %collective-permute-done.9.refs_1_.refs_0_, bf16[192,768]{1,0:T(8,128)(2,1)S(1)} %collective-permute-done.2.refs_1_.refs_2_, ...), custom_call_target="tpu_custom_call" | custom-call | flops 1207959552 | bytes 4194304 | tf_op jit(solution)/shard_map/last_attention/pallas_call | solution.py:163
  55.5 3.0 %collective-permute-start.12 = (bf16[208,384]{1,0:T(8,128)(2,1)S(1)}, bf16[208,384]{1,0:T(8,128)(2,1)S(1)}, u32[]{:S(2)}, u32[]{:S(2)}) collective-permute-start(bf16[208,384]{1,0:T(8,128)(2,1)S(1)} %get-tuple-element.38), channel_id=1, source_target_pairs={{0,12},{4,8},{8,4},{12,0},{1,13},{5,9},{9,5},{13,1},{2,14},{6,10},... | collective-permute-start | bytes 479240 | tf_op jit(solution)/shard_map/ppermute | solution.py:390
  58.5 2.1 %first_attention.3 = (f32[192,384]{1,0:T(8,128)S(1)}, f32[192,128]{1,0:T(8,128)S(1)}, f32[192,128]{1,0:T(8,128)S(1)}) custom-call(bf16[192,384]{1,0:T(8,128)(2,1)S(1)} %get-tuple-element.24.refs_0_.a_ref, bf16[192,768]{1,0:T(8,128)(2,1)S(1)} %get-tuple-element.25.refs_1_.refs_2_, bf16[192,768]{1,0:T(8,128)(2,1)S(1)} %collective-permute-done.refs_2_.refs_3_, ...), custom_call_target="tpu_custom_call" | custom-call | flops 754974720 | bytes 4194304 | tf_op jit(solution)/shard_map/first_attention/pallas_call | solution.py:147
  60.6 1.9 %last_attention.3.refs_0_ = bf16[208,384]{1,0:T(8,128)(2,1)S(1)} custom-call(bf16[192,384]{1,0:T(8,128)(2,1)S(1)} %get-tuple-element.24.refs_0_.a_ref, bf16[192,768]{1,0:T(8,128)(2,1)S(1)} %collective-permute-done.2.refs_1_.refs_2_, bf16[192,768]{1,0:T(8,128)(2,1)S(1)} %collective-permute-done.5.refs_2_.refs_3_, ...), custom_call_target="tpu_custom_call" | custom-call | flops 603979776 | bytes 4194304 | tf_op jit(solution)/shard_map/last_attention/pallas_call | solution.py:163
  64.0 9.2 %all-gather = bf16[768,384]{1,0:T(8,128)(2,1)S(1)} all-gather(bf16[192,384]{1,0:T(8,128)(2,1)S(1)} %combine.1), channel_id=2, replica_groups=mesh['batch'=2,'z'=8,'y'=4,'xh'=2,'core'=2] {'xh','core'}, dimensions={0}, use_global_device_ids=true | all-gather | bytes 737280 | tf_op jit(solution)/shard_map/all_gather | solution.py:435
  73.3 2.5 %middle.1 = (bf16[192,384]{1,0:T(8,128)(2,1)S(1)}, bf16[192,384]{1,0:T(8,128)(2,1)S(1)}, bf16[16,384]{1,0:T(8,128)(2,1)S(1)}, bf16[16,384]{1,0:T(8,128)(2,1)S(1)}) custom-call(bf16[192,1536]{1,0:T(8,128)(2,1)S(1)} %all_gather.9.rows_ref, bf16[4,192,384]{2,1,0:T(8,128)(2,1)S(1)} %bitcast.1, bf16[384,1536]{1,0:T(8,128)(2,1)S(1)} %copy-done.6, ...), custom_call_target="tpu_custom_call" | custom-call | flops 20000000000 | bytes 1048576 | tf_op jit(solution)/shard_map/middle/pallas_call | solution.py:233
  75.8 5.4 %collective-permute-start.16 = (bf16[16,384]{1,0:T(8,128)(2,1)S(1)}, bf16[16,384]{1,0:T(8,128)(2,1)S(1)}, u32[]{:S(2)}, u32[]{:S(2)}) collective-permute-start(bf16[16,384]{1,0:T(8,128)(2,1)S(1)} %get-tuple-element.39), channel_id=1, source_target_pairs={{0,4},{4,8},{8,12},{12,16},{16,20},{20,24},{24,28},{28,32},{32,36}... | collective-permute-start | bytes 36872 | tf_op jit(solution)/shard_map/ppermute | solution.py:439
  81.3 1.9 %collective-permute-start.17 = (bf16[16,384]{1,0:T(8,128)(2,1)S(1)}, bf16[16,384]{1,0:T(8,128)(2,1)S(1)}, u32[]{:S(2)}, u32[]{:S(2)}) collective-permute-start(bf16[16,384]{1,0:T(8,128)(2,1)S(1)} %get-tuple-element.41), channel_id=1, source_target_pairs={{4,0},{8,4},{12,8},{16,12},{20,16},{24,20},{28,24},{32,28},{36,32}... | collective-permute-start | bytes 36872 | tf_op jit(solution)/shard_map/ppermute | solution.py:440
  84.3 4.6 %collective-permute-done.17.after_ref = bf16[16,384]{1,0:T(8,128)(2,1)S(1)} collective-permute-done((bf16[16,384]{1,0:T(8,128)(2,1)S(1)}, bf16[16,384]{1,0:T(8,128)(2,1)S(1)}, u32[]{:S(2)}, u32[]{:S(2)}) %collective-permute-start.17) | collective-permute-done | bytes 12320 | tf_op jit(solution)/shard_map/ppermute | solution.py:440
  91.1 2.2 %collective-permute-start.20 = (bf16[192,384]{1,0:T(8,128)(2,1)S(1)}, bf16[192,384]{1,0:T(8,128)(2,1)S(1)}, u32[]{:S(2)}, u32[]{:S(2)}) collective-permute-start(bf16[192,384]{1,0:T(8,128)(2,1)S(1)} %part_sum.2), channel_id=1, source_target_pairs={{0,2},{2,0},{1,3},{3,1},{4,6},{6,4},{5,7},{7,5},{8,10},{10,8},{9,1... | collective-permute-start | bytes 442376 | tf_op jit(solution)/shard_map/ppermute | solution.py:390
  93.3 5.2 %collective-permute-done.20.refs_1_ = bf16[192,384]{1,0:T(8,128)(2,1)S(1)} collective-permute-done((bf16[192,384]{1,0:T(8,128)(2,1)S(1)}, bf16[192,384]{1,0:T(8,128)(2,1)S(1)}, u32[]{:S(2)}, u32[]{:S(2)}) %collective-permute-start.20) | collective-permute-done | bytes 147488 | tf_op jit(solution)/shard_map/ppermute | solution.py:390
  (54 shorter events, 13.0 us)
Async XLA Ops:
  0.0 10.1 %copy-start.3 = (f32[1536]{0:T(1024)S(1)}, f32[1536]{0:T(1024)}, u32[]{:S(2)}) copy-start(f32[1536]{0:T(1024)} %gain_ref.2) | copy-start | bytes 18436
  11.6 9.3 %collective-permute-start = (bf16[192,768]{1,0:T(8,128)(2,1)S(1)}, bf16[192,768]{1,0:T(8,128)(2,1)S(1)}, u32[]{:S(2)}, u32[]{:S(2)}) collective-permute-start(bf16[192,768]{1,0:T(8,128)(2,1)S(1)} %get-tuple-element.25.refs_1_.refs_2_), channel_id=1, source_target_pairs={{0,16},{16,32},{32,48},{48,64},{64,80},{80,96},{96,112},{112,0},{1... | collective-permute-start | bytes 884744 | tf_op jit(solution)/shard_map/ppermute | solution.py:394
  13.6 9.3 %collective-permute-start.3 = (bf16[192,768]{1,0:T(8,128)(2,1)S(1)}, bf16[192,768]{1,0:T(8,128)(2,1)S(1)}, u32[]{:S(2)}, u32[]{:S(2)}) collective-permute-start(bf16[192,768]{1,0:T(8,128)(2,1)S(1)} %get-tuple-element.25.refs_1_.refs_2_), channel_id=1, source_target_pairs={{0,112},{16,0},{32,16},{48,32},{64,48},{80,64},{96,80},{112,96},{1... | collective-permute-start | bytes 884744 | tf_op jit(solution)/shard_map/ppermute | solution.py:394
  13.7 49.5 %collective-permute-start.14 = (bf16[384,1536]{1,0:T(8,128)(2,1)S(1)}, bf16[384,1536]{1,0:T(8,128)(2,1)S(1)}, u32[]{:S(2)}, u32[]{:S(2)}) collective-permute-start(bf16[384,1536]{1,0:T(8,128)(2,1)S(1)} %copy-done.6), channel_id=1, source_target_pairs={{0,2},{2,0},{1,3},{3,1},{4,6},{6,4},{5,7},{7,5},{8,10},{10,8},{9,1... | collective-permute-start | bytes 3538952 | tf_op jit(solution)/shard_map/ppermute | solution.py:390
  16.3 8.9 %collective-permute-start.8 = (bf16[192,384]{1,0:T(8,128)(2,1)S(1)}, bf16[192,384]{1,0:T(8,128)(2,1)S(1)}, u32[]{:S(2)}, u32[]{:S(2)}) collective-permute-start(bf16[192,384]{1,0:T(8,128)(2,1)S(1)} %get-tuple-element.24.refs_0_.a_ref), channel_id=1, source_target_pairs={{0,4},{4,0},{8,12},{12,8},{1,5},{5,1},{9,13},{13,9},{2,6},{6,2},{1... | collective-permute-start | bytes 442376 | tf_op jit(solution)/shard_map/ppermute | solution.py:390
  20.9 11.2 %collective-permute-start.1 = (bf16[192,768]{1,0:T(8,128)(2,1)S(1)}, bf16[192,768]{1,0:T(8,128)(2,1)S(1)}, u32[]{:S(2)}, u32[]{:S(2)}) collective-permute-start(bf16[192,768]{1,0:T(8,128)(2,1)S(1)} %collective-permute-done.refs_2_.refs_3_), channel_id=1, source_target_pairs={{0,16},{16,32},{32,48},{48,64},{64,80},{80,96},{96,112},{112,0},{1... | collective-permute-start | bytes 884744 | tf_op jit(solution)/shard_map/ppermute | solution.py:394
  22.9 9.7 %collective-permute-start.4 = (bf16[192,768]{1,0:T(8,128)(2,1)S(1)}, bf16[192,768]{1,0:T(8,128)(2,1)S(1)}, u32[]{:S(2)}, u32[]{:S(2)}) collective-permute-start(bf16[192,768]{1,0:T(8,128)(2,1)S(1)} %collective-permute-done.3.refs_3_.refs_4_), channel_id=1, source_target_pairs={{0,112},{16,0},{32,16},{48,32},{64,48},{80,64},{96,80},{112,96},{1... | collective-permute-start | bytes 884744 | tf_op jit(solution)/shard_map/ppermute | solution.py:394
  25.2 13.1 %collective-permute-start.9 = (bf16[384,384]{1,0:T(8,128)(2,1)S(1)}, bf16[384,384]{1,0:T(8,128)(2,1)S(1)}, u32[]{:S(2)}, u32[]{:S(2)}) collective-permute-start(bf16[384,384]{1,0:T(8,128)(2,1)S(1)} %join.1), channel_id=1, source_target_pairs={{0,8},{4,12},{8,0},{12,4},{1,9},{5,13},{9,1},{13,5},{2,10},{6,14},... | collective-permute-start | bytes 884744 | tf_op jit(solution)/shard_map/ppermute | solution.py:390
  32.2 17.8 %collective-permute-start.2 = (bf16[192,768]{1,0:T(8,128)(2,1)S(1)}, bf16[192,768]{1,0:T(8,128)(2,1)S(1)}, u32[]{:S(2)}, u32[]{:S(2)}) collective-permute-start(bf16[192,768]{1,0:T(8,128)(2,1)S(1)} %collective-permute-done.1.a_ref.refs_4_.refs_5_), channel_id=1, source_target_pairs={{0,16},{16,32},{32,48},{48,64},{64,80},{80,96},{96,112},{112,0},{1... | collective-permute-start | bytes 884744 | tf_op jit(solution)/shard_map/ppermute | solution.py:394
  32.6 17.4 %collective-permute-start.5 = (bf16[192,768]{1,0:T(8,128)(2,1)S(1)}, bf16[192,768]{1,0:T(8,128)(2,1)S(1)}, u32[]{:S(2)}, u32[]{:S(2)}) collective-permute-start(bf16[192,768]{1,0:T(8,128)(2,1)S(1)} %collective-permute-done.4.b_ref.refs_5_.refs_6_), channel_id=1, source_target_pairs={{0,112},{16,0},{32,16},{48,32},{64,48},{80,64},{96,80},{112,96},{1... | collective-permute-start | bytes 884744 | tf_op jit(solution)/shard_map/ppermute | solution.py:394
  35.2 14.8 %collective-permute-start.6 = (bf16[96,768]{1,0:T(8,128)(2,1)S(1)}, bf16[96,768]{1,0:T(8,128)(2,1)S(1)}, u32[]{:S(2)}, u32[]{:S(2)}) collective-permute-start(bf16[96,768]{1,0:T(8,128)(2,1)S(1)} %get-tuple-element.26), channel_id=1, source_target_pairs={{0,32},{16,48},{32,64},{48,80},{64,96},{80,112},{96,0},{112,16},{1... | collective-permute-start | bytes 442376 | tf_op jit(solution)/shard_map/ppermute | solution.py:394
  38.3 11.7 %collective-permute-start.7 = (bf16[96,768]{1,0:T(8,128)(2,1)S(1)}, bf16[96,768]{1,0:T(8,128)(2,1)S(1)}, u32[]{:S(2)}, u32[]{:S(2)}) collective-permute-start(bf16[96,768]{1,0:T(8,128)(2,1)S(1)} %get-tuple-element.27), channel_id=1, source_target_pairs={{0,96},{16,112},{32,0},{48,16},{64,32},{80,48},{96,64},{112,80},{1... | collective-permute-start | bytes 442376 | tf_op jit(solution)/shard_map/ppermute | solution.py:394
  51.9 10.6 %collective-permute-start.11 = (bf16[208,384]{1,0:T(8,128)(2,1)S(1)}, bf16[208,384]{1,0:T(8,128)(2,1)S(1)}, u32[]{:S(2)}, u32[]{:S(2)}) collective-permute-start(bf16[208,384]{1,0:T(8,128)(2,1)S(1)} %last_attention.5), channel_id=1, source_target_pairs={{0,8},{4,12},{8,0},{12,4},{1,9},{5,13},{9,1},{13,5},{2,10},{6,14},... | collective-permute-start | bytes 479240 | tf_op jit(solution)/shard_map/ppermute | solution.py:390
  55.4 7.9 %collective-permute-start.10 = (bf16[208,384]{1,0:T(8,128)(2,1)S(1)}, bf16[208,384]{1,0:T(8,128)(2,1)S(1)}, u32[]{:S(2)}, u32[]{:S(2)}) collective-permute-start(bf16[208,384]{1,0:T(8,128)(2,1)S(1)} %get-tuple-element.34), channel_id=1, source_target_pairs={{0,4},{4,0},{8,12},{12,8},{1,5},{5,1},{9,13},{13,9},{2,6},{6,2},{1... | collective-permute-start | bytes 479240 | tf_op jit(solution)/shard_map/ppermute | solution.py:390
  55.5 7.8 %collective-permute-start.12 = (bf16[208,384]{1,0:T(8,128)(2,1)S(1)}, bf16[208,384]{1,0:T(8,128)(2,1)S(1)}, u32[]{:S(2)}, u32[]{:S(2)}) collective-permute-start(bf16[208,384]{1,0:T(8,128)(2,1)S(1)} %get-tuple-element.38), channel_id=1, source_target_pairs={{0,12},{4,8},{8,4},{12,0},{1,13},{5,9},{9,5},{13,1},{2,14},{6,10},... | collective-permute-start | bytes 479240 | tf_op jit(solution)/shard_map/ppermute | solution.py:390
  58.5 14.7 %collective-permute-start.13 = (bf16[384,1536]{1,0:T(8,128)(2,1)S(1)}, bf16[384,1536]{1,0:T(8,128)(2,1)S(1)}, u32[]{:S(2)}, u32[]{:S(2)}) collective-permute-start(bf16[384,1536]{1,0:T(8,128)(2,1)S(1)} %copy-done.6), channel_id=1, source_target_pairs={{0,1},{1,0},{2,3},{3,2},{4,5},{5,4},{6,7},{7,6},{8,9},{9,8},{10,11... | collective-permute-start | bytes 3538952 | tf_op jit(solution)/shard_map/ppermute | solution.py:390
  62.5 10.7 %copy-start.5 = (bf16[2,1536,384]{2,1,0:T(8,128)(2,1)S(1)}, bf16[2,1536,384]{2,1,0:T(8,128)(2,1)}, u32[]{:S(2)}) copy-start(bf16[2,1536,384]{2,1,0:T(8,128)(2,1)} %glu_ref.1) | copy-start | bytes 7077892
  62.5 10.7 %copy-start.8 = (f32[1536]{0:T(1024)S(1)}, f32[1536]{0:T(1024)}, u32[]{:S(2)}) copy-start(f32[1536]{0:T(1024)} %gain_ref.3) | copy-start | bytes 18436
  62.6 26.8 %collective-permute-start.19 = (bf16[384,1536]{1,0:T(8,128)(2,1)S(1)}, bf16[384,1536]{1,0:T(8,128)(2,1)S(1)}, u32[]{:S(2)}, u32[]{:S(2)}) collective-permute-start(bf16[384,1536]{1,0:T(8,128)(2,1)S(1)} %copy-done), channel_id=1, source_target_pairs={{0,1},{1,0},{2,3},{3,2},{4,5},{5,4},{6,7},{7,6},{8,9},{9,8},{10,11... | collective-permute-start | bytes 3538952 | tf_op jit(solution)/shard_map/ppermute | solution.py:390
  63.2 10.0 %collective-permute-start.15 = (bf16[384,1536]{1,0:T(8,128)(2,1)S(1)}, bf16[384,1536]{1,0:T(8,128)(2,1)S(1)}, u32[]{:S(2)}, u32[]{:S(2)}) collective-permute-start(bf16[384,1536]{1,0:T(8,128)(2,1)S(1)} %collective-permute-done.14.w2), channel_id=1, source_target_pairs={{0,1},{1,0},{2,3},{3,2},{4,5},{5,4},{6,7},{7,6},{8,9},{9,8},{10,11... | collective-permute-start | bytes 3538952 | tf_op jit(solution)/shard_map/ppermute | solution.py:390
  75.8 8.5 %collective-permute-start.16 = (bf16[16,384]{1,0:T(8,128)(2,1)S(1)}, bf16[16,384]{1,0:T(8,128)(2,1)S(1)}, u32[]{:S(2)}, u32[]{:S(2)}) collective-permute-start(bf16[16,384]{1,0:T(8,128)(2,1)S(1)} %get-tuple-element.39), channel_id=1, source_target_pairs={{0,4},{4,8},{8,12},{12,16},{16,20},{20,24},{24,28},{28,32},{32,36}... | collective-permute-start | bytes 36872 | tf_op jit(solution)/shard_map/ppermute | solution.py:439
  81.3 7.7 %collective-permute-start.17 = (bf16[16,384]{1,0:T(8,128)(2,1)S(1)}, bf16[16,384]{1,0:T(8,128)(2,1)S(1)}, u32[]{:S(2)}, u32[]{:S(2)}) collective-permute-start(bf16[16,384]{1,0:T(8,128)(2,1)S(1)} %get-tuple-element.41), channel_id=1, source_target_pairs={{4,0},{8,4},{12,8},{16,12},{20,16},{24,20},{28,24},{32,28},{36,32}... | collective-permute-start | bytes 36872 | tf_op jit(solution)/shard_map/ppermute | solution.py:440
  89.3 1.5 %collective-permute-start.18 = (bf16[192,384]{1,0:T(8,128)(2,1)S(1)}, bf16[192,384]{1,0:T(8,128)(2,1)S(1)}, u32[]{:S(2)}, u32[]{:S(2)}) collective-permute-start(bf16[192,384]{1,0:T(8,128)(2,1)S(1)} %edges.1.own_ref), channel_id=1, source_target_pairs={{0,1},{1,0},{2,3},{3,2},{4,5},{5,4},{6,7},{7,6},{8,9},{9,8},{10,11... | collective-permute-start | bytes 442376 | tf_op jit(solution)/shard_map/ppermute | solution.py:390
  91.1 7.5 %collective-permute-start.20 = (bf16[192,384]{1,0:T(8,128)(2,1)S(1)}, bf16[192,384]{1,0:T(8,128)(2,1)S(1)}, u32[]{:S(2)}, u32[]{:S(2)}) collective-permute-start(bf16[192,384]{1,0:T(8,128)(2,1)S(1)} %part_sum.2), channel_id=1, source_target_pairs={{0,2},{2,0},{1,3},{3,1},{4,6},{6,4},{5,7},{7,5},{8,10},{10,8},{9,1... | collective-permute-start | bytes 442376 | tf_op jit(solution)/shard_map/ppermute | solution.py:390
  (6 other events, 35.6 us)

commit v4 on v3

--- a/solution.py
+++ b/solution.py
@@ -16,6 +16,7 @@
 ROWS = 192
 REACH = 15
 HALO = 16
+INNER = ROWS - 2 * HALO
 STATS = 16
 TP = ("xh", "core")
 CTX = ("z", "y")
@@ -24,12 +25,12 @@
 OVERLAPPED = pl.CostEstimate(flops=2 * 10**10, bytes_accessed=2**20, transcendentals=0)
 
 
-def layer_norm(inputs, gain):
+def layer_norm(inputs, gain, eps=1e-05):
     inputs = inputs.astype(jnp.float32)
     average = jnp.mean(inputs, axis=-1, keepdims=True)
     centered = inputs - average
     variance = jnp.mean(centered * centered, axis=-1, keepdims=True)
-    return (centered * lax.rsqrt(variance + 1e-05) * gain).astype(jnp.bfloat16)
+    return (centered * lax.rsqrt(variance + eps) * gain).astype(jnp.bfloat16)
 
 
 def split_three(value):
@@ -39,15 +40,17 @@
     return high, mid, rest - mid
 
 
-def head_window(head):
-    start = 0 if head < 2 else 128
+def head_mask(head):
+    start = 128 * (head // 2)
     lane = lax.broadcasted_iota(jnp.int32, (1, 256), 1) + start
-    return start, (lane >= head * HEAD) & (lane < (head + 1) * HEAD)
-
-
-def attend(queries, keys, values, head):
-    start, inside = head_window(head)
-    masked = jnp.where(inside, queries[:, start : start + 256], 0)
+    return (lane >= head * HEAD) & (lane < (head + 1) * HEAD)
+
+
+def attend(queries, keys, values, pair):
+    start = 128 * pair
+    window = queries[:, start : start + 256]
+    masks = [head_mask(2 * pair + side) for side in range(2)]
+    masked = jnp.concatenate([jnp.where(mask, window, 0) for mask in masks], 0)
     window = jnp.concatenate([block[:, start : start + 256] for block in keys], 0)
     scores = lax.dot_general(
         masked, window, (((1,), (1,)), ((), ())), preferred_element_type=jnp.float32
@@ -57,12 +60,12 @@
     denominator = jnp.sum(weights, axis=1, keepdims=True)
     window = jnp.concatenate([block[:, start : start + 256] for block in values], 0)
     summed = jnp.dot(weights.astype(jnp.bfloat16), window, preferred_element_type=jnp.float32)
-    return inside, summed, top, denominator
-
-
-def widen(part, head):
+    return masks, summed, top, denominator
+
+
+def widen(part, pair):
     blank = jnp.zeros((part.shape[0], 128), jnp.float32)
-    return jnp.concatenate([part, blank] if head < 2 else [blank, part], 1)
+    return jnp.concatenate([part, blank] if pair == 0 else [blank, part], 1)
 
 
 def split_refs(refs, count):
@@ -82,11 +85,14 @@
     total = jnp.zeros((count, COLS), jnp.float32)
     tops = jnp.zeros((count, 128), jnp.float32)
     sums = jnp.ones((count, 128), jnp.float32)
-    for head in range(HEADS_HERE):
-        inside, summed, top, denominator = attend(queries, keys, values, head)
-        total = total + widen(jnp.where(inside, summed, 0.0), head)
-        tops = jnp.where(lane == head, top, tops)
-        sums = jnp.where(lane == head, denominator, sums)
+    for pair in range(2):
+        masks, summed, top, denominator = attend(queries, keys, values, pair)
+        both = jnp.where(masks[0], summed[:count], jnp.where(masks[1], summed[count:], 0.0))
+        total = total + widen(both, pair)
+        for side in range(2):
+            rows = slice(side * count, (side + 1) * count)
+            tops = jnp.where(lane == 2 * pair + side, top[rows], tops)
+            sums = jnp.where(lane == 2 * pair + side, denominator[rows], sums)
     o_ref[...] = total
     top_ref[...] = tops
     sum_ref[...] = sums
@@ -103,11 +109,13 @@
     tops = jnp.zeros((count, 128), jnp.float32)
     sums = jnp.zeros((count, 128), jnp.float32)
     products = []
-    for head in range(HEADS_HERE):
-        inside, summed, top, denominator = attend(queries, keys, values, head)
-        products.append((inside, summed))
-        tops = jnp.where(lane == head, top, tops)
-        sums = jnp.where(lane == head, denominator, sums)
+    for pair in range(2):
+        masks, summed, top, denominator = attend(queries, keys, values, pair)
+        products.append((masks, summed))
+        for side in range(2):
+            rows = slice(side * count, (side + 1) * count)
+            tops = jnp.where(lane == 2 * pair + side, top[rows], tops)
+            sums = jnp.where(lane == 2 * pair + side, denominator[rows], sums)
     joint = jnp.maximum(tops, top_ref[...])
     rescale = jnp.exp2(tops - joint)
     prior_rescale = jnp.exp2(top_ref[...] - joint)
@@ -116,13 +124,14 @@
     rescale = rescale * inverse
     prior_rescale = prior_rescale * inverse
     total = jnp.zeros((count, COLS), jnp.float32)
-    for head, (inside, summed) in enumerate(products):
-        start = 0 if head < 2 else 128
-        part = (
-            summed * rescale[:, head : head + 1]
-            + prior_ref[:, start : start + 256] * prior_rescale[:, head : head + 1]
-        )
-        total = total + widen(jnp.where(inside, part, 0.0), head)
+    for pair, (masks, summed) in enumerate(products):
+        prior = prior_ref[:, 128 * pair : 128 * pair + 256]
+        both = jnp.zeros((count, 256), jnp.float32)
+        for side, mask in enumerate(masks):
+            head = slice(2 * pair + side, 2 * pair + side + 1)
+            part = summed[side * count : (side + 1) * count] * rescale[:, head]
+            both = jnp.where(mask, part + prior * prior_rescale[:, head], both)
+        total = total + widen(both, pair)
     high, mid, low = split_three(joint + jnp.log2(denominator))
     stats = jnp.where(
         lane < 4, high, jnp.where(lane < 8, pltpu.roll(mid, 4, 1), pltpu.roll(low, 8, 1))
@@ -262,8 +271,7 @@
     convolve(held, taps_ref, bias_ref, ROWS - 2 * HALO, store)
 
 
-def edges_kernel(before_ref, glu_ref, after_ref, inner_ref, taps_ref, bias_ref, o_ref, held):
-    o_ref[HALO : ROWS - HALO] = inner_ref[...]
+def edges_kernel(before_ref, glu_ref, after_ref, taps_ref, bias_ref, o_ref, held):
     for side in range(2):
         if side == 0:
             held[:HALO] = before_ref[...].astype(jnp.float32)
@@ -273,30 +281,34 @@
             held[2 * HALO :] = after_ref[...].astype(jnp.float32)
 
         def store(here, value):
-            o_ref[side * (ROWS - HALO) : side * (ROWS - HALO) + HALO, here] = value
+            o_ref[side * HALO : (side + 1) * HALO, here] = value
 
         convolve(held, taps_ref, bias_ref, HALO, store)
 
 
-def depthwise(before, glu, after, taps, bias):
-    inner = pl.pallas_call(
+def conv_inner(glu, taps, bias):
+    return pl.pallas_call(
         inner_kernel,
-        out_shape=jax.ShapeDtypeStruct((ROWS - 2 * HALO, COLS), jnp.bfloat16),
+        out_shape=jax.ShapeDtypeStruct((INNER, COLS), jnp.bfloat16),
         scratch_shapes=[pltpu.VMEM((ROWS, COLS), jnp.float32)],
         compiler_params=pltpu.CompilerParams(vmem_limit_bytes=VMEM_LIMIT),
         name="inner",
     )(glu, taps, bias)
+
+
+def conv_edges(before, glu, after, taps, bias):
     return pl.pallas_call(
         edges_kernel,
-        out_shape=jax.ShapeDtypeStruct((ROWS, COLS), jnp.bfloat16),
+        out_shape=jax.ShapeDtypeStruct((2 * HALO, COLS), jnp.bfloat16),
         scratch_shapes=[pltpu.VMEM((3 * HALO, COLS), jnp.float32)],
         compiler_params=pltpu.CompilerParams(vmem_limit_bytes=VMEM_LIMIT),
+        cost_estimate=OVERLAPPED,
         name="edges",
-    )(before, glu, after, inner, taps, bias)
-
-
-def project_kernel(rows_ref, gain_ref, w_ref, kv_ref, q_ref):
-    normed = layer_norm(rows_ref[...], gain_ref[...].reshape(1, D))
+    )(before, glu, after, taps, bias)
+
+
+def project_kernel(eps_ref, rows_ref, gain_ref, w_ref, kv_ref, q_ref):
+    normed = layer_norm(rows_ref[...], gain_ref[...].reshape(1, D), eps_ref[0:1, 0:1])
     for half in range(2):
         kv_ref[:, half * COLS : (half + 1) * COLS] = jnp.dot(
             normed, w_ref[1 + half], preferred_element_type=jnp.float32
@@ -305,7 +317,7 @@
     q_ref[...] = (query * Q_SCALE).astype(jnp.bfloat16)
 
 
-def project(rows, gain, weights):
+def project(eps, rows, gain, weights):
     return pl.pallas_call(
         project_kernel,
         out_shape=[
@@ -314,21 +326,21 @@
         ],
         compiler_params=pltpu.CompilerParams(vmem_limit_bytes=VMEM_LIMIT),
         name="project",
-    )(rows, gain, weights)
-
-
-def stage_kernel(frames_ref, o_ref):
-    o_ref[...] = frames_ref[...]
-
-
-def stage(frames):
-    return pl.pallas_call(
-        stage_kernel,
-        out_shape=jax.ShapeDtypeStruct(frames.shape, frames.dtype),
+    )(eps, rows, gain, weights)
+
+
+def epsilon_kernel(o_ref):
+    o_ref[...] = jnp.full((8, 128), 1e-05, jnp.float32)
+
+
+def epsilon():
+    return pl.pallas_call(
+        epsilon_kernel,
+        out_shape=jax.ShapeDtypeStruct((8, 128), jnp.float32),
         compiler_params=pltpu.CompilerParams(vmem_limit_bytes=VMEM_LIMIT),
         cost_estimate=OVERLAPPED,
-        name="stage",
-    )(frames)
+        name="epsilon",
+    )()
 
 
 def join_kernel(a_ref, b_ref, o_ref):
@@ -359,31 +371,45 @@
     )(a, b)
 
 
-def part_kernel(flip, own_ref, other_ref, w_own, w_other, *refs):
-    o_ref = refs[-1]
+def product(flip, own_ref, other_ref, w_own, w_other):
     columns = pl.ds(pl.multiple_of((lax.axis_index(TP) ^ flip) * COLS, 128), COLS)
     total = jnp.dot(own_ref[...], w_own[:, columns], preferred_element_type=jnp.float32)
-    total = total + jnp.dot(
+    return total + jnp.dot(
         other_ref[...], w_other[:, columns], preferred_element_type=jnp.float32
     )
-    for extra in refs[:-1]:
-        total = total + extra[...].astype(jnp.float32)
-    o_ref[...] = total.astype(o_ref.dtype)
-
-
-def part_sum(flip, own, other, weights, extra):
-    vmem = pl.BlockSpec(memory_space=pltpu.VMEM)
+
+
+def part_kernel(flip, own_ref, other_ref, w_own, w_other, o_ref):
+    o_ref[...] = product(flip, own_ref, other_ref, w_own, w_other).astype(o_ref.dtype)
+
+
+def part_sum(flip, own, other, weights, kind):
     return pl.pallas_call(
         functools.partial(part_kernel, flip),
-        in_specs=[vmem] * (4 + len(extra)),
-        out_specs=vmem,
+        out_shape=jax.ShapeDtypeStruct(own.shape, kind),
+        compiler_params=pltpu.CompilerParams(vmem_limit_bytes=VMEM_LIMIT),
+        name="part_sum",
+    )(own, other, *weights)
+
+
+def final_kernel(own_ref, other_ref, w_own, w_other, middle_ref, ours_ref, inner_ref, edges_ref, o_ref):
+    here = slice(HALO, HALO + INNER)
+    total = ours_ref[...] + inner_ref[...].astype(jnp.float32)
+    o_ref[here] = (middle_ref[here].astype(jnp.float32) + total).astype(jnp.bfloat16)
+    total = product(0, own_ref, other_ref, w_own, w_other) + edges_ref[...].astype(jnp.float32)
+    for side in range(2):
+        here = slice(side * (ROWS - HALO), side * (ROWS - HALO) + HALO)
+        part = total[side * HALO : (side + 1) * HALO]
+        o_ref[here] = (middle_ref[here].astype(jnp.float32) + part).astype(jnp.bfloat16)
+
+
+def final(own, other, weights, middle, ours, inner, edges):
+    return pl.pallas_call(
+        final_kernel,
         out_shape=jax.ShapeDtypeStruct((ROWS, COLS), jnp.bfloat16),
         compiler_params=pltpu.CompilerParams(vmem_limit_bytes=VMEM_LIMIT),
-        cost_estimate=pl.CostEstimate(
-            flops=4 * ROWS * COLS * COLS, bytes_accessed=3 * 2**20, transcendentals=0
-        ),
-        name="part_sum",
-    )(own, other, *weights, *extra)
+        name="final",
+    )(own, other, *weights, middle, ours, inner, edges)
 
 
 def swap(value, axis, count, flip):
@@ -407,8 +433,8 @@
 ):
     out_core = swap(out_weight, "core", 2, 1)
     out_far = swap(out_weight, "xh", 2, 1)
-    whole_rows = lax.all_gather(stage(frames), TP, axis=1, tiled=True)
-    mine, query = project(whole_rows, attn_gain, query_key_value)
+    whole_rows = lax.all_gather(frames, TP, axis=1, tiled=True)
+    mine, query = project(epsilon(), whole_rows, attn_gain, query_key_value)
     lower1, upper1 = shift(mine, "z", 8, 1), shift(mine, "z", 8, -1)
     query1 = swap(query, "y", 4, 1)
     lower2, upper2 = shift(lower1, "z", 8, 1), shift(upper1, "z", 8, -1)
@@ -438,11 +464,15 @@
     )
     before = lax.ppermute(end, CTX, [(i, i + 1) for i in range(31)])
     after = lax.ppermute(top, CTX, [(i + 1, i) for i in range(31)])
-    activated = depthwise(before, glu, after, depth_kernel, depth_bias)
-    other = swap(activated, "core", 2, 1)
     weights = (proj_weight, proj_core)
-    theirs = swap(part_sum(2, activated, other, weights, ()), "xh", 2, 1)
-    return part_sum(0, activated, other, weights, (middle, theirs))
+    inner = conv_inner(glu, depth_kernel, depth_bias)
+    inner_other = swap(inner, "core", 2, 1)
+    inner_far = swap(part_sum(2, inner, inner_other, weights, jnp.bfloat16), "xh", 2, 1)
+    ours = part_sum(0, inner, inner_other, weights, jnp.float32)
+    edges = conv_edges(before, glu, after, depth_kernel, depth_bias)
+    edges_other = swap(edges, "core", 2, 1)
+    edges_far = swap(part_sum(2, edges, edges_other, weights, jnp.bfloat16), "xh", 2, 1)
+    return final(edges, edges_other, weights, middle, ours, inner_far, edges_far)
 
 
 def solution(mesh):

time: 99.7 us -> 98.3 us (0.986)
  waiting for transfers between devices: 27.2 us -> 23.4 us
  starting transfers between devices: 32.4 us -> 36.1 us
  Pallas kernels: 20.4 us -> 19.1 us
    ppermute x11 -> x13, starting transfers between devices: 11.9 us -> 14.6 us  [swap(): return lax.ppermute(value, axis, [(i, i ^ flip) for i in range(count)])]
    ppermute x11 -> x13, waiting for transfers between devices: 6.63 us -> 4.1 us  [swap(): return lax.ppermute(value, axis, [(i, i ^ flip) for i in range(count)])]
    ppermute x1, waiting for transfers between devices: 4.61 us -> 3.17 us  [per_device(): after = lax.ppermute(top, CTX, [(i + 1, i) for i in range(31)])]
    pallas_call x3, Pallas kernels: 6.19 us -> 5.03 us  [last_attention(): pl.pallas_call(functools.partial(last_attention_kernel, places, len(block...]
    ppermute x1, starting transfers between devices: 5.43 us -> 6.45 us  [per_device(): before = lax.ppermute(end, CTX, [(i, i + 1) for i in range(31)])]
    pallas_call x5 -> x7, Pallas kernels: 2.8 us -> 3.13 us  [the longest x1 1.12 us: conv_inner(): pl.pallas_call(inner_kernel, out_shape=jax.ShapeDtypeStruct((INNER, COLS)...]
  transfers between devices with their start and end apart: 21 -> 23, of which waited for: 7 -> 7; matrix products, arithmetic and copies ran while one was open for 0% -> 0% of each run, Pallas kernels for 18% -> 17%
where the time goes in v4:
time: 98.3 us; the launch traced here: 98.1 us
  starting transfers between devices  36.1 us (37%)
  waiting for transfers between devices  23.4 us (24%)
  Pallas kernels  19.1 us (19%)
  blocking collectives  18.4 us (19%)
    ppermute x8, waiting for transfers between devices, shift(): lax.ppermute(value, axis, [(i, (i + offset) % count) for i in range(count)])  16.1 us
    ppermute x13, starting transfers between devices, swap(): return lax.ppermute(value, axis, [(i, i ^ flip) for i in range(count)])  14.6 us
    ppermute x8, starting transfers between devices, shift(): lax.ppermute(value, axis, [(i, (i + offset) % count) for i in range(count)])  13.1 us
    all_gather x1, blocking collectives, per_device(): context = lax.all_gather(context, TP, axis=0, tiled=False)  9.24 us
    all_gather x1, blocking collectives, per_device(): whole_rows = lax.all_gather(frames, TP, axis=1, tiled=True)  9.18 us
    ppermute x1, starting transfers between devices, per_device(): before = lax.ppermute(end, CTX, [(i, i + 1) for i in range(31)])  6.45 us
    pallas_call x3, Pallas kernels, first_attention(): pl.pallas_call(functools.partial(first_attention_kernel, places, len(bloc...  6.14 us
    pallas_call x3, Pallas kernels, last_attention(): pl.pallas_call(functools.partial(last_attention_kernel, places, len(block...  5.03 us
  transfers between devices with their start and end apart: 23, of which 7 were waited for; matrix products, arithmetic and copies ran while one was open for 0% of the time, Pallas kernels for 17%

profile of v4, /device:TPU:56, one launch (start us, length us, event | category | flops | bytes accessed | tf_op | source)
XLA Modules:
  0.0 98.1 jit_solution(14187623880233616963)
XLA Ops:
  0.9 9.2 %all_gather.9.rows_ref = bf16[192,1536]{1,0:T(8,128)(2,1)S(1)} all-gather(bf16[192,384]{1,0:T(8,128)(2,1)S(1)} %copy-done.8), channel_id=1, replica_groups=mesh['batch'=2,'z'=8,'y'=4,'xh'=2,'core'=2] {'xh','core'}, dimensions={1}, use_global_device_ids=true | all-gather | bytes 737280 | tf_op jit(solution)/shard_map/all_gather | solution.py:436
  10.1 1.5 %project.1 = (bf16[192,768]{1,0:T(8,128)(2,1)S(1)}, bf16[192,384]{1,0:T(8,128)(2,1)S(1)}) custom-call(f32[8,128]{1,0:T(8,128)S(1)} %epsilon.1.eps_ref, bf16[192,1536]{1,0:T(8,128)(2,1)S(1)} %all_gather.9.rows_ref, f32[1536]{0:T(1024)S(1)} %copy-done.3, bf16[3,1536,384]{2,1,0:T(8,128)(2,1)S(1)} %copy-done.1), custom_call_target="tpu_custom_call" | custom-call | tf_op jit(solution)/shard_map/project/pallas_call | solution.py:321
  11.6 2.0 %collective-permute-start = (bf16[192,768]{1,0:T(8,128)(2,1)S(1)}, bf16[192,768]{1,0:T(8,128)(2,1)S(1)}, u32[]{:S(2)}, u32[]{:S(2)}) collective-permute-start(bf16[192,768]{1,0:T(8,128)(2,1)S(1)} %get-tuple-element.25.refs_1_.refs_2_), channel_id=1, source_target_pairs={{0,16},{16,32},{32,48},{48,64},{64,80},{80,96},{96,112},{112,0},{1... | collective-permute-start | bytes 884744 | tf_op jit(solution)/shard_map/ppermute | solution.py:420
  13.7 2.6 %collective-permute-start.14 = (bf16[384,1536]{1,0:T(8,128)(2,1)S(1)}, bf16[384,1536]{1,0:T(8,128)(2,1)S(1)}, u32[]{:S(2)}, u32[]{:S(2)}) collective-permute-start(bf16[384,1536]{1,0:T(8,128)(2,1)S(1)} %copy-done.6), channel_id=1, source_target_pairs={{0,2},{2,0},{1,3},{3,1},{4,6},{6,4},{5,7},{7,5},{8,10},{10,8},{9,1... | collective-permute-start | bytes 3538952 | tf_op jit(solution)/shard_map/ppermute | solution.py:416
  17.1 3.9 %collective-permute-done.refs_2_.refs_3_ = bf16[192,768]{1,0:T(8,128)(2,1)S(1)} collective-permute-done((bf16[192,768]{1,0:T(8,128)(2,1)S(1)}, bf16[192,768]{1,0:T(8,128)(2,1)S(1)}, u32[]{:S(2)}, u32[]{:S(2)}) %collective-permute-start) | collective-permute-done | bytes 294944 | tf_op jit(solution)/shard_map/ppermute | solution.py:420
  21.0 1.9 %collective-permute-start.1 = (bf16[192,768]{1,0:T(8,128)(2,1)S(1)}, bf16[192,768]{1,0:T(8,128)(2,1)S(1)}, u32[]{:S(2)}, u32[]{:S(2)}) collective-permute-start(bf16[192,768]{1,0:T(8,128)(2,1)S(1)} %collective-permute-done.refs_2_.refs_3_), channel_id=1, source_target_pairs={{0,16},{16,32},{32,48},{48,64},{64,80},{80,96},{96,112},{112,0},{1... | collective-permute-start | bytes 884744 | tf_op jit(solution)/shard_map/ppermute | solution.py:420
  22.9 2.3 %collective-permute-start.4 = (bf16[192,768]{1,0:T(8,128)(2,1)S(1)}, bf16[192,768]{1,0:T(8,128)(2,1)S(1)}, u32[]{:S(2)}, u32[]{:S(2)}) collective-permute-start(bf16[192,768]{1,0:T(8,128)(2,1)S(1)} %collective-permute-done.3.refs_3_.refs_4_), channel_id=1, source_target_pairs={{0,112},{16,0},{32,16},{48,32},{64,48},{80,64},{96,80},{112,96},{1... | collective-permute-start | bytes 884744 | tf_op jit(solution)/shard_map/ppermute | solution.py:420
  26.5 5.7 %collective-permute-done.1.a_ref.refs_4_.refs_5_ = bf16[192,768]{1,0:T(8,128)(2,1)S(1)} collective-permute-done((bf16[192,768]{1,0:T(8,128)(2,1)S(1)}, bf16[192,768]{1,0:T(8,128)(2,1)S(1)}, u32[]{:S(2)}, u32[]{:S(2)}) %collective-permute-start.1) | collective-permute-done | bytes 294944 | tf_op jit(solution)/shard_map/ppermute | solution.py:420
  32.6 2.6 %collective-permute-start.5 = (bf16[192,768]{1,0:T(8,128)(2,1)S(1)}, bf16[192,768]{1,0:T(8,128)(2,1)S(1)}, u32[]{:S(2)}, u32[]{:S(2)}) collective-permute-start(bf16[192,768]{1,0:T(8,128)(2,1)S(1)} %collective-permute-done.4.b_ref.refs_5_.refs_6_), channel_id=1, source_target_pairs={{0,112},{16,0},{32,16},{48,32},{64,48},{80,64},{96,80},{112,96},{1... | collective-permute-start | bytes 884744 | tf_op jit(solution)/shard_map/ppermute | solution.py:420
  35.2 3.2 %collective-permute-start.6 = (bf16[96,768]{1,0:T(8,128)(2,1)S(1)}, bf16[96,768]{1,0:T(8,128)(2,1)S(1)}, u32[]{:S(2)}, u32[]{:S(2)}) collective-permute-start(bf16[96,768]{1,0:T(8,128)(2,1)S(1)} %get-tuple-element.26), channel_id=1, source_target_pairs={{0,32},{16,48},{32,64},{48,80},{64,96},{80,112},{96,0},{112,16},{1... | collective-permute-start | bytes 442376 | tf_op jit(solution)/shard_map/ppermute | solution.py:420
  39.4 1.7 %first_attention.5 = (f32[192,384]{1,0:T(8,128)S(1)}, f32[192,128]{1,0:T(8,128)S(1)}, f32[192,128]{1,0:T(8,128)S(1)}) custom-call(bf16[384,384]{1,0:T(8,128)(2,1)S(1)} %collective-permute-done.9.refs_1_.refs_0_, bf16[192,768]{1,0:T(8,128)(2,1)S(1)} %get-tuple-element.25.refs_1_.refs_2_, bf16[192,768]{1,0:T(8,128)(2,1)S(1)} %collective-permute-done.refs_2_.refs_3_, ...), custom_call_target="tpu_custom_call" | custom-call | flops 754974720 | bytes 4194304 | tf_op jit(solution)/shard_map/first_attention/pallas_call | solution.py:156
  41.1 2.8 %first_attention.4 = (f32[384,384]{1,0:T(8,128)S(1)}, f32[384,128]{1,0:T(8,128)S(1)}, f32[384,128]{1,0:T(8,128)S(1)}) custom-call(bf16[192,384]{1,0:T(8,128)(2,1)S(1)} %collective-permute-done.8.b_ref.refs_0_, bf16[384,384]{1,0:T(8,128)(2,1)S(1)} %collective-permute-done.9.refs_1_.refs_0_, bf16[192,768]{1,0:T(8,128)(2,1)S(1)} %get-tuple-element.25.refs_1_.refs_2_, ...), custom_call_target="tpu_custom_call" | custom-call | flops 1509949440 | bytes 4194304 | tf_op jit(solution)/shard_map/first_attention/pallas_call | solution.py:156
  43.9 6.1 %collective-permute-done.6.refs_3_.refs_4_ = bf16[96,768]{1,0:T(8,128)(2,1)S(1)} collective-permute-done((bf16[96,768]{1,0:T(8,128)(2,1)S(1)}, bf16[96,768]{1,0:T(8,128)(2,1)S(1)}, u32[]{:S(2)}, u32[]{:S(2)}) %collective-permute-start.6) | collective-permute-done | bytes 147488 | tf_op jit(solution)/shard_map/ppermute | solution.py:420
  52.5 2.4 %last_attention.4 = (bf16[208,384]{1,0:T(8,128)(2,1)S(1)}, bf16[208,384]{1,0:T(8,128)(2,1)S(1)}) custom-call(bf16[192,384]{1,0:T(8,128)(2,1)S(1)} %collective-permute-done.8.b_ref.refs_0_, bf16[384,384]{1,0:T(8,128)(2,1)S(1)} %collective-permute-done.9.refs_1_.refs_0_, bf16[192,768]{1,0:T(8,128)(2,1)S(1)} %collective-permute-done.2.refs_1_.refs_2_, ...), custom_call_target="tpu_custom_call" | custom-call | flops 1207959552 | bytes 4194304 | tf_op jit(solution)/shard_map/last_attention/pallas_call | solution.py:172
  55.0 3.0 %collective-permute-start.12 = (bf16[208,384]{1,0:T(8,128)(2,1)S(1)}, bf16[208,384]{1,0:T(8,128)(2,1)S(1)}, u32[]{:S(2)}, u32[]{:S(2)}) collective-permute-start(bf16[208,384]{1,0:T(8,128)(2,1)S(1)} %get-tuple-element.38), channel_id=1, source_target_pairs={{0,12},{4,8},{8,4},{12,0},{1,13},{5,9},{9,5},{13,1},{2,14},{6,10},... | collective-permute-start | bytes 479240 | tf_op jit(solution)/shard_map/ppermute | solution.py:416
  58.0 1.7 %first_attention.3 = (f32[192,384]{1,0:T(8,128)S(1)}, f32[192,128]{1,0:T(8,128)S(1)}, f32[192,128]{1,0:T(8,128)S(1)}) custom-call(bf16[192,384]{1,0:T(8,128)(2,1)S(1)} %get-tuple-element.24.refs_0_.a_ref, bf16[192,768]{1,0:T(8,128)(2,1)S(1)} %get-tuple-element.25.refs_1_.refs_2_, bf16[192,768]{1,0:T(8,128)(2,1)S(1)} %collective-permute-done.refs_2_.refs_3_, ...), custom_call_target="tpu_custom_call" | custom-call | flops 754974720 | bytes 4194304 | tf_op jit(solution)/shard_map/first_attention/pallas_call | solution.py:156
  62.4 9.2 %all-gather = bf16[768,384]{1,0:T(8,128)(2,1)S(1)} all-gather(bf16[192,384]{1,0:T(8,128)(2,1)S(1)} %combine.1), channel_id=2, replica_groups=mesh['batch'=2,'z'=8,'y'=4,'xh'=2,'core'=2] {'xh','core'}, dimensions={0}, use_global_device_ids=true | all-gather | bytes 737280 | tf_op jit(solution)/shard_map/all_gather | solution.py:461
  71.7 2.5 %middle.1 = (bf16[192,384]{1,0:T(8,128)(2,1)S(1)}, bf16[192,384]{1,0:T(8,128)(2,1)S(1)}, bf16[16,384]{1,0:T(8,128)(2,1)S(1)}, bf16[16,384]{1,0:T(8,128)(2,1)S(1)}) custom-call(bf16[192,1536]{1,0:T(8,128)(2,1)S(1)} %all_gather.9.rows_ref, bf16[4,192,384]{2,1,0:T(8,128)(2,1)S(1)} %bitcast.1, bf16[384,1536]{1,0:T(8,128)(2,1)S(1)} %copy-done.6, ...), custom_call_target="tpu_custom_call" | custom-call | flops 20000000000 | bytes 1048576 | tf_op jit(solution)/shard_map/middle/pallas_call | solution.py:242
  75.8 6.4 %collective-permute-start.16 = (bf16[16,384]{1,0:T(8,128)(2,1)S(1)}, bf16[16,384]{1,0:T(8,128)(2,1)S(1)}, u32[]{:S(2)}, u32[]{:S(2)}) collective-permute-start(bf16[16,384]{1,0:T(8,128)(2,1)S(1)} %get-tuple-element.39), channel_id=1, source_target_pairs={{0,4},{4,8},{8,12},{12,16},{16,20},{20,24},{24,28},{28,32},{32,36}... | collective-permute-start | bytes 36872 | tf_op jit(solution)/shard_map/ppermute | solution.py:465
  82.3 1.9 %collective-permute-start.17 = (bf16[16,384]{1,0:T(8,128)(2,1)S(1)}, bf16[16,384]{1,0:T(8,128)(2,1)S(1)}, u32[]{:S(2)}, u32[]{:S(2)}) collective-permute-start(bf16[16,384]{1,0:T(8,128)(2,1)S(1)} %get-tuple-element.41), channel_id=1, source_target_pairs={{4,0},{8,4},{12,8},{16,12},{20,16},{24,20},{28,24},{32,28},{36,32}... | collective-permute-start | bytes 36872 | tf_op jit(solution)/shard_map/ppermute | solution.py:466
  84.6 2.2 %collective-permute-start.21 = (bf16[160,384]{1,0:T(8,128)(2,1)S(1)}, bf16[160,384]{1,0:T(8,128)(2,1)S(1)}, u32[]{:S(2)}, u32[]{:S(2)}) collective-permute-start(bf16[160,384]{1,0:T(8,128)(2,1)S(1)} %part_sum.4), channel_id=1, source_target_pairs={{0,2},{2,0},{1,3},{3,1},{4,6},{6,4},{5,7},{7,5},{8,10},{10,8},{9,1... | collective-permute-start | bytes 368648 | tf_op jit(solution)/shard_map/ppermute | solution.py:416
  86.8 3.2 %collective-permute-done.17.after_ref = bf16[16,384]{1,0:T(8,128)(2,1)S(1)} collective-permute-done((bf16[16,384]{1,0:T(8,128)(2,1)S(1)}, bf16[16,384]{1,0:T(8,128)(2,1)S(1)}, u32[]{:S(2)}, u32[]{:S(2)}) %collective-permute-start.17) | collective-permute-done | bytes 12320 | tf_op jit(solution)/shard_map/ppermute | solution.py:466
  91.8 2.2 %collective-permute-start.22 = (bf16[32,384]{1,0:T(8,128)(2,1)S(1)}, bf16[32,384]{1,0:T(8,128)(2,1)S(1)}, u32[]{:S(2)}, u32[]{:S(2)}) collective-permute-start(bf16[32,384]{1,0:T(8,128)(2,1)S(1)} %part_sum.5), channel_id=1, source_target_pairs={{0,2},{2,0},{1,3},{3,1},{4,6},{6,4},{5,7},{7,5},{8,10},{10,8},{9,1... | collective-permute-start | bytes 73736 | tf_op jit(solution)/shard_map/ppermute | solution.py:416
  94.4 2.9 %collective-permute-done.22.edges_ref = bf16[32,384]{1,0:T(8,128)(2,1)S(1)} collective-permute-done((bf16[32,384]{1,0:T(8,128)(2,1)S(1)}, bf16[32,384]{1,0:T(8,128)(2,1)S(1)}, u32[]{:S(2)}, u32[]{:S(2)}) %collective-permute-start.22) | collective-permute-done | bytes 24608 | tf_op jit(solution)/shard_map/ppermute | solution.py:416
  (60 shorter events, 14.7 us)
Async XLA Ops:
  11.6 9.3 %collective-permute-start = (bf16[192,768]{1,0:T(8,128)(2,1)S(1)}, bf16[192,768]{1,0:T(8,128)(2,1)S(1)}, u32[]{:S(2)}, u32[]{:S(2)}) collective-permute-start(bf16[192,768]{1,0:T(8,128)(2,1)S(1)} %get-tuple-element.25.refs_1_.refs_2_), channel_id=1, source_target_pairs={{0,16},{16,32},{32,48},{48,64},{64,80},{80,96},{96,112},{112,0},{1... | collective-permute-start | bytes 884744 | tf_op jit(solution)/shard_map/ppermute | solution.py:420
  13.6 9.3 %collective-permute-start.3 = (bf16[192,768]{1,0:T(8,128)(2,1)S(1)}, bf16[192,768]{1,0:T(8,128)(2,1)S(1)}, u32[]{:S(2)}, u32[]{:S(2)}) collective-permute-start(bf16[192,768]{1,0:T(8,128)(2,1)S(1)} %get-tuple-element.25.refs_1_.refs_2_), channel_id=1, source_target_pairs={{0,112},{16,0},{32,16},{48,32},{64,48},{80,64},{96,80},{112,96},{1... | collective-permute-start | bytes 884744 | tf_op jit(solution)/shard_map/ppermute | solution.py:420
  13.7 47.9 %collective-permute-start.14 = (bf16[384,1536]{1,0:T(8,128)(2,1)S(1)}, bf16[384,1536]{1,0:T(8,128)(2,1)S(1)}, u32[]{:S(2)}, u32[]{:S(2)}) collective-permute-start(bf16[384,1536]{1,0:T(8,128)(2,1)S(1)} %copy-done.6), channel_id=1, source_target_pairs={{0,2},{2,0},{1,3},{3,1},{4,6},{6,4},{5,7},{7,5},{8,10},{10,8},{9,1... | collective-permute-start | bytes 3538952 | tf_op jit(solution)/shard_map/ppermute | solution.py:416
  16.3 8.9 %collective-permute-start.8 = (bf16[192,384]{1,0:T(8,128)(2,1)S(1)}, bf16[192,384]{1,0:T(8,128)(2,1)S(1)}, u32[]{:S(2)}, u32[]{:S(2)}) collective-permute-start(bf16[192,384]{1,0:T(8,128)(2,1)S(1)} %get-tuple-element.24.refs_0_.a_ref), channel_id=1, source_target_pairs={{0,4},{4,0},{8,12},{12,8},{1,5},{5,1},{9,13},{13,9},{2,6},{6,2},{1... | collective-permute-start | bytes 442376 | tf_op jit(solution)/shard_map/ppermute | solution.py:416
  21.0 11.3 %collective-permute-start.1 = (bf16[192,768]{1,0:T(8,128)(2,1)S(1)}, bf16[192,768]{1,0:T(8,128)(2,1)S(1)}, u32[]{:S(2)}, u32[]{:S(2)}) collective-permute-start(bf16[192,768]{1,0:T(8,128)(2,1)S(1)} %collective-permute-done.refs_2_.refs_3_), channel_id=1, source_target_pairs={{0,16},{16,32},{32,48},{48,64},{64,80},{80,96},{96,112},{112,0},{1... | collective-permute-start | bytes 884744 | tf_op jit(solution)/shard_map/ppermute | solution.py:420
  22.9 9.7 %collective-permute-start.4 = (bf16[192,768]{1,0:T(8,128)(2,1)S(1)}, bf16[192,768]{1,0:T(8,128)(2,1)S(1)}, u32[]{:S(2)}, u32[]{:S(2)}) collective-permute-start(bf16[192,768]{1,0:T(8,128)(2,1)S(1)} %collective-permute-done.3.refs_3_.refs_4_), channel_id=1, source_target_pairs={{0,112},{16,0},{32,16},{48,32},{64,48},{80,64},{96,80},{112,96},{1... | collective-permute-start | bytes 884744 | tf_op jit(solution)/shard_map/ppermute | solution.py:420
  25.2 13.1 %collective-permute-start.9 = (bf16[384,384]{1,0:T(8,128)(2,1)S(1)}, bf16[384,384]{1,0:T(8,128)(2,1)S(1)}, u32[]{:S(2)}, u32[]{:S(2)}) collective-permute-start(bf16[384,384]{1,0:T(8,128)(2,1)S(1)} %join.1), channel_id=1, source_target_pairs={{0,8},{4,12},{8,0},{12,4},{1,9},{5,13},{9,1},{13,5},{2,10},{6,14},... | collective-permute-start | bytes 884744 | tf_op jit(solution)/shard_map/ppermute | solution.py:416
  32.2 17.8 %collective-permute-start.2 = (bf16[192,768]{1,0:T(8,128)(2,1)S(1)}, bf16[192,768]{1,0:T(8,128)(2,1)S(1)}, u32[]{:S(2)}, u32[]{:S(2)}) collective-permute-start(bf16[192,768]{1,0:T(8,128)(2,1)S(1)} %collective-permute-done.1.a_ref.refs_4_.refs_5_), channel_id=1, source_target_pairs={{0,16},{16,32},{32,48},{48,64},{64,80},{80,96},{96,112},{112,0},{1... | collective-permute-start | bytes 884744 | tf_op jit(solution)/shard_map/ppermute | solution.py:420
  32.6 17.4 %collective-permute-start.5 = (bf16[192,768]{1,0:T(8,128)(2,1)S(1)}, bf16[192,768]{1,0:T(8,128)(2,1)S(1)}, u32[]{:S(2)}, u32[]{:S(2)}) collective-permute-start(bf16[192,768]{1,0:T(8,128)(2,1)S(1)} %collective-permute-done.4.b_ref.refs_5_.refs_6_), channel_id=1, source_target_pairs={{0,112},{16,0},{32,16},{48,32},{64,48},{80,64},{96,80},{112,96},{1... | collective-permute-start | bytes 884744 | tf_op jit(solution)/shard_map/ppermute | solution.py:420
  35.2 14.8 %collective-permute-start.6 = (bf16[96,768]{1,0:T(8,128)(2,1)S(1)}, bf16[96,768]{1,0:T(8,128)(2,1)S(1)}, u32[]{:S(2)}, u32[]{:S(2)}) collective-permute-start(bf16[96,768]{1,0:T(8,128)(2,1)S(1)} %get-tuple-element.26), channel_id=1, source_target_pairs={{0,32},{16,48},{32,64},{48,80},{64,96},{80,112},{96,0},{112,16},{1... | collective-permute-start | bytes 442376 | tf_op jit(solution)/shard_map/ppermute | solution.py:420
  38.4 11.7 %collective-permute-start.7 = (bf16[96,768]{1,0:T(8,128)(2,1)S(1)}, bf16[96,768]{1,0:T(8,128)(2,1)S(1)}, u32[]{:S(2)}, u32[]{:S(2)}) collective-permute-start(bf16[96,768]{1,0:T(8,128)(2,1)S(1)} %get-tuple-element.27), channel_id=1, source_target_pairs={{0,96},{16,112},{32,0},{48,16},{64,32},{80,48},{96,64},{112,80},{1... | collective-permute-start | bytes 442376 | tf_op jit(solution)/shard_map/ppermute | solution.py:420
  51.4 9.7 %collective-permute-start.11 = (bf16[208,384]{1,0:T(8,128)(2,1)S(1)}, bf16[208,384]{1,0:T(8,128)(2,1)S(1)}, u32[]{:S(2)}, u32[]{:S(2)}) collective-permute-start(bf16[208,384]{1,0:T(8,128)(2,1)S(1)} %last_attention.5), channel_id=1, source_target_pairs={{0,8},{4,12},{8,0},{12,4},{1,9},{5,13},{9,1},{13,5},{2,10},{6,14},... | collective-permute-start | bytes 479240 | tf_op jit(solution)/shard_map/ppermute | solution.py:416
  54.9 6.8 %collective-permute-start.10 = (bf16[208,384]{1,0:T(8,128)(2,1)S(1)}, bf16[208,384]{1,0:T(8,128)(2,1)S(1)}, u32[]{:S(2)}, u32[]{:S(2)}) collective-permute-start(bf16[208,384]{1,0:T(8,128)(2,1)S(1)} %get-tuple-element.34), channel_id=1, source_target_pairs={{0,4},{4,0},{8,12},{12,8},{1,5},{5,1},{9,13},{13,9},{2,6},{6,2},{1... | collective-permute-start | bytes 479240 | tf_op jit(solution)/shard_map/ppermute | solution.py:416
  55.0 6.8 %collective-permute-start.12 = (bf16[208,384]{1,0:T(8,128)(2,1)S(1)}, bf16[208,384]{1,0:T(8,128)(2,1)S(1)}, u32[]{:S(2)}, u32[]{:S(2)}) collective-permute-start(bf16[208,384]{1,0:T(8,128)(2,1)S(1)} %get-tuple-element.38), channel_id=1, source_target_pairs={{0,12},{4,8},{8,4},{12,0},{1,13},{5,9},{9,5},{13,1},{2,14},{6,10},... | collective-permute-start | bytes 479240 | tf_op jit(solution)/shard_map/ppermute | solution.py:416
  58.0 13.7 %collective-permute-start.13 = (bf16[384,1536]{1,0:T(8,128)(2,1)S(1)}, bf16[384,1536]{1,0:T(8,128)(2,1)S(1)}, u32[]{:S(2)}, u32[]{:S(2)}) collective-permute-start(bf16[384,1536]{1,0:T(8,128)(2,1)S(1)} %copy-done.6), channel_id=1, source_target_pairs={{0,1},{1,0},{2,3},{3,2},{4,5},{5,4},{6,7},{7,6},{8,9},{9,8},{10,11... | collective-permute-start | bytes 3538952 | tf_op jit(solution)/shard_map/ppermute | solution.py:416
  61.0 10.7 %copy-start.7 = (f32[1536]{0:T(1024)S(1)}, f32[1536]{0:T(1024)}, u32[]{:S(2)}) copy-start(f32[1536]{0:T(1024)} %gain_ref.3) | copy-start | bytes 18436
  61.0 23.2 %collective-permute-start.19 = (bf16[384,1536]{1,0:T(8,128)(2,1)S(1)}, bf16[384,1536]{1,0:T(8,128)(2,1)S(1)}, u32[]{:S(2)}, u32[]{:S(2)}) collective-permute-start(bf16[384,1536]{1,0:T(8,128)(2,1)S(1)} %copy-done), channel_id=1, source_target_pairs={{0,1},{1,0},{2,3},{3,2},{4,5},{5,4},{6,7},{7,6},{8,9},{9,8},{10,11... | collective-permute-start | bytes 3538952 | tf_op jit(solution)/shard_map/ppermute | solution.py:416
  61.6 10.0 %collective-permute-start.15 = (bf16[384,1536]{1,0:T(8,128)(2,1)S(1)}, bf16[384,1536]{1,0:T(8,128)(2,1)S(1)}, u32[]{:S(2)}, u32[]{:S(2)}) collective-permute-start(bf16[384,1536]{1,0:T(8,128)(2,1)S(1)} %collective-permute-done.14.w2), channel_id=1, source_target_pairs={{0,1},{1,0},{2,3},{3,2},{4,5},{5,4},{6,7},{7,6},{8,9},{9,8},{10,11... | collective-permute-start | bytes 3538952 | tf_op jit(solution)/shard_map/ppermute | solution.py:416
  75.4 8.8 %collective-permute-start.20 = (bf16[160,384]{1,0:T(8,128)(2,1)S(1)}, bf16[160,384]{1,0:T(8,128)(2,1)S(1)}, u32[]{:S(2)}, u32[]{:S(2)}) collective-permute-start(bf16[160,384]{1,0:T(8,128)(2,1)S(1)} %inner.1.own_ref), channel_id=1, source_target_pairs={{0,1},{1,0},{2,3},{3,2},{4,5},{5,4},{6,7},{7,6},{8,9},{9,8},{10,11... | collective-permute-start | bytes 368648 | tf_op jit(solution)/shard_map/ppermute | solution.py:416
  75.8 11.0 %collective-permute-start.16 = (bf16[16,384]{1,0:T(8,128)(2,1)S(1)}, bf16[16,384]{1,0:T(8,128)(2,1)S(1)}, u32[]{:S(2)}, u32[]{:S(2)}) collective-permute-start(bf16[16,384]{1,0:T(8,128)(2,1)S(1)} %get-tuple-element.39), channel_id=1, source_target_pairs={{0,4},{4,8},{8,12},{12,16},{16,20},{20,24},{24,28},{28,32},{32,36}... | collective-permute-start | bytes 36872 | tf_op jit(solution)/shard_map/ppermute | solution.py:465
  82.3 7.7 %collective-permute-start.17 = (bf16[16,384]{1,0:T(8,128)(2,1)S(1)}, bf16[16,384]{1,0:T(8,128)(2,1)S(1)}, u32[]{:S(2)}, u32[]{:S(2)}) collective-permute-start(bf16[16,384]{1,0:T(8,128)(2,1)S(1)} %get-tuple-element.41), channel_id=1, source_target_pairs={{4,0},{8,4},{12,8},{16,12},{20,16},{24,20},{28,24},{32,28},{36,32}... | collective-permute-start | bytes 36872 | tf_op jit(solution)/shard_map/ppermute | solution.py:466
  84.6 12.7 %collective-permute-start.21 = (bf16[160,384]{1,0:T(8,128)(2,1)S(1)}, bf16[160,384]{1,0:T(8,128)(2,1)S(1)}, u32[]{:S(2)}, u32[]{:S(2)}) collective-permute-start(bf16[160,384]{1,0:T(8,128)(2,1)S(1)} %part_sum.4), channel_id=1, source_target_pairs={{0,2},{2,0},{1,3},{3,1},{4,6},{6,4},{5,7},{7,5},{8,10},{10,8},{9,1... | collective-permute-start | bytes 368648 | tf_op jit(solution)/shard_map/ppermute | solution.py:416
  90.3 1.3 %collective-permute-start.18 = (bf16[32,384]{1,0:T(8,128)(2,1)S(1)}, bf16[32,384]{1,0:T(8,128)(2,1)S(1)}, u32[]{:S(2)}, u32[]{:S(2)}) collective-permute-start(bf16[32,384]{1,0:T(8,128)(2,1)S(1)} %edges.1.own_ref), channel_id=1, source_target_pairs={{0,1},{1,0},{2,3},{3,2},{4,5},{5,4},{6,7},{7,6},{8,9},{9,8},{10,11... | collective-permute-start | bytes 73736 | tf_op jit(solution)/shard_map/ppermute | solution.py:416
  91.8 5.4 %collective-permute-start.22 = (bf16[32,384]{1,0:T(8,128)(2,1)S(1)}, bf16[32,384]{1,0:T(8,128)(2,1)S(1)}, u32[]{:S(2)}, u32[]{:S(2)}) collective-permute-start(bf16[32,384]{1,0:T(8,128)(2,1)S(1)} %part_sum.5), channel_id=1, source_target_pairs={{0,2},{2,0},{1,3},{3,1},{4,6},{6,4},{5,7},{7,5},{8,10},{10,8},{9,1... | collective-permute-start | bytes 73736 | tf_op jit(solution)/shard_map/ppermute | solution.py:416
  (8 other events, 42.0 us)

commit v5 on v4

--- a/solution.py
+++ b/solution.py
@@ -179,7 +179,7 @@
 
 
 def combine_kernel(*refs):
-    parts, o_ref = refs[:-1], refs[-1]
+    parts, o_ref = refs[:4], refs[-1]
     lane = lax.broadcasted_iota(jnp.int32, (1, COLS), 1)
     logs = []
     for part in parts:
@@ -202,18 +202,22 @@
     o_ref[...] = total.astype(jnp.bfloat16)
 
 
-def combine(parts):
+def combine(parts, others):
+    vmem = pl.BlockSpec(memory_space=pltpu.VMEM)
+    anywhere = pl.BlockSpec(memory_space=pl.ANY)
     return pl.pallas_call(
         combine_kernel,
+        in_specs=[vmem] * len(parts) + [anywhere] * len(others),
+        out_specs=vmem,
         out_shape=jax.ShapeDtypeStruct((ROWS, COLS), jnp.bfloat16),
         compiler_params=pltpu.CompilerParams(vmem_limit_bytes=VMEM_LIMIT),
         cost_estimate=OVERLAPPED,
         name="combine",
-    )(*parts)
+    )(*parts, *others)
 
 
 def middle_kernel(
-    rows_ref, context_ref, w0, w1, w2, w3, gain_ref, glu_ref, m_ref, g_ref, top_ref, end_ref
+    rows_ref, context_ref, w0, w1, w2, w3, gain_ref, glu_ref, other_ref, m_ref, g_ref, top_ref, end_ref
 ):
     place = lax.axis_index(TP)
     total = rows_ref[...].astype(jnp.float32)
@@ -229,49 +233,62 @@
             m_ref[...] = middle[:, position * COLS : (position + 1) * COLS]
 
     normed = layer_norm(middle, gain_ref[...].reshape(1, D))
-    value = jnp.dot(normed, glu_ref[0], preferred_element_type=jnp.float32)
-    gate = jnp.dot(normed, glu_ref[1], preferred_element_type=jnp.float32)
-    glu = (value * (1.0 / (1.0 + jnp.exp(-gate)))).astype(jnp.bfloat16)
-    g_ref[...] = glu
-    top_ref[...] = glu[:HALO]
-    end_ref[...] = glu[ROWS - HALO :]
-
-
-def middle_and_glu(rows, context, weights, gain, glu_weight):
+    for half, weight in enumerate((glu_ref, other_ref)):
+        value = jnp.dot(normed, weight[0], preferred_element_type=jnp.float32)
+        gate = jnp.dot(normed, weight[1], preferred_element_type=jnp.float32)
+        glu = (value * (1.0 / (1.0 + jnp.exp(-gate)))).astype(jnp.bfloat16)
+        here = slice(half * COLS, (half + 1) * COLS)
+        g_ref[:, here] = glu
+        top_ref[:, here] = glu[:HALO]
+        end_ref[:, here] = glu[ROWS - HALO :]
+
+
+def middle_and_glu(rows, context, weights, gain, glu_weight, glu_other):
     vmem = pl.BlockSpec(memory_space=pltpu.VMEM)
     return pl.pallas_call(
         middle_kernel,
-        in_specs=[vmem] * 8,
+        in_specs=[vmem] * 9,
         out_specs=[vmem] * 4,
-        out_shape=[jax.ShapeDtypeStruct((ROWS, COLS), jnp.bfloat16)] * 2
-        + [jax.ShapeDtypeStruct((HALO, COLS), jnp.bfloat16)] * 2,
+        out_shape=[
+            jax.ShapeDtypeStruct((ROWS, COLS), jnp.bfloat16),
+            jax.ShapeDtypeStruct((ROWS, 2 * COLS), jnp.bfloat16),
+            jax.ShapeDtypeStruct((HALO, 2 * COLS), jnp.bfloat16),
+            jax.ShapeDtypeStruct((HALO, 2 * COLS), jnp.bfloat16),
+        ],
         compiler_params=pltpu.CompilerParams(vmem_limit_bytes=VMEM_LIMIT),
         cost_estimate=OVERLAPPED,
         name="middle",
-    )(rows, context, *weights, gain, glu_weight)
-
-
-def convolve(held, taps_ref, bias_ref, count, store):
-    taps = taps_ref[...].astype(jnp.float32)
-    for column in range(COLS // 128):
-        here = slice(column * 128, (column + 1) * 128)
-        total = jnp.zeros((count, 128), jnp.float32) + bias_ref[here].reshape(1, 128)
-        for tap in range(2 * REACH + 1):
-            begin = HALO - REACH + tap
-            total = total + held[begin : begin + count, here] * taps[tap : tap + 1, here]
-        store(here, (total / (1.0 + jnp.exp(-total))).astype(jnp.bfloat16))
-
-
-def inner_kernel(glu_ref, taps_ref, bias_ref, o_ref, held):
+    )(rows, context, *weights, gain, glu_weight, glu_other)
+
+
+def convolve(held, filters, count, store):
+    for half, (taps_ref, bias_ref) in enumerate(filters):
+        taps = taps_ref[...].astype(jnp.float32)
+        for column in range(COLS // 128):
+            local = slice(column * 128, (column + 1) * 128)
+            here = slice(half * COLS + column * 128, half * COLS + (column + 1) * 128)
+            total = jnp.zeros((count, 128), jnp.float32) + bias_ref[local].reshape(1, 128)
+            for offset in range(8):
+                group = jnp.zeros((count + 8, 128), jnp.float32)
+                for begin in range(offset, 2 * HALO, 8):
+                    tap = begin - (HALO - REACH)
+                    if tap >= 0:
+                        aligned = held[begin - offset : begin - offset + count + 8, here]
+                        group = group + aligned * taps[tap : tap + 1, local]
+                total = total + group[offset : offset + count]
+            store(here, (total / (1.0 + jnp.exp(-total))).astype(jnp.bfloat16))
+
+
+def inner_kernel(glu_ref, taps0, bias0, taps1, bias1, o_ref, held):
     held[...] = glu_ref[...].astype(jnp.float32)
 
     def store(here, value):
         o_ref[:, here] = value
 
-    convolve(held, taps_ref, bias_ref, ROWS - 2 * HALO, store)
-
-
-def edges_kernel(before_ref, glu_ref, after_ref, taps_ref, bias_ref, o_ref, held):
+    convolve(held, ((taps0, bias0), (taps1, bias1)), INNER, store)
+
+
+def edges_kernel(before_ref, glu_ref, after_ref, taps0, bias0, taps1, bias1, o_ref, held):
     for side in range(2):
         if side == 0:
             held[:HALO] = before_ref[...].astype(jnp.float32)
@@ -283,28 +300,28 @@
         def store(here, value):
             o_ref[side * HALO : (side + 1) * HALO, here] = value
 
-        convolve(held, taps_ref, bias_ref, HALO, store)
-
-
-def conv_inner(glu, taps, bias):
+        convolve(held, ((taps0, bias0), (taps1, bias1)), HALO, store)
+
+
+def conv_inner(glu, filters):
     return pl.pallas_call(
         inner_kernel,
-        out_shape=jax.ShapeDtypeStruct((INNER, COLS), jnp.bfloat16),
-        scratch_shapes=[pltpu.VMEM((ROWS, COLS), jnp.float32)],
+        out_shape=jax.ShapeDtypeStruct((INNER, 2 * COLS), jnp.bfloat16),
+        scratch_shapes=[pltpu.VMEM((ROWS, 2 * COLS), jnp.float32)],
         compiler_params=pltpu.CompilerParams(vmem_limit_bytes=VMEM_LIMIT),
         name="inner",
-    )(glu, taps, bias)
-
-
-def conv_edges(before, glu, after, taps, bias):
+    )(glu, *filters)
+
+
+def conv_edges(before, glu, after, filters):
     return pl.pallas_call(
         edges_kernel,
-        out_shape=jax.ShapeDtypeStruct((2 * HALO, COLS), jnp.bfloat16),
-        scratch_shapes=[pltpu.VMEM((3 * HALO, COLS), jnp.float32)],
+        out_shape=jax.ShapeDtypeStruct((2 * HALO, 2 * COLS), jnp.bfloat16),
+        scratch_shapes=[pltpu.VMEM((3 * HALO, 2 * COLS), jnp.float32)],
         compiler_params=pltpu.CompilerParams(vmem_limit_bytes=VMEM_LIMIT),
         cost_estimate=OVERLAPPED,
         name="edges",
-    )(before, glu, after, taps, bias)
+    )(before, glu, after, *filters)
 
 
 def project_kernel(eps_ref, rows_ref, gain_ref, w_ref, kv_ref, q_ref):
@@ -343,73 +360,77 @@
     )()
 
 
-def join_kernel(a_ref, b_ref, o_ref):
+def join_kernel(a_ref, b_ref, _, o_ref):
     o_ref[:ROWS] = a_ref[...]
     o_ref[ROWS:] = b_ref[...]
 
 
-def join(a, b):
+def join(a, b, other):
+    vmem = pl.BlockSpec(memory_space=pltpu.VMEM)
     return pl.pallas_call(
         join_kernel,
+        in_specs=[vmem, vmem, pl.BlockSpec(memory_space=pl.ANY)],
         out_shape=jax.ShapeDtypeStruct((2 * ROWS, COLS), jnp.bfloat16),
         compiler_params=pltpu.CompilerParams(vmem_limit_bytes=VMEM_LIMIT),
         name="join",
-    )(a, b)
-
-
-def halves_kernel(a_ref, b_ref, a_out, b_out):
+    )(a, b, other)
+
+
+def halves_kernel(a_ref, b_ref, _, a_out, b_out):
     a_out[...] = a_ref[: ROWS // 2]
     b_out[...] = b_ref[ROWS // 2 :]
 
 
-def halves(a, b):
+def halves(a, b, other):
+    vmem = pl.BlockSpec(memory_space=pltpu.VMEM)
     return pl.pallas_call(
         halves_kernel,
+        in_specs=[vmem, vmem, pl.BlockSpec(memory_space=pl.ANY)],
         out_shape=[jax.ShapeDtypeStruct((ROWS // 2, 2 * COLS), jnp.bfloat16)] * 2,
         compiler_params=pltpu.CompilerParams(vmem_limit_bytes=VMEM_LIMIT),
         name="halves",
-    )(a, b)
-
-
-def product(flip, own_ref, other_ref, w_own, w_other):
+    )(a, b, other)
+
+
+def product(flip, act_ref, w_own, w_other):
     columns = pl.ds(pl.multiple_of((lax.axis_index(TP) ^ flip) * COLS, 128), COLS)
-    total = jnp.dot(own_ref[...], w_own[:, columns], preferred_element_type=jnp.float32)
+    total = jnp.dot(act_ref[:, :COLS], w_own[:, columns], preferred_element_type=jnp.float32)
     return total + jnp.dot(
-        other_ref[...], w_other[:, columns], preferred_element_type=jnp.float32
+        act_ref[:, COLS:], w_other[:, columns], preferred_element_type=jnp.float32
     )
 
 
-def part_kernel(flip, own_ref, other_ref, w_own, w_other, o_ref):
-    o_ref[...] = product(flip, own_ref, other_ref, w_own, w_other).astype(o_ref.dtype)
-
-
-def part_sum(flip, own, other, weights, kind):
+def part_kernel(flip, act_ref, w_own, w_other, o_ref):
+    o_ref[...] = product(flip, act_ref, w_own, w_other).astype(o_ref.dtype)
+
+
+def part_sum(flip, act, weights, kind):
     return pl.pallas_call(
         functools.partial(part_kernel, flip),
-        out_shape=jax.ShapeDtypeStruct(own.shape, kind),
+        out_shape=jax.ShapeDtypeStruct((act.shape[0], COLS), kind),
         compiler_params=pltpu.CompilerParams(vmem_limit_bytes=VMEM_LIMIT),
         name="part_sum",
-    )(own, other, *weights)
-
-
-def final_kernel(own_ref, other_ref, w_own, w_other, middle_ref, ours_ref, inner_ref, edges_ref, o_ref):
+    )(act, *weights)
+
+
+def final_kernel(act_ref, w_own, w_other, middle_ref, ours_ref, inner_ref, edges_ref, o_ref):
     here = slice(HALO, HALO + INNER)
     total = ours_ref[...] + inner_ref[...].astype(jnp.float32)
     o_ref[here] = (middle_ref[here].astype(jnp.float32) + total).astype(jnp.bfloat16)
-    total = product(0, own_ref, other_ref, w_own, w_other) + edges_ref[...].astype(jnp.float32)
+    total = product(0, act_ref, w_own, w_other) + edges_ref[...].astype(jnp.float32)
     for side in range(2):
         here = slice(side * (ROWS - HALO), side * (ROWS - HALO) + HALO)
         part = total[side * HALO : (side + 1) * HALO]
         o_ref[here] = (middle_ref[here].astype(jnp.float32) + part).astype(jnp.bfloat16)
 
 
-def final(own, other, weights, middle, ours, inner, edges):
+def final(act, weights, middle, ours, inner, edges):
     return pl.pallas_call(
         final_kernel,
         out_shape=jax.ShapeDtypeStruct((ROWS, COLS), jnp.bfloat16),
         compiler_params=pltpu.CompilerParams(vmem_limit_bytes=VMEM_LIMIT),
         name="final",
-    )(own, other, *weights, middle, ours, inner, edges)
+    )(act, *weights, middle, ours, inner, edges)
 
 
 def swap(value, axis, count, flip):
@@ -432,14 +453,15 @@
     proj_weight,
 ):
     out_core = swap(out_weight, "core", 2, 1)
+    glu_core = swap(glu_weight, "core", 2, 1)
     out_far = swap(out_weight, "xh", 2, 1)
     whole_rows = lax.all_gather(frames, TP, axis=1, tiled=True)
     mine, query = project(epsilon(), whole_rows, attn_gain, query_key_value)
     lower1, upper1 = shift(mine, "z", 8, 1), shift(mine, "z", 8, -1)
     query1 = swap(query, "y", 4, 1)
     lower2, upper2 = shift(lower1, "z", 8, 1), shift(upper1, "z", 8, -1)
-    pair2 = swap(join(query, query1), "y", 4, 2)
-    low_half, high_half = halves(lower2, upper2)
+    pair2 = swap(join(query, query1, out_core), "y", 4, 2)
+    low_half, high_half = halves(lower2, upper2, glu_core)
     second = [
         shift(lower2, "z", 8, 1),
         shift(upper2, "z", 8, -1),
@@ -456,23 +478,24 @@
     (partial0,) = last_attention(groups[2], second, priors[2])
     out_far_core = swap(out_far, "core", 2, 1)
     out_pieces = (out_weight, out_core, out_far, out_far_core)
-    context = combine([partial0, part1, part2, part3])
+    taps_core = swap(depth_kernel, "core", 2, 1)
+    bias_core = swap(depth_bias, "core", 2, 1)
+    context = combine([partial0, part1, part2, part3], [taps_core, bias_core])
     proj_core = swap(proj_weight, "core", 2, 1)
     context = lax.all_gather(context, TP, axis=0, tiled=False)
     middle, glu, top, end = middle_and_glu(
-        whole_rows, context, out_pieces, conv_gain, glu_weight
+        whole_rows, context, out_pieces, conv_gain, glu_weight, glu_core
     )
     before = lax.ppermute(end, CTX, [(i, i + 1) for i in range(31)])
     after = lax.ppermute(top, CTX, [(i + 1, i) for i in range(31)])
     weights = (proj_weight, proj_core)
-    inner = conv_inner(glu, depth_kernel, depth_bias)
-    inner_other = swap(inner, "core", 2, 1)
-    inner_far = swap(part_sum(2, inner, inner_other, weights, jnp.bfloat16), "xh", 2, 1)
-    ours = part_sum(0, inner, inner_other, weights, jnp.float32)
-    edges = conv_edges(before, glu, after, depth_kernel, depth_bias)
-    edges_other = swap(edges, "core", 2, 1)
-    edges_far = swap(part_sum(2, edges, edges_other, weights, jnp.bfloat16), "xh", 2, 1)
-    return final(edges, edges_other, weights, middle, ours, inner_far, edges_far)
+    filters = (depth_kernel, depth_bias, taps_core, bias_core)
+    inner = conv_inner(glu, filters)
+    inner_far = swap(part_sum(2, inner, weights, jnp.bfloat16), "xh", 2, 1)
+    ours = part_sum(0, inner, weights, jnp.float32)
+    edges = conv_edges(before, glu, after, filters)
+    edges_far = swap(part_sum(2, edges, weights, jnp.bfloat16), "xh", 2, 1)
+    return final(edges, weights, middle, ours, inner_far, edges_far)
 
 
 def solution(mesh):

time: 98.3 us -> 97.5 us (level)
  waiting for transfers between devices: 23.4 us -> 21.3 us
  Pallas kernels: 19.1 us -> 20.5 us
    ppermute x8, waiting for transfers between devices: 16.1 us -> 12.7 us  [shift(): lax.ppermute(value, axis, [(i, (i + offset) % count) for i in range(count)])]
    ppermute x13 -> x14, waiting for transfers between devices: 4.1 us -> 6.76 us  [swap(): return lax.ppermute(value, axis, [(i, i ^ flip) for i in range(count)])]
    ppermute x1, waiting for transfers between devices: 3.17 us -> 1.8 us  [per_device(): after = lax.ppermute(top, CTX, [(i + 1, i) for i in range(31)])]
    pallas_call x6, Pallas kernels: 4.71 us -> 5.85 us  [the longest x1 3.18 us: middle_and_glu(): pl.pallas_call(middle_kernel, in_specs=[vmem] * 9, out_specs=[vmem] * 4,...]
    ppermute x13 -> x14, starting transfers between devices: 14.6 us -> 15.7 us  [swap(): return lax.ppermute(value, axis, [(i, i ^ flip) for i in range(count)])]
  transfers between devices with their start and end apart: 23 -> 24, of which waited for: 7 -> 8; matrix products, arithmetic and copies ran while one was open for 0% -> 0% of each run, Pallas kernels for 17% -> 20%
where the time goes in v5:
time: 97.5 us; the launch traced here: 96.6 us
  starting transfers between devices  36.4 us (37%)
  waiting for transfers between devices  21.3 us (22%)
  Pallas kernels  20.5 us (21%)
  blocking collectives  17.8 us (18%)
    ppermute x14, starting transfers between devices, swap(): return lax.ppermute(value, axis, [(i, i ^ flip) for i in range(count)])  15.7 us
    ppermute x8, starting transfers between devices, shift(): lax.ppermute(value, axis, [(i, (i + offset) % count) for i in range(count)])  13 us
    ppermute x8, waiting for transfers between devices, shift(): lax.ppermute(value, axis, [(i, (i + offset) % count) for i in range(count)])  12.7 us
    all_gather x1, blocking collectives, per_device(): whole_rows = lax.all_gather(frames, TP, axis=1, tiled=True)  9.18 us
    all_gather x1, blocking collectives, per_device(): context = lax.all_gather(context, TP, axis=0, tiled=False)  8.65 us
    ppermute x14, waiting for transfers between devices, swap(): return lax.ppermute(value, axis, [(i, i ^ flip) for i in range(count)])  6.76 us
    pallas_call x3, Pallas kernels, first_attention(): pl.pallas_call(functools.partial(first_attention_kernel, places, len(bloc...  6.29 us
    ppermute x1, starting transfers between devices, per_device(): before = lax.ppermute(end, CTX, [(i, i + 1) for i in range(31)])  5.78 us
  transfers between devices with their start and end apart: 24, of which 8 were waited for; matrix products, arithmetic and copies ran while one was open for 0% of the time, Pallas kernels for 20%

profile of v5, /device:TPU:56, one launch (start us, length us, event | category | flops | bytes accessed | tf_op | source)
XLA Modules:
  0.0 96.6 jit_solution(8010108825239595457)
XLA Ops:
  0.9 9.2 %all_gather.9.rows_ref = bf16[192,1536]{1,0:T(8,128)(2,1)S(1)} all-gather(bf16[192,384]{1,0:T(8,128)(2,1)S(1)} %copy-done.8), channel_id=1, replica_groups=mesh['batch'=2,'z'=8,'y'=4,'xh'=2,'core'=2] {'xh','core'}, dimensions={1}, use_global_device_ids=true | all-gather | bytes 737280 | tf_op jit(solution)/shard_map/all_gather | solution.py:458
  10.1 1.5 %project.1 = (bf16[192,768]{1,0:T(8,128)(2,1)S(1)}, bf16[192,384]{1,0:T(8,128)(2,1)S(1)}) custom-call(f32[8,128]{1,0:T(8,128)S(1)} %epsilon.1.eps_ref, bf16[192,1536]{1,0:T(8,128)(2,1)S(1)} %all_gather.9.rows_ref, f32[1536]{0:T(1024)S(1)} %copy-done.3, bf16[3,1536,384]{2,1,0:T(8,128)(2,1)S(1)} %copy-done.1), custom_call_target="tpu_custom_call" | custom-call | tf_op jit(solution)/shard_map/project/pallas_call | solution.py:338
  12.4 1.9 %collective-permute-start = (bf16[192,768]{1,0:T(8,128)(2,1)S(1)}, bf16[192,768]{1,0:T(8,128)(2,1)S(1)}, u32[]{:S(2)}, u32[]{:S(2)}) collective-permute-start(bf16[192,768]{1,0:T(8,128)(2,1)S(1)} %get-tuple-element.25.refs_1_.refs_2_), channel_id=1, source_target_pairs={{0,16},{16,32},{32,48},{48,64},{64,80},{80,96},{96,112},{112,0},{1... | collective-permute-start | bytes 884744 | tf_op jit(solution)/shard_map/ppermute | solution.py:441
  14.5 3.3 %collective-permute-done.9.b_ref.refs_0_ = bf16[192,384]{1,0:T(8,128)(2,1)S(1)} collective-permute-done((bf16[192,384]{1,0:T(8,128)(2,1)S(1)}, bf16[192,384]{1,0:T(8,128)(2,1)S(1)}, u32[]{:S(2)}, u32[]{:S(2)}) %collective-permute-start.9) | collective-permute-done | bytes 147488 | tf_op jit(solution)/shard_map/ppermute | solution.py:437
  17.8 2.6 %collective-permute-start.17 = (bf16[384,1536]{1,0:T(8,128)(2,1)S(1)}, bf16[384,1536]{1,0:T(8,128)(2,1)S(1)}, u32[]{:S(2)}, u32[]{:S(2)}) collective-permute-start(bf16[384,1536]{1,0:T(8,128)(2,1)S(1)} %copy-done.6), channel_id=1, source_target_pairs={{0,2},{2,0},{1,3},{3,1},{4,6},{6,4},{5,7},{7,5},{8,10},{10,8},{9,1... | collective-permute-start | bytes 3538952 | tf_op jit(solution)/shard_map/ppermute | solution.py:437
  21.4 1.9 %collective-permute-start.1 = (bf16[192,768]{1,0:T(8,128)(2,1)S(1)}, bf16[192,768]{1,0:T(8,128)(2,1)S(1)}, u32[]{:S(2)}, u32[]{:S(2)}) collective-permute-start(bf16[192,768]{1,0:T(8,128)(2,1)S(1)} %collective-permute-done.refs_2_.refs_3_), channel_id=1, source_target_pairs={{0,16},{16,32},{32,48},{48,64},{64,80},{80,96},{96,112},{112,0},{1... | collective-permute-start | bytes 884744 | tf_op jit(solution)/shard_map/ppermute | solution.py:441
  23.4 2.3 %collective-permute-start.4 = (bf16[192,768]{1,0:T(8,128)(2,1)S(1)}, bf16[192,768]{1,0:T(8,128)(2,1)S(1)}, u32[]{:S(2)}, u32[]{:S(2)}) collective-permute-start(bf16[192,768]{1,0:T(8,128)(2,1)S(1)} %collective-permute-done.3.refs_3_.refs_4_), channel_id=1, source_target_pairs={{0,112},{16,0},{32,16},{48,32},{64,48},{80,64},{96,80},{112,96},{1... | collective-permute-start | bytes 884744 | tf_op jit(solution)/shard_map/ppermute | solution.py:441
  26.7 5.6 %collective-permute-done.1.a_ref.refs_4_.refs_5_ = bf16[192,768]{1,0:T(8,128)(2,1)S(1)} collective-permute-done((bf16[192,768]{1,0:T(8,128)(2,1)S(1)}, bf16[192,768]{1,0:T(8,128)(2,1)S(1)}, u32[]{:S(2)}, u32[]{:S(2)}) %collective-permute-start.1) | collective-permute-done | bytes 294944 | tf_op jit(solution)/shard_map/ppermute | solution.py:441
  32.8 2.5 %collective-permute-start.5 = (bf16[192,768]{1,0:T(8,128)(2,1)S(1)}, bf16[192,768]{1,0:T(8,128)(2,1)S(1)}, u32[]{:S(2)}, u32[]{:S(2)}) collective-permute-start(bf16[192,768]{1,0:T(8,128)(2,1)S(1)} %collective-permute-done.4.b_ref.refs_5_.refs_6_), channel_id=1, source_target_pairs={{0,112},{16,0},{32,16},{48,32},{64,48},{80,64},{96,80},{112,96},{1... | collective-permute-start | bytes 884744 | tf_op jit(solution)/shard_map/ppermute | solution.py:441
  35.4 3.2 %collective-permute-start.7 = (bf16[96,768]{1,0:T(8,128)(2,1)S(1)}, bf16[96,768]{1,0:T(8,128)(2,1)S(1)}, u32[]{:S(2)}, u32[]{:S(2)}) collective-permute-start(bf16[96,768]{1,0:T(8,128)(2,1)S(1)} %get-tuple-element.26), channel_id=1, source_target_pairs={{0,32},{16,48},{32,64},{48,80},{64,96},{80,112},{96,0},{112,16},{1... | collective-permute-start | bytes 442376 | tf_op jit(solution)/shard_map/ppermute | solution.py:441
  39.6 1.7 %first_attention.5 = (f32[192,384]{1,0:T(8,128)S(1)}, f32[192,128]{1,0:T(8,128)S(1)}, f32[192,128]{1,0:T(8,128)S(1)}) custom-call(bf16[384,384]{1,0:T(8,128)(2,1)S(1)} %collective-permute-done.11.refs_1_.refs_0_, bf16[192,768]{1,0:T(8,128)(2,1)S(1)} %get-tuple-element.25.refs_1_.refs_2_, bf16[192,768]{1,0:T(8,128)(2,1)S(1)} %collective-permute-done.refs_2_.refs_3_, ...), custom_call_target="tpu_custom_call" | custom-call | flops 754974720 | bytes 4194304 | tf_op jit(solution)/shard_map/first_attention/pallas_call | solution.py:156
  41.3 2.9 %first_attention.4 = (f32[384,384]{1,0:T(8,128)S(1)}, f32[384,128]{1,0:T(8,128)S(1)}, f32[384,128]{1,0:T(8,128)S(1)}) custom-call(bf16[192,384]{1,0:T(8,128)(2,1)S(1)} %collective-permute-done.9.b_ref.refs_0_, bf16[384,384]{1,0:T(8,128)(2,1)S(1)} %collective-permute-done.11.refs_1_.refs_0_, bf16[192,768]{1,0:T(8,128)(2,1)S(1)} %get-tuple-element.25.refs_1_.refs_2_, ...), custom_call_target="tpu_custom_call" | custom-call | flops 1509949440 | bytes 4194304 | tf_op jit(solution)/shard_map/first_attention/pallas_call | solution.py:156
  44.2 5.6 %collective-permute-done.7.refs_3_.refs_4_ = bf16[96,768]{1,0:T(8,128)(2,1)S(1)} collective-permute-done((bf16[96,768]{1,0:T(8,128)(2,1)S(1)}, bf16[96,768]{1,0:T(8,128)(2,1)S(1)}, u32[]{:S(2)}, u32[]{:S(2)}) %collective-permute-start.7) | collective-permute-done | bytes 147488 | tf_op jit(solution)/shard_map/ppermute | solution.py:441
  49.8 2.5 %last_attention.4 = (bf16[208,384]{1,0:T(8,128)(2,1)S(1)}, bf16[208,384]{1,0:T(8,128)(2,1)S(1)}) custom-call(bf16[192,384]{1,0:T(8,128)(2,1)S(1)} %collective-permute-done.9.b_ref.refs_0_, bf16[384,384]{1,0:T(8,128)(2,1)S(1)} %collective-permute-done.11.refs_1_.refs_0_, bf16[192,768]{1,0:T(8,128)(2,1)S(1)} %collective-permute-done.2.refs_1_.refs_2_, ...), custom_call_target="tpu_custom_call" | custom-call | flops 1207959552 | bytes 4194304 | tf_op jit(solution)/shard_map/last_attention/pallas_call | solution.py:172
  56.3 2.2 %collective-permute-start.14 = (bf16[208,384]{1,0:T(8,128)(2,1)S(1)}, bf16[208,384]{1,0:T(8,128)(2,1)S(1)}, u32[]{:S(2)}, u32[]{:S(2)}) collective-permute-start(bf16[208,384]{1,0:T(8,128)(2,1)S(1)} %get-tuple-element.38), channel_id=1, source_target_pairs={{0,12},{4,8},{8,4},{12,0},{1,13},{5,9},{9,5},{13,1},{2,14},{6,10},... | collective-permute-start | bytes 479240 | tf_op jit(solution)/shard_map/ppermute | solution.py:437
  58.5 1.7 %first_attention.3 = (f32[192,384]{1,0:T(8,128)S(1)}, f32[192,128]{1,0:T(8,128)S(1)}, f32[192,128]{1,0:T(8,128)S(1)}) custom-call(bf16[192,384]{1,0:T(8,128)(2,1)S(1)} %get-tuple-element.24.refs_0_.a_ref, bf16[192,768]{1,0:T(8,128)(2,1)S(1)} %get-tuple-element.25.refs_1_.refs_2_, bf16[192,768]{1,0:T(8,128)(2,1)S(1)} %collective-permute-done.refs_2_.refs_3_, ...), custom_call_target="tpu_custom_call" | custom-call | flops 754974720 | bytes 4194304 | tf_op jit(solution)/shard_map/first_attention/pallas_call | solution.py:156
  64.2 8.7 %all-gather = bf16[768,384]{1,0:T(8,128)(2,1)S(1)} all-gather(bf16[192,384]{1,0:T(8,128)(2,1)S(1)} %combine.1), channel_id=2, replica_groups=mesh['batch'=2,'z'=8,'y'=4,'xh'=2,'core'=2] {'xh','core'}, dimensions={0}, use_global_device_ids=true | all-gather | bytes 737280 | tf_op jit(solution)/shard_map/all_gather | solution.py:485
  72.9 3.2 %middle.1 = (bf16[192,384]{1,0:T(8,128)(2,1)S(1)}, bf16[192,768]{1,0:T(8,128)(2,1)S(1)}, bf16[16,768]{1,0:T(8,128)(2,1)S(1)}, bf16[16,768]{1,0:T(8,128)(2,1)S(1)}) custom-call(bf16[192,1536]{1,0:T(8,128)(2,1)S(1)} %all_gather.9.rows_ref, bf16[4,192,384]{2,1,0:T(8,128)(2,1)S(1)} %bitcast.1, bf16[384,1536]{1,0:T(8,128)(2,1)S(1)} %copy-done.6, ...), custom_call_target="tpu_custom_call" | custom-call | flops 20000000000 | bytes 1048576 | tf_op jit(solution)/shard_map/middle/pallas_call | solution.py:248
  76.1 5.8 %collective-permute-start.19 = (bf16[16,768]{1,0:T(8,128)(2,1)S(1)}, bf16[16,768]{1,0:T(8,128)(2,1)S(1)}, u32[]{:S(2)}, u32[]{:S(2)}) collective-permute-start(bf16[16,768]{1,0:T(8,128)(2,1)S(1)} %get-tuple-element.39), channel_id=1, source_target_pairs={{0,4},{4,8},{8,12},{12,16},{16,20},{20,24},{24,28},{28,32},{32,36}... | collective-permute-start | bytes 73736 | tf_op jit(solution)/shard_map/ppermute | solution.py:489
  81.8 1.9 %collective-permute-start.20 = (bf16[16,768]{1,0:T(8,128)(2,1)S(1)}, bf16[16,768]{1,0:T(8,128)(2,1)S(1)}, u32[]{:S(2)}, u32[]{:S(2)}) collective-permute-start(bf16[16,768]{1,0:T(8,128)(2,1)S(1)} %get-tuple-element.41), channel_id=1, source_target_pairs={{4,0},{8,4},{12,8},{16,12},{20,16},{24,20},{28,24},{32,28},{36,32}... | collective-permute-start | bytes 73736 | tf_op jit(solution)/shard_map/ppermute | solution.py:490
  85.6 2.2 %collective-permute-start.22 = (bf16[160,384]{1,0:T(8,128)(2,1)S(1)}, bf16[160,384]{1,0:T(8,128)(2,1)S(1)}, u32[]{:S(2)}, u32[]{:S(2)}) collective-permute-start(bf16[160,384]{1,0:T(8,128)(2,1)S(1)} %part_sum.4), channel_id=1, source_target_pairs={{0,2},{2,0},{1,3},{3,1},{4,6},{6,4},{5,7},{7,5},{8,10},{10,8},{9,1... | collective-permute-start | bytes 368648 | tf_op jit(solution)/shard_map/ppermute | solution.py:437
  87.9 1.8 %collective-permute-done.20.after_ref = bf16[16,768]{1,0:T(8,128)(2,1)S(1)} collective-permute-done((bf16[16,768]{1,0:T(8,128)(2,1)S(1)}, bf16[16,768]{1,0:T(8,128)(2,1)S(1)}, u32[]{:S(2)}, u32[]{:S(2)}) %collective-permute-start.20) | collective-permute-done | bytes 24608 | tf_op jit(solution)/shard_map/ppermute | solution.py:490
  90.3 2.2 %collective-permute-start.23 = (bf16[32,384]{1,0:T(8,128)(2,1)S(1)}, bf16[32,384]{1,0:T(8,128)(2,1)S(1)}, u32[]{:S(2)}, u32[]{:S(2)}) collective-permute-start(bf16[32,384]{1,0:T(8,128)(2,1)S(1)} %part_sum.5), channel_id=1, source_target_pairs={{0,2},{2,0},{1,3},{3,1},{4,6},{6,4},{5,7},{7,5},{8,10},{10,8},{9,1... | collective-permute-start | bytes 73736 | tf_op jit(solution)/shard_map/ppermute | solution.py:437
  92.9 2.9 %collective-permute-done.23.edges_ref = bf16[32,384]{1,0:T(8,128)(2,1)S(1)} collective-permute-done((bf16[32,384]{1,0:T(8,128)(2,1)S(1)}, bf16[32,384]{1,0:T(8,128)(2,1)S(1)}, u32[]{:S(2)}, u32[]{:S(2)}) %collective-permute-start.23) | collective-permute-done | bytes 24608 | tf_op jit(solution)/shard_map/ppermute | solution.py:437
  (62 shorter events, 17.1 us)
Async XLA Ops:
  0.0 35.3 %collective-permute-start.6 = (bf16[2,1536,384]{2,1,0:T(8,128)(2,1)}, bf16[2,1536,384]{2,1,0:T(8,128)(2,1)S(1)}, u32[]{:S(2)}, u32[]{:S(2)}) collective-permute-start(bf16[2,1536,384]{2,1,0:T(8,128)(2,1)} %glu_ref.1), channel_id=1, source_target_pairs={{0,1},{1,0},{2,3},{3,2},{4,5},{5,4},{6,7},{7,6},{8,9},{9,8},{10,11... | collective-permute-start | bytes 7077896 | tf_op jit(solution)/shard_map/ppermute | solution.py:437
  0.0 25.6 %collective-permute-start.10 = (bf16[384,1536]{1,0:T(8,128)(2,1)}, bf16[384,1536]{1,0:T(8,128)(2,1)S(1)}, u32[]{:S(2)}, u32[]{:S(2)}) collective-permute-start(bf16[384,1536]{1,0:T(8,128)(2,1)} %w0.1), channel_id=1, source_target_pairs={{0,1},{1,0},{2,3},{3,2},{4,5},{5,4},{6,7},{7,6},{8,9},{9,8},{10,11... | collective-permute-start | bytes 3538952 | tf_op jit(solution)/shard_map/ppermute | solution.py:437
  11.6 6.2 %collective-permute-start.9 = (bf16[192,384]{1,0:T(8,128)(2,1)S(1)}, bf16[192,384]{1,0:T(8,128)(2,1)S(1)}, u32[]{:S(2)}, u32[]{:S(2)}) collective-permute-start(bf16[192,384]{1,0:T(8,128)(2,1)S(1)} %get-tuple-element.24.refs_0_.a_ref), channel_id=1, source_target_pairs={{0,4},{4,0},{8,12},{12,8},{1,5},{5,1},{9,13},{13,9},{2,6},{6,2},{1... | collective-permute-start | bytes 442376 | tf_op jit(solution)/shard_map/ppermute | solution.py:437
  12.4 9.0 %collective-permute-start = (bf16[192,768]{1,0:T(8,128)(2,1)S(1)}, bf16[192,768]{1,0:T(8,128)(2,1)S(1)}, u32[]{:S(2)}, u32[]{:S(2)}) collective-permute-start(bf16[192,768]{1,0:T(8,128)(2,1)S(1)} %get-tuple-element.25.refs_1_.refs_2_), channel_id=1, source_target_pairs={{0,16},{16,32},{32,48},{48,64},{64,80},{80,96},{96,112},{112,0},{1... | collective-permute-start | bytes 884744 | tf_op jit(solution)/shard_map/ppermute | solution.py:441
  14.4 9.0 %collective-permute-start.3 = (bf16[192,768]{1,0:T(8,128)(2,1)S(1)}, bf16[192,768]{1,0:T(8,128)(2,1)S(1)}, u32[]{:S(2)}, u32[]{:S(2)}) collective-permute-start(bf16[192,768]{1,0:T(8,128)(2,1)S(1)} %get-tuple-element.25.refs_1_.refs_2_), channel_id=1, source_target_pairs={{0,112},{16,0},{32,16},{48,32},{64,48},{80,64},{96,80},{112,96},{1... | collective-permute-start | bytes 884744 | tf_op jit(solution)/shard_map/ppermute | solution.py:441
  17.8 44.7 %collective-permute-start.17 = (bf16[384,1536]{1,0:T(8,128)(2,1)S(1)}, bf16[384,1536]{1,0:T(8,128)(2,1)S(1)}, u32[]{:S(2)}, u32[]{:S(2)}) collective-permute-start(bf16[384,1536]{1,0:T(8,128)(2,1)S(1)} %copy-done.6), channel_id=1, source_target_pairs={{0,2},{2,0},{1,3},{3,1},{4,6},{6,4},{5,7},{7,5},{8,10},{10,8},{9,1... | collective-permute-start | bytes 3538952 | tf_op jit(solution)/shard_map/ppermute | solution.py:437
  21.4 10.9 %collective-permute-start.1 = (bf16[192,768]{1,0:T(8,128)(2,1)S(1)}, bf16[192,768]{1,0:T(8,128)(2,1)S(1)}, u32[]{:S(2)}, u32[]{:S(2)}) collective-permute-start(bf16[192,768]{1,0:T(8,128)(2,1)S(1)} %collective-permute-done.refs_2_.refs_3_), channel_id=1, source_target_pairs={{0,16},{16,32},{32,48},{48,64},{64,80},{80,96},{96,112},{112,0},{1... | collective-permute-start | bytes 884744 | tf_op jit(solution)/shard_map/ppermute | solution.py:441
  23.4 9.4 %collective-permute-start.4 = (bf16[192,768]{1,0:T(8,128)(2,1)S(1)}, bf16[192,768]{1,0:T(8,128)(2,1)S(1)}, u32[]{:S(2)}, u32[]{:S(2)}) collective-permute-start(bf16[192,768]{1,0:T(8,128)(2,1)S(1)} %collective-permute-done.3.refs_3_.refs_4_), channel_id=1, source_target_pairs={{0,112},{16,0},{32,16},{48,32},{64,48},{80,64},{96,80},{112,96},{1... | collective-permute-start | bytes 884744 | tf_op jit(solution)/shard_map/ppermute | solution.py:441
  25.7 12.8 %collective-permute-start.11 = (bf16[384,384]{1,0:T(8,128)(2,1)S(1)}, bf16[384,384]{1,0:T(8,128)(2,1)S(1)}, u32[]{:S(2)}, u32[]{:S(2)}) collective-permute-start(bf16[384,384]{1,0:T(8,128)(2,1)S(1)} %join.1), channel_id=1, source_target_pairs={{0,8},{4,12},{8,0},{12,4},{1,9},{5,13},{9,1},{13,5},{2,10},{6,14},... | collective-permute-start | bytes 884744 | tf_op jit(solution)/shard_map/ppermute | solution.py:437
  32.4 11.8 %collective-permute-start.2 = (bf16[192,768]{1,0:T(8,128)(2,1)S(1)}, bf16[192,768]{1,0:T(8,128)(2,1)S(1)}, u32[]{:S(2)}, u32[]{:S(2)}) collective-permute-start(bf16[192,768]{1,0:T(8,128)(2,1)S(1)} %collective-permute-done.1.a_ref.refs_4_.refs_5_), channel_id=1, source_target_pairs={{0,16},{16,32},{32,48},{48,64},{64,80},{80,96},{96,112},{112,0},{1... | collective-permute-start | bytes 884744 | tf_op jit(solution)/shard_map/ppermute | solution.py:441
  32.8 11.4 %collective-permute-start.5 = (bf16[192,768]{1,0:T(8,128)(2,1)S(1)}, bf16[192,768]{1,0:T(8,128)(2,1)S(1)}, u32[]{:S(2)}, u32[]{:S(2)}) collective-permute-start(bf16[192,768]{1,0:T(8,128)(2,1)S(1)} %collective-permute-done.4.b_ref.refs_5_.refs_6_), channel_id=1, source_target_pairs={{0,112},{16,0},{32,16},{48,32},{64,48},{80,64},{96,80},{112,96},{1... | collective-permute-start | bytes 884744 | tf_op jit(solution)/shard_map/ppermute | solution.py:441
  35.4 14.5 %collective-permute-start.7 = (bf16[96,768]{1,0:T(8,128)(2,1)S(1)}, bf16[96,768]{1,0:T(8,128)(2,1)S(1)}, u32[]{:S(2)}, u32[]{:S(2)}) collective-permute-start(bf16[96,768]{1,0:T(8,128)(2,1)S(1)} %get-tuple-element.26), channel_id=1, source_target_pairs={{0,32},{16,48},{32,64},{48,80},{64,96},{80,112},{96,0},{112,16},{1... | collective-permute-start | bytes 442376 | tf_op jit(solution)/shard_map/ppermute | solution.py:441
  38.5 11.3 %collective-permute-start.8 = (bf16[96,768]{1,0:T(8,128)(2,1)S(1)}, bf16[96,768]{1,0:T(8,128)(2,1)S(1)}, u32[]{:S(2)}, u32[]{:S(2)}) collective-permute-start(bf16[96,768]{1,0:T(8,128)(2,1)S(1)} %get-tuple-element.27), channel_id=1, source_target_pairs={{0,96},{16,112},{32,0},{48,16},{64,32},{80,48},{96,64},{112,80},{1... | collective-permute-start | bytes 442376 | tf_op jit(solution)/shard_map/ppermute | solution.py:441
  52.3 10.7 %collective-permute-start.12 = (bf16[208,384]{1,0:T(8,128)(2,1)S(1)}, bf16[208,384]{1,0:T(8,128)(2,1)S(1)}, u32[]{:S(2)}, u32[]{:S(2)}) collective-permute-start(bf16[208,384]{1,0:T(8,128)(2,1)S(1)} %get-tuple-element.34), channel_id=1, source_target_pairs={{0,4},{4,0},{8,12},{12,8},{1,5},{5,1},{9,13},{13,9},{2,6},{6,2},{1... | collective-permute-start | bytes 479240 | tf_op jit(solution)/shard_map/ppermute | solution.py:437
  55.0 8.1 %collective-permute-start.13 = (bf16[208,384]{1,0:T(8,128)(2,1)S(1)}, bf16[208,384]{1,0:T(8,128)(2,1)S(1)}, u32[]{:S(2)}, u32[]{:S(2)}) collective-permute-start(bf16[208,384]{1,0:T(8,128)(2,1)S(1)} %last_attention.5), channel_id=1, source_target_pairs={{0,8},{4,12},{8,0},{12,4},{1,9},{5,13},{9,1},{13,5},{2,10},{6,14},... | collective-permute-start | bytes 479240 | tf_op jit(solution)/shard_map/ppermute | solution.py:437
  56.3 7.2 %collective-permute-start.14 = (bf16[208,384]{1,0:T(8,128)(2,1)S(1)}, bf16[208,384]{1,0:T(8,128)(2,1)S(1)}, u32[]{:S(2)}, u32[]{:S(2)}) collective-permute-start(bf16[208,384]{1,0:T(8,128)(2,1)S(1)} %get-tuple-element.38), channel_id=1, source_target_pairs={{0,12},{4,8},{8,4},{12,0},{1,13},{5,9},{9,5},{13,1},{2,14},{6,10},... | collective-permute-start | bytes 479240 | tf_op jit(solution)/shard_map/ppermute | solution.py:437
  58.5 1.7 %collective-permute-start.16 = (f32[384]{0:T(512)S(1)}, f32[384]{0:T(512)S(1)}, u32[]{:S(2)}, u32[]{:S(2)}) collective-permute-start(f32[384]{0:T(512)S(1)} %copy-done.4), channel_id=1, source_target_pairs={{0,1},{1,0},{2,3},{3,2},{4,5},{5,4},{6,7},{7,6},{8,9},{9,8},{10,11... | collective-permute-start | bytes 4616 | tf_op jit(solution)/shard_map/ppermute | solution.py:437
  60.2 2.2 %collective-permute-start.15 = (bf16[31,384]{1,0:T(8,128)(2,1)S(1)}, bf16[31,384]{1,0:T(8,128)(2,1)S(1)}, u32[]{:S(2)}, u32[]{:S(2)}) collective-permute-start(bf16[31,384]{1,0:T(8,128)(2,1)S(1)} %copy-done.2), channel_id=1, source_target_pairs={{0,1},{1,0},{2,3},{3,2},{4,5},{5,4},{6,7},{7,6},{8,9},{9,8},{10,11... | collective-permute-start | bytes 71432 | tf_op jit(solution)/shard_map/ppermute | solution.py:437
  62.4 22.9 %collective-permute-start.21 = (bf16[384,1536]{1,0:T(8,128)(2,1)S(1)}, bf16[384,1536]{1,0:T(8,128)(2,1)S(1)}, u32[]{:S(2)}, u32[]{:S(2)}) collective-permute-start(bf16[384,1536]{1,0:T(8,128)(2,1)S(1)} %copy-done), channel_id=1, source_target_pairs={{0,1},{1,0},{2,3},{3,2},{4,5},{5,4},{6,7},{7,6},{8,9},{9,8},{10,11... | collective-permute-start | bytes 3538952 | tf_op jit(solution)/shard_map/ppermute | solution.py:437
  62.5 10.3 %collective-permute-start.18 = (bf16[384,1536]{1,0:T(8,128)(2,1)S(1)}, bf16[384,1536]{1,0:T(8,128)(2,1)S(1)}, u32[]{:S(2)}, u32[]{:S(2)}) collective-permute-start(bf16[384,1536]{1,0:T(8,128)(2,1)S(1)} %collective-permute-done.17.w2), channel_id=1, source_target_pairs={{0,1},{1,0},{2,3},{3,2},{4,5},{5,4},{6,7},{7,6},{8,9},{9,8},{10,11... | collective-permute-start | bytes 3538952 | tf_op jit(solution)/shard_map/ppermute | solution.py:437
  76.1 11.8 %collective-permute-start.19 = (bf16[16,768]{1,0:T(8,128)(2,1)S(1)}, bf16[16,768]{1,0:T(8,128)(2,1)S(1)}, u32[]{:S(2)}, u32[]{:S(2)}) collective-permute-start(bf16[16,768]{1,0:T(8,128)(2,1)S(1)} %get-tuple-element.39), channel_id=1, source_target_pairs={{0,4},{4,8},{8,12},{12,16},{16,20},{20,24},{24,28},{28,32},{32,36}... | collective-permute-start | bytes 73736 | tf_op jit(solution)/shard_map/ppermute | solution.py:489
  81.8 7.8 %collective-permute-start.20 = (bf16[16,768]{1,0:T(8,128)(2,1)S(1)}, bf16[16,768]{1,0:T(8,128)(2,1)S(1)}, u32[]{:S(2)}, u32[]{:S(2)}) collective-permute-start(bf16[16,768]{1,0:T(8,128)(2,1)S(1)} %get-tuple-element.41), channel_id=1, source_target_pairs={{4,0},{8,4},{12,8},{16,12},{20,16},{24,20},{28,24},{32,28},{36,32}... | collective-permute-start | bytes 73736 | tf_op jit(solution)/shard_map/ppermute | solution.py:490
  85.6 10.1 %collective-permute-start.22 = (bf16[160,384]{1,0:T(8,128)(2,1)S(1)}, bf16[160,384]{1,0:T(8,128)(2,1)S(1)}, u32[]{:S(2)}, u32[]{:S(2)}) collective-permute-start(bf16[160,384]{1,0:T(8,128)(2,1)S(1)} %part_sum.4), channel_id=1, source_target_pairs={{0,2},{2,0},{1,3},{3,1},{4,6},{6,4},{5,7},{7,5},{8,10},{10,8},{9,1... | collective-permute-start | bytes 368648 | tf_op jit(solution)/shard_map/ppermute | solution.py:437
  90.3 5.4 %collective-permute-start.23 = (bf16[32,384]{1,0:T(8,128)(2,1)S(1)}, bf16[32,384]{1,0:T(8,128)(2,1)S(1)}, u32[]{:S(2)}, u32[]{:S(2)}) collective-permute-start(bf16[32,384]{1,0:T(8,128)(2,1)S(1)} %part_sum.5), channel_id=1, source_target_pairs={{0,2},{2,0},{1,3},{3,1},{4,6},{6,4},{5,7},{7,5},{8,10},{10,8},{9,1... | collective-permute-start | bytes 73736 | tf_op jit(solution)/shard_map/ppermute | solution.py:437
  (9 other events, 61.6 us)

commit v6 on v5

--- a/solution.py
+++ b/solution.py
@@ -413,24 +413,24 @@
     )(act, *weights)
 
 
-def final_kernel(act_ref, w_own, w_other, middle_ref, ours_ref, inner_ref, edges_ref, o_ref):
+def final_kernel(middle_ref, ours_ref, ours_edges_ref, inner_ref, edges_ref, o_ref):
     here = slice(HALO, HALO + INNER)
     total = ours_ref[...] + inner_ref[...].astype(jnp.float32)
     o_ref[here] = (middle_ref[here].astype(jnp.float32) + total).astype(jnp.bfloat16)
-    total = product(0, act_ref, w_own, w_other) + edges_ref[...].astype(jnp.float32)
+    total = ours_edges_ref[...] + edges_ref[...].astype(jnp.float32)
     for side in range(2):
         here = slice(side * (ROWS - HALO), side * (ROWS - HALO) + HALO)
         part = total[side * HALO : (side + 1) * HALO]
         o_ref[here] = (middle_ref[here].astype(jnp.float32) + part).astype(jnp.bfloat16)
 
 
-def final(act, weights, middle, ours, inner, edges):
+def final(middle, ours, ours_edges, inner, edges):
     return pl.pallas_call(
         final_kernel,
         out_shape=jax.ShapeDtypeStruct((ROWS, COLS), jnp.bfloat16),
         compiler_params=pltpu.CompilerParams(vmem_limit_bytes=VMEM_LIMIT),
         name="final",
-    )(act, *weights, middle, ours, inner, edges)
+    )(middle, ours, ours_edges, inner, edges)
 
 
 def swap(value, axis, count, flip):
@@ -495,7 +495,8 @@
     ours = part_sum(0, inner, weights, jnp.float32)
     edges = conv_edges(before, glu, after, filters)
     edges_far = swap(part_sum(2, edges, weights, jnp.bfloat16), "xh", 2, 1)
-    return final(edges, weights, middle, ours, inner_far, edges_far)
+    ours_edges = part_sum(0, edges, weights, jnp.float32)
+    return final(middle, ours, ours_edges, inner_far, edges_far)
 
 
 def solution(mesh):

time: 97.5 us -> 97.4 us (level)
  transfers between devices with their start and end apart: 24 -> 24, of which waited for: 8 -> 8; matrix products, arithmetic and copies ran while one was open for 0% -> 0% of each run, Pallas kernels for 20% -> 21%
where the time goes in v6:
time: 97.4 us; the launch traced here: 96.5 us
  starting transfers between devices  36.4 us (37%)
  waiting for transfers between devices  21 us (22%)
  Pallas kernels  20.6 us (21%)
  blocking collectives  17.8 us (18%)
    ppermute x14, starting transfers between devices, swap(): return lax.ppermute(value, axis, [(i, i ^ flip) for i in range(count)])  15.7 us
    ppermute x8, starting transfers between devices, shift(): lax.ppermute(value, axis, [(i, (i + offset) % count) for i in range(count)])  13 us
    ppermute x8, waiting for transfers between devices, shift(): lax.ppermute(value, axis, [(i, (i + offset) % count) for i in range(count)])  12.7 us
    all_gather x1, blocking collectives, per_device(): whole_rows = lax.all_gather(frames, TP, axis=1, tiled=True)  9.18 us
    all_gather x1, blocking collectives, per_device(): context = lax.all_gather(context, TP, axis=0, tiled=False)  8.65 us
    ppermute x14, waiting for transfers between devices, swap(): return lax.ppermute(value, axis, [(i, i ^ flip) for i in range(count)])  6.55 us
    pallas_call x3, Pallas kernels, first_attention(): pl.pallas_call(functools.partial(first_attention_kernel, places, len(bloc...  6.29 us
    ppermute x1, starting transfers between devices, per_device(): before = lax.ppermute(end, CTX, [(i, i + 1) for i in range(31)])  5.78 us
  transfers between devices with their start and end apart: 24, of which 8 were waited for; matrix products, arithmetic and copies ran while one was open for 0% of the time, Pallas kernels for 21%

profile of v6, /device:TPU:56, one launch (start us, length us, event | category | flops | bytes accessed | tf_op | source)
XLA Modules:
  0.0 96.5 jit_solution(2715398381417686104)
XLA Ops:
  0.9 9.2 %all_gather.9.rows_ref = bf16[192,1536]{1,0:T(8,128)(2,1)S(1)} all-gather(bf16[192,384]{1,0:T(8,128)(2,1)S(1)} %copy-done.8), channel_id=1, replica_groups=mesh['batch'=2,'z'=8,'y'=4,'xh'=2,'core'=2] {'xh','core'}, dimensions={1}, use_global_device_ids=true | all-gather | bytes 737280 | tf_op jit(solution)/shard_map/all_gather | solution.py:458
  10.1 1.5 %project.1 = (bf16[192,768]{1,0:T(8,128)(2,1)S(1)}, bf16[192,384]{1,0:T(8,128)(2,1)S(1)}) custom-call(f32[8,128]{1,0:T(8,128)S(1)} %epsilon.1.eps_ref, bf16[192,1536]{1,0:T(8,128)(2,1)S(1)} %all_gather.9.rows_ref, f32[1536]{0:T(1024)S(1)} %copy-done.3, bf16[3,1536,384]{2,1,0:T(8,128)(2,1)S(1)} %copy-done.1), custom_call_target="tpu_custom_call" | custom-call | tf_op jit(solution)/shard_map/project/pallas_call | solution.py:338
  12.4 1.9 %collective-permute-start = (bf16[192,768]{1,0:T(8,128)(2,1)S(1)}, bf16[192,768]{1,0:T(8,128)(2,1)S(1)}, u32[]{:S(2)}, u32[]{:S(2)}) collective-permute-start(bf16[192,768]{1,0:T(8,128)(2,1)S(1)} %get-tuple-element.25.refs_1_.refs_2_), channel_id=1, source_target_pairs={{0,16},{16,32},{32,48},{48,64},{64,80},{80,96},{96,112},{112,0},{1... | collective-permute-start | bytes 884744 | tf_op jit(solution)/shard_map/ppermute | solution.py:441
  14.5 3.3 %collective-permute-done.9.b_ref.refs_0_ = bf16[192,384]{1,0:T(8,128)(2,1)S(1)} collective-permute-done((bf16[192,384]{1,0:T(8,128)(2,1)S(1)}, bf16[192,384]{1,0:T(8,128)(2,1)S(1)}, u32[]{:S(2)}, u32[]{:S(2)}) %collective-permute-start.9) | collective-permute-done | bytes 147488 | tf_op jit(solution)/shard_map/ppermute | solution.py:437
  17.8 2.6 %collective-permute-start.17 = (bf16[384,1536]{1,0:T(8,128)(2,1)S(1)}, bf16[384,1536]{1,0:T(8,128)(2,1)S(1)}, u32[]{:S(2)}, u32[]{:S(2)}) collective-permute-start(bf16[384,1536]{1,0:T(8,128)(2,1)S(1)} %copy-done.6), channel_id=1, source_target_pairs={{0,2},{2,0},{1,3},{3,1},{4,6},{6,4},{5,7},{7,5},{8,10},{10,8},{9,1... | collective-permute-start | bytes 3538952 | tf_op jit(solution)/shard_map/ppermute | solution.py:437
  21.4 1.9 %collective-permute-start.1 = (bf16[192,768]{1,0:T(8,128)(2,1)S(1)}, bf16[192,768]{1,0:T(8,128)(2,1)S(1)}, u32[]{:S(2)}, u32[]{:S(2)}) collective-permute-start(bf16[192,768]{1,0:T(8,128)(2,1)S(1)} %collective-permute-done.refs_2_.refs_3_), channel_id=1, source_target_pairs={{0,16},{16,32},{32,48},{48,64},{64,80},{80,96},{96,112},{112,0},{1... | collective-permute-start | bytes 884744 | tf_op jit(solution)/shard_map/ppermute | solution.py:441
  23.4 2.3 %collective-permute-start.4 = (bf16[192,768]{1,0:T(8,128)(2,1)S(1)}, bf16[192,768]{1,0:T(8,128)(2,1)S(1)}, u32[]{:S(2)}, u32[]{:S(2)}) collective-permute-start(bf16[192,768]{1,0:T(8,128)(2,1)S(1)} %collective-permute-done.3.refs_3_.refs_4_), channel_id=1, source_target_pairs={{0,112},{16,0},{32,16},{48,32},{64,48},{80,64},{96,80},{112,96},{1... | collective-permute-start | bytes 884744 | tf_op jit(solution)/shard_map/ppermute | solution.py:441
  26.7 5.6 %collective-permute-done.1.a_ref.refs_4_.refs_5_ = bf16[192,768]{1,0:T(8,128)(2,1)S(1)} collective-permute-done((bf16[192,768]{1,0:T(8,128)(2,1)S(1)}, bf16[192,768]{1,0:T(8,128)(2,1)S(1)}, u32[]{:S(2)}, u32[]{:S(2)}) %collective-permute-start.1) | collective-permute-done | bytes 294944 | tf_op jit(solution)/shard_map/ppermute | solution.py:441
  32.8 2.5 %collective-permute-start.5 = (bf16[192,768]{1,0:T(8,128)(2,1)S(1)}, bf16[192,768]{1,0:T(8,128)(2,1)S(1)}, u32[]{:S(2)}, u32[]{:S(2)}) collective-permute-start(bf16[192,768]{1,0:T(8,128)(2,1)S(1)} %collective-permute-done.4.b_ref.refs_5_.refs_6_), channel_id=1, source_target_pairs={{0,112},{16,0},{32,16},{48,32},{64,48},{80,64},{96,80},{112,96},{1... | collective-permute-start | bytes 884744 | tf_op jit(solution)/shard_map/ppermute | solution.py:441
  35.4 3.2 %collective-permute-start.7 = (bf16[96,768]{1,0:T(8,128)(2,1)S(1)}, bf16[96,768]{1,0:T(8,128)(2,1)S(1)}, u32[]{:S(2)}, u32[]{:S(2)}) collective-permute-start(bf16[96,768]{1,0:T(8,128)(2,1)S(1)} %get-tuple-element.26), channel_id=1, source_target_pairs={{0,32},{16,48},{32,64},{48,80},{64,96},{80,112},{96,0},{112,16},{1... | collective-permute-start | bytes 442376 | tf_op jit(solution)/shard_map/ppermute | solution.py:441
  39.6 1.7 %first_attention.5 = (f32[192,384]{1,0:T(8,128)S(1)}, f32[192,128]{1,0:T(8,128)S(1)}, f32[192,128]{1,0:T(8,128)S(1)}) custom-call(bf16[384,384]{1,0:T(8,128)(2,1)S(1)} %collective-permute-done.11.refs_1_.refs_0_, bf16[192,768]{1,0:T(8,128)(2,1)S(1)} %get-tuple-element.25.refs_1_.refs_2_, bf16[192,768]{1,0:T(8,128)(2,1)S(1)} %collective-permute-done.refs_2_.refs_3_, ...), custom_call_target="tpu_custom_call" | custom-call | flops 754974720 | bytes 4194304 | tf_op jit(solution)/shard_map/first_attention/pallas_call | solution.py:156
  41.3 2.9 %first_attention.4 = (f32[384,384]{1,0:T(8,128)S(1)}, f32[384,128]{1,0:T(8,128)S(1)}, f32[384,128]{1,0:T(8,128)S(1)}) custom-call(bf16[192,384]{1,0:T(8,128)(2,1)S(1)} %collective-permute-done.9.b_ref.refs_0_, bf16[384,384]{1,0:T(8,128)(2,1)S(1)} %collective-permute-done.11.refs_1_.refs_0_, bf16[192,768]{1,0:T(8,128)(2,1)S(1)} %get-tuple-element.25.refs_1_.refs_2_, ...), custom_call_target="tpu_custom_call" | custom-call | flops 1509949440 | bytes 4194304 | tf_op jit(solution)/shard_map/first_attention/pallas_call | solution.py:156
  44.2 5.6 %collective-permute-done.7.refs_3_.refs_4_ = bf16[96,768]{1,0:T(8,128)(2,1)S(1)} collective-permute-done((bf16[96,768]{1,0:T(8,128)(2,1)S(1)}, bf16[96,768]{1,0:T(8,128)(2,1)S(1)}, u32[]{:S(2)}, u32[]{:S(2)}) %collective-permute-start.7) | collective-permute-done | bytes 147488 | tf_op jit(solution)/shard_map/ppermute | solution.py:441
  49.8 2.5 %last_attention.4 = (bf16[208,384]{1,0:T(8,128)(2,1)S(1)}, bf16[208,384]{1,0:T(8,128)(2,1)S(1)}) custom-call(bf16[192,384]{1,0:T(8,128)(2,1)S(1)} %collective-permute-done.9.b_ref.refs_0_, bf16[384,384]{1,0:T(8,128)(2,1)S(1)} %collective-permute-done.11.refs_1_.refs_0_, bf16[192,768]{1,0:T(8,128)(2,1)S(1)} %collective-permute-done.2.refs_1_.refs_2_, ...), custom_call_target="tpu_custom_call" | custom-call | flops 1207959552 | bytes 4194304 | tf_op jit(solution)/shard_map/last_attention/pallas_call | solution.py:172
  56.3 2.2 %collective-permute-start.14 = (bf16[208,384]{1,0:T(8,128)(2,1)S(1)}, bf16[208,384]{1,0:T(8,128)(2,1)S(1)}, u32[]{:S(2)}, u32[]{:S(2)}) collective-permute-start(bf16[208,384]{1,0:T(8,128)(2,1)S(1)} %get-tuple-element.38), channel_id=1, source_target_pairs={{0,12},{4,8},{8,4},{12,0},{1,13},{5,9},{9,5},{13,1},{2,14},{6,10},... | collective-permute-start | bytes 479240 | tf_op jit(solution)/shard_map/ppermute | solution.py:437
  58.5 1.7 %first_attention.3 = (f32[192,384]{1,0:T(8,128)S(1)}, f32[192,128]{1,0:T(8,128)S(1)}, f32[192,128]{1,0:T(8,128)S(1)}) custom-call(bf16[192,384]{1,0:T(8,128)(2,1)S(1)} %get-tuple-element.24.refs_0_.a_ref, bf16[192,768]{1,0:T(8,128)(2,1)S(1)} %get-tuple-element.25.refs_1_.refs_2_, bf16[192,768]{1,0:T(8,128)(2,1)S(1)} %collective-permute-done.refs_2_.refs_3_, ...), custom_call_target="tpu_custom_call" | custom-call | flops 754974720 | bytes 4194304 | tf_op jit(solution)/shard_map/first_attention/pallas_call | solution.py:156
  64.2 8.7 %all-gather = bf16[768,384]{1,0:T(8,128)(2,1)S(1)} all-gather(bf16[192,384]{1,0:T(8,128)(2,1)S(1)} %combine.1), channel_id=2, replica_groups=mesh['batch'=2,'z'=8,'y'=4,'xh'=2,'core'=2] {'xh','core'}, dimensions={0}, use_global_device_ids=true | all-gather | bytes 737280 | tf_op jit(solution)/shard_map/all_gather | solution.py:485
  72.9 3.2 %middle.1 = (bf16[192,384]{1,0:T(8,128)(2,1)S(1)}, bf16[192,768]{1,0:T(8,128)(2,1)S(1)}, bf16[16,768]{1,0:T(8,128)(2,1)S(1)}, bf16[16,768]{1,0:T(8,128)(2,1)S(1)}) custom-call(bf16[192,1536]{1,0:T(8,128)(2,1)S(1)} %all_gather.9.rows_ref, bf16[4,192,384]{2,1,0:T(8,128)(2,1)S(1)} %bitcast.1, bf16[384,1536]{1,0:T(8,128)(2,1)S(1)} %copy-done.6, ...), custom_call_target="tpu_custom_call" | custom-call | flops 20000000000 | bytes 1048576 | tf_op jit(solution)/shard_map/middle/pallas_call | solution.py:248
  76.1 5.8 %collective-permute-start.20 = (bf16[16,768]{1,0:T(8,128)(2,1)S(1)}, bf16[16,768]{1,0:T(8,128)(2,1)S(1)}, u32[]{:S(2)}, u32[]{:S(2)}) collective-permute-start(bf16[16,768]{1,0:T(8,128)(2,1)S(1)} %get-tuple-element.41), channel_id=1, source_target_pairs={{0,4},{4,8},{8,12},{12,16},{16,20},{20,24},{24,28},{28,32},{32,36}... | collective-permute-start | bytes 73736 | tf_op jit(solution)/shard_map/ppermute | solution.py:489
  81.8 1.9 %collective-permute-start.21 = (bf16[16,768]{1,0:T(8,128)(2,1)S(1)}, bf16[16,768]{1,0:T(8,128)(2,1)S(1)}, u32[]{:S(2)}, u32[]{:S(2)}) collective-permute-start(bf16[16,768]{1,0:T(8,128)(2,1)S(1)} %get-tuple-element.42), channel_id=1, source_target_pairs={{4,0},{8,4},{12,8},{16,12},{20,16},{24,20},{28,24},{32,28},{36,32}... | collective-permute-start | bytes 73736 | tf_op jit(solution)/shard_map/ppermute | solution.py:490
  85.6 2.2 %collective-permute-start.22 = (bf16[160,384]{1,0:T(8,128)(2,1)S(1)}, bf16[160,384]{1,0:T(8,128)(2,1)S(1)}, u32[]{:S(2)}, u32[]{:S(2)}) collective-permute-start(bf16[160,384]{1,0:T(8,128)(2,1)S(1)} %part_sum.6), channel_id=1, source_target_pairs={{0,2},{2,0},{1,3},{3,1},{4,6},{6,4},{5,7},{7,5},{8,10},{10,8},{9,1... | collective-permute-start | bytes 368648 | tf_op jit(solution)/shard_map/ppermute | solution.py:437
  87.9 1.8 %collective-permute-done.21.after_ref = bf16[16,768]{1,0:T(8,128)(2,1)S(1)} collective-permute-done((bf16[16,768]{1,0:T(8,128)(2,1)S(1)}, bf16[16,768]{1,0:T(8,128)(2,1)S(1)}, u32[]{:S(2)}, u32[]{:S(2)}) %collective-permute-start.21) | collective-permute-done | bytes 24608 | tf_op jit(solution)/shard_map/ppermute | solution.py:490
  90.3 2.2 %collective-permute-start.23 = (bf16[32,384]{1,0:T(8,128)(2,1)S(1)}, bf16[32,384]{1,0:T(8,128)(2,1)S(1)}, u32[]{:S(2)}, u32[]{:S(2)}) collective-permute-start(bf16[32,384]{1,0:T(8,128)(2,1)S(1)} %part_sum.7), channel_id=1, source_target_pairs={{0,2},{2,0},{1,3},{3,1},{4,6},{6,4},{5,7},{7,5},{8,10},{10,8},{9,1... | collective-permute-start | bytes 73736 | tf_op jit(solution)/shard_map/ppermute | solution.py:437
  93.1 2.7 %collective-permute-done.23.edges_ref = bf16[32,384]{1,0:T(8,128)(2,1)S(1)} collective-permute-done((bf16[32,384]{1,0:T(8,128)(2,1)S(1)}, bf16[32,384]{1,0:T(8,128)(2,1)S(1)}, u32[]{:S(2)}, u32[]{:S(2)}) %collective-permute-start.23) | collective-permute-done | bytes 24608 | tf_op jit(solution)/shard_map/ppermute | solution.py:437
  (63 shorter events, 17.1 us)
Async XLA Ops:
  0.0 35.3 %collective-permute-start.6 = (bf16[2,1536,384]{2,1,0:T(8,128)(2,1)}, bf16[2,1536,384]{2,1,0:T(8,128)(2,1)S(1)}, u32[]{:S(2)}, u32[]{:S(2)}) collective-permute-start(bf16[2,1536,384]{2,1,0:T(8,128)(2,1)} %glu_ref.1), channel_id=1, source_target_pairs={{0,1},{1,0},{2,3},{3,2},{4,5},{5,4},{6,7},{7,6},{8,9},{9,8},{10,11... | collective-permute-start | bytes 7077896 | tf_op jit(solution)/shard_map/ppermute | solution.py:437
  0.0 25.6 %collective-permute-start.10 = (bf16[384,1536]{1,0:T(8,128)(2,1)}, bf16[384,1536]{1,0:T(8,128)(2,1)S(1)}, u32[]{:S(2)}, u32[]{:S(2)}) collective-permute-start(bf16[384,1536]{1,0:T(8,128)(2,1)} %w0.1), channel_id=1, source_target_pairs={{0,1},{1,0},{2,3},{3,2},{4,5},{5,4},{6,7},{7,6},{8,9},{9,8},{10,11... | collective-permute-start | bytes 3538952 | tf_op jit(solution)/shard_map/ppermute | solution.py:437
  11.6 6.2 %collective-permute-start.9 = (bf16[192,384]{1,0:T(8,128)(2,1)S(1)}, bf16[192,384]{1,0:T(8,128)(2,1)S(1)}, u32[]{:S(2)}, u32[]{:S(2)}) collective-permute-start(bf16[192,384]{1,0:T(8,128)(2,1)S(1)} %get-tuple-element.24.refs_0_.a_ref), channel_id=1, source_target_pairs={{0,4},{4,0},{8,12},{12,8},{1,5},{5,1},{9,13},{13,9},{2,6},{6,2},{1... | collective-permute-start | bytes 442376 | tf_op jit(solution)/shard_map/ppermute | solution.py:437
  12.4 9.0 %collective-permute-start = (bf16[192,768]{1,0:T(8,128)(2,1)S(1)}, bf16[192,768]{1,0:T(8,128)(2,1)S(1)}, u32[]{:S(2)}, u32[]{:S(2)}) collective-permute-start(bf16[192,768]{1,0:T(8,128)(2,1)S(1)} %get-tuple-element.25.refs_1_.refs_2_), channel_id=1, source_target_pairs={{0,16},{16,32},{32,48},{48,64},{64,80},{80,96},{96,112},{112,0},{1... | collective-permute-start | bytes 884744 | tf_op jit(solution)/shard_map/ppermute | solution.py:441
  14.4 9.0 %collective-permute-start.3 = (bf16[192,768]{1,0:T(8,128)(2,1)S(1)}, bf16[192,768]{1,0:T(8,128)(2,1)S(1)}, u32[]{:S(2)}, u32[]{:S(2)}) collective-permute-start(bf16[192,768]{1,0:T(8,128)(2,1)S(1)} %get-tuple-element.25.refs_1_.refs_2_), channel_id=1, source_target_pairs={{0,112},{16,0},{32,16},{48,32},{64,48},{80,64},{96,80},{112,96},{1... | collective-permute-start | bytes 884744 | tf_op jit(solution)/shard_map/ppermute | solution.py:441
  17.8 44.7 %collective-permute-start.17 = (bf16[384,1536]{1,0:T(8,128)(2,1)S(1)}, bf16[384,1536]{1,0:T(8,128)(2,1)S(1)}, u32[]{:S(2)}, u32[]{:S(2)}) collective-permute-start(bf16[384,1536]{1,0:T(8,128)(2,1)S(1)} %copy-done.6), channel_id=1, source_target_pairs={{0,2},{2,0},{1,3},{3,1},{4,6},{6,4},{5,7},{7,5},{8,10},{10,8},{9,1... | collective-permute-start | bytes 3538952 | tf_op jit(solution)/shard_map/ppermute | solution.py:437
  21.4 10.9 %collective-permute-start.1 = (bf16[192,768]{1,0:T(8,128)(2,1)S(1)}, bf16[192,768]{1,0:T(8,128)(2,1)S(1)}, u32[]{:S(2)}, u32[]{:S(2)}) collective-permute-start(bf16[192,768]{1,0:T(8,128)(2,1)S(1)} %collective-permute-done.refs_2_.refs_3_), channel_id=1, source_target_pairs={{0,16},{16,32},{32,48},{48,64},{64,80},{80,96},{96,112},{112,0},{1... | collective-permute-start | bytes 884744 | tf_op jit(solution)/shard_map/ppermute | solution.py:441
  23.4 9.4 %collective-permute-start.4 = (bf16[192,768]{1,0:T(8,128)(2,1)S(1)}, bf16[192,768]{1,0:T(8,128)(2,1)S(1)}, u32[]{:S(2)}, u32[]{:S(2)}) collective-permute-start(bf16[192,768]{1,0:T(8,128)(2,1)S(1)} %collective-permute-done.3.refs_3_.refs_4_), channel_id=1, source_target_pairs={{0,112},{16,0},{32,16},{48,32},{64,48},{80,64},{96,80},{112,96},{1... | collective-permute-start | bytes 884744 | tf_op jit(solution)/shard_map/ppermute | solution.py:441
  25.7 12.8 %collective-permute-start.11 = (bf16[384,384]{1,0:T(8,128)(2,1)S(1)}, bf16[384,384]{1,0:T(8,128)(2,1)S(1)}, u32[]{:S(2)}, u32[]{:S(2)}) collective-permute-start(bf16[384,384]{1,0:T(8,128)(2,1)S(1)} %join.1), channel_id=1, source_target_pairs={{0,8},{4,12},{8,0},{12,4},{1,9},{5,13},{9,1},{13,5},{2,10},{6,14},... | collective-permute-start | bytes 884744 | tf_op jit(solution)/shard_map/ppermute | solution.py:437
  32.4 11.8 %collective-permute-start.2 = (bf16[192,768]{1,0:T(8,128)(2,1)S(1)}, bf16[192,768]{1,0:T(8,128)(2,1)S(1)}, u32[]{:S(2)}, u32[]{:S(2)}) collective-permute-start(bf16[192,768]{1,0:T(8,128)(2,1)S(1)} %collective-permute-done.1.a_ref.refs_4_.refs_5_), channel_id=1, source_target_pairs={{0,16},{16,32},{32,48},{48,64},{64,80},{80,96},{96,112},{112,0},{1... | collective-permute-start | bytes 884744 | tf_op jit(solution)/shard_map/ppermute | solution.py:441
  32.8 11.4 %collective-permute-start.5 = (bf16[192,768]{1,0:T(8,128)(2,1)S(1)}, bf16[192,768]{1,0:T(8,128)(2,1)S(1)}, u32[]{:S(2)}, u32[]{:S(2)}) collective-permute-start(bf16[192,768]{1,0:T(8,128)(2,1)S(1)} %collective-permute-done.4.b_ref.refs_5_.refs_6_), channel_id=1, source_target_pairs={{0,112},{16,0},{32,16},{48,32},{64,48},{80,64},{96,80},{112,96},{1... | collective-permute-start | bytes 884744 | tf_op jit(solution)/shard_map/ppermute | solution.py:441
  35.4 14.5 %collective-permute-start.7 = (bf16[96,768]{1,0:T(8,128)(2,1)S(1)}, bf16[96,768]{1,0:T(8,128)(2,1)S(1)}, u32[]{:S(2)}, u32[]{:S(2)}) collective-permute-start(bf16[96,768]{1,0:T(8,128)(2,1)S(1)} %get-tuple-element.26), channel_id=1, source_target_pairs={{0,32},{16,48},{32,64},{48,80},{64,96},{80,112},{96,0},{112,16},{1... | collective-permute-start | bytes 442376 | tf_op jit(solution)/shard_map/ppermute | solution.py:441
  38.5 11.3 %collective-permute-start.8 = (bf16[96,768]{1,0:T(8,128)(2,1)S(1)}, bf16[96,768]{1,0:T(8,128)(2,1)S(1)}, u32[]{:S(2)}, u32[]{:S(2)}) collective-permute-start(bf16[96,768]{1,0:T(8,128)(2,1)S(1)} %get-tuple-element.27), channel_id=1, source_target_pairs={{0,96},{16,112},{32,0},{48,16},{64,32},{80,48},{96,64},{112,80},{1... | collective-permute-start | bytes 442376 | tf_op jit(solution)/shard_map/ppermute | solution.py:441
  52.3 10.7 %collective-permute-start.12 = (bf16[208,384]{1,0:T(8,128)(2,1)S(1)}, bf16[208,384]{1,0:T(8,128)(2,1)S(1)}, u32[]{:S(2)}, u32[]{:S(2)}) collective-permute-start(bf16[208,384]{1,0:T(8,128)(2,1)S(1)} %get-tuple-element.34), channel_id=1, source_target_pairs={{0,4},{4,0},{8,12},{12,8},{1,5},{5,1},{9,13},{13,9},{2,6},{6,2},{1... | collective-permute-start | bytes 479240 | tf_op jit(solution)/shard_map/ppermute | solution.py:437
  55.0 8.1 %collective-permute-start.13 = (bf16[208,384]{1,0:T(8,128)(2,1)S(1)}, bf16[208,384]{1,0:T(8,128)(2,1)S(1)}, u32[]{:S(2)}, u32[]{:S(2)}) collective-permute-start(bf16[208,384]{1,0:T(8,128)(2,1)S(1)} %last_attention.5), channel_id=1, source_target_pairs={{0,8},{4,12},{8,0},{12,4},{1,9},{5,13},{9,1},{13,5},{2,10},{6,14},... | collective-permute-start | bytes 479240 | tf_op jit(solution)/shard_map/ppermute | solution.py:437
  56.3 7.2 %collective-permute-start.14 = (bf16[208,384]{1,0:T(8,128)(2,1)S(1)}, bf16[208,384]{1,0:T(8,128)(2,1)S(1)}, u32[]{:S(2)}, u32[]{:S(2)}) collective-permute-start(bf16[208,384]{1,0:T(8,128)(2,1)S(1)} %get-tuple-element.38), channel_id=1, source_target_pairs={{0,12},{4,8},{8,4},{12,0},{1,13},{5,9},{9,5},{13,1},{2,14},{6,10},... | collective-permute-start | bytes 479240 | tf_op jit(solution)/shard_map/ppermute | solution.py:437
  58.5 1.7 %collective-permute-start.16 = (f32[384]{0:T(512)S(1)}, f32[384]{0:T(512)S(1)}, u32[]{:S(2)}, u32[]{:S(2)}) collective-permute-start(f32[384]{0:T(512)S(1)} %copy-done.4), channel_id=1, source_target_pairs={{0,1},{1,0},{2,3},{3,2},{4,5},{5,4},{6,7},{7,6},{8,9},{9,8},{10,11... | collective-permute-start | bytes 4616 | tf_op jit(solution)/shard_map/ppermute | solution.py:437
  60.2 2.2 %collective-permute-start.15 = (bf16[31,384]{1,0:T(8,128)(2,1)S(1)}, bf16[31,384]{1,0:T(8,128)(2,1)S(1)}, u32[]{:S(2)}, u32[]{:S(2)}) collective-permute-start(bf16[31,384]{1,0:T(8,128)(2,1)S(1)} %copy-done.2), channel_id=1, source_target_pairs={{0,1},{1,0},{2,3},{3,2},{4,5},{5,4},{6,7},{7,6},{8,9},{9,8},{10,11... | collective-permute-start | bytes 71432 | tf_op jit(solution)/shard_map/ppermute | solution.py:437
  62.4 22.9 %collective-permute-start.19 = (bf16[384,1536]{1,0:T(8,128)(2,1)S(1)}, bf16[384,1536]{1,0:T(8,128)(2,1)S(1)}, u32[]{:S(2)}, u32[]{:S(2)}) collective-permute-start(bf16[384,1536]{1,0:T(8,128)(2,1)S(1)} %copy-done), channel_id=1, source_target_pairs={{0,1},{1,0},{2,3},{3,2},{4,5},{5,4},{6,7},{7,6},{8,9},{9,8},{10,11... | collective-permute-start | bytes 3538952 | tf_op jit(solution)/shard_map/ppermute | solution.py:437
  62.5 10.3 %collective-permute-start.18 = (bf16[384,1536]{1,0:T(8,128)(2,1)S(1)}, bf16[384,1536]{1,0:T(8,128)(2,1)S(1)}, u32[]{:S(2)}, u32[]{:S(2)}) collective-permute-start(bf16[384,1536]{1,0:T(8,128)(2,1)S(1)} %collective-permute-done.17.w2), channel_id=1, source_target_pairs={{0,1},{1,0},{2,3},{3,2},{4,5},{5,4},{6,7},{7,6},{8,9},{9,8},{10,11... | collective-permute-start | bytes 3538952 | tf_op jit(solution)/shard_map/ppermute | solution.py:437
  76.1 11.8 %collective-permute-start.20 = (bf16[16,768]{1,0:T(8,128)(2,1)S(1)}, bf16[16,768]{1,0:T(8,128)(2,1)S(1)}, u32[]{:S(2)}, u32[]{:S(2)}) collective-permute-start(bf16[16,768]{1,0:T(8,128)(2,1)S(1)} %get-tuple-element.41), channel_id=1, source_target_pairs={{0,4},{4,8},{8,12},{12,16},{16,20},{20,24},{24,28},{28,32},{32,36}... | collective-permute-start | bytes 73736 | tf_op jit(solution)/shard_map/ppermute | solution.py:489
  81.8 7.8 %collective-permute-start.21 = (bf16[16,768]{1,0:T(8,128)(2,1)S(1)}, bf16[16,768]{1,0:T(8,128)(2,1)S(1)}, u32[]{:S(2)}, u32[]{:S(2)}) collective-permute-start(bf16[16,768]{1,0:T(8,128)(2,1)S(1)} %get-tuple-element.42), channel_id=1, source_target_pairs={{4,0},{8,4},{12,8},{16,12},{20,16},{24,20},{28,24},{32,28},{36,32}... | collective-permute-start | bytes 73736 | tf_op jit(solution)/shard_map/ppermute | solution.py:490
  85.6 10.1 %collective-permute-start.22 = (bf16[160,384]{1,0:T(8,128)(2,1)S(1)}, bf16[160,384]{1,0:T(8,128)(2,1)S(1)}, u32[]{:S(2)}, u32[]{:S(2)}) collective-permute-start(bf16[160,384]{1,0:T(8,128)(2,1)S(1)} %part_sum.6), channel_id=1, source_target_pairs={{0,2},{2,0},{1,3},{3,1},{4,6},{6,4},{5,7},{7,5},{8,10},{10,8},{9,1... | collective-permute-start | bytes 368648 | tf_op jit(solution)/shard_map/ppermute | solution.py:437
  90.3 5.4 %collective-permute-start.23 = (bf16[32,384]{1,0:T(8,128)(2,1)S(1)}, bf16[32,384]{1,0:T(8,128)(2,1)S(1)}, u32[]{:S(2)}, u32[]{:S(2)}) collective-permute-start(bf16[32,384]{1,0:T(8,128)(2,1)S(1)} %part_sum.7), channel_id=1, source_target_pairs={{0,2},{2,0},{1,3},{3,1},{4,6},{6,4},{5,7},{7,5},{8,10},{10,8},{9,1... | collective-permute-start | bytes 73736 | tf_op jit(solution)/shard_map/ppermute | solution.py:437
  (9 other events, 61.6 us)

commit v7 on v6

--- a/solution.py
+++ b/solution.py
@@ -288,7 +288,7 @@
     convolve(held, ((taps0, bias0), (taps1, bias1)), INNER, store)
 
 
-def edges_kernel(before_ref, glu_ref, after_ref, taps0, bias0, taps1, bias1, o_ref, held):
+def edges_kernel(before_ref, glu_ref, after_ref, taps0, bias0, taps1, bias1, w_own, w_other, o_ref, far_ref, held):
     for side in range(2):
         if side == 0:
             held[:HALO] = before_ref[...].astype(jnp.float32)
@@ -301,6 +301,7 @@
             o_ref[side * HALO : (side + 1) * HALO, here] = value
 
         convolve(held, ((taps0, bias0), (taps1, bias1)), HALO, store)
+    far_ref[...] = product(2, o_ref, w_own, w_other).astype(jnp.bfloat16)
 
 
 def conv_inner(glu, filters):
@@ -313,15 +314,18 @@
     )(glu, *filters)
 
 
-def conv_edges(before, glu, after, filters):
+def conv_edges(before, glu, after, filters, weights):
     return pl.pallas_call(
         edges_kernel,
-        out_shape=jax.ShapeDtypeStruct((2 * HALO, 2 * COLS), jnp.bfloat16),
+        out_shape=[
+            jax.ShapeDtypeStruct((2 * HALO, 2 * COLS), jnp.bfloat16),
+            jax.ShapeDtypeStruct((2 * HALO, COLS), jnp.bfloat16),
+        ],
         scratch_shapes=[pltpu.VMEM((3 * HALO, 2 * COLS), jnp.float32)],
         compiler_params=pltpu.CompilerParams(vmem_limit_bytes=VMEM_LIMIT),
         cost_estimate=OVERLAPPED,
         name="edges",
-    )(before, glu, after, *filters)
+    )(before, glu, after, *filters, *weights)
 
 
 def project_kernel(eps_ref, rows_ref, gain_ref, w_ref, kv_ref, q_ref):
@@ -493,8 +497,8 @@
     inner = conv_inner(glu, filters)
     inner_far = swap(part_sum(2, inner, weights, jnp.bfloat16), "xh", 2, 1)
     ours = part_sum(0, inner, weights, jnp.float32)
-    edges = conv_edges(before, glu, after, filters)
-    edges_far = swap(part_sum(2, edges, weights, jnp.bfloat16), "xh", 2, 1)
+    edges, edges_far = conv_edges(before, glu, after, filters, weights)
+    edges_far = swap(edges_far, "xh", 2, 1)
     ours_edges = part_sum(0, edges, weights, jnp.float32)
     return final(middle, ours, ours_edges, inner_far, edges_far)
 

time: 97.4 us -> 97.2 us (level)
  transfers between devices with their start and end apart: 24 -> 24, of which waited for: 8 -> 8; matrix products, arithmetic and copies ran while one was open for 0% -> 0% of each run, Pallas kernels for 21% -> 20%
where the time goes in v7:
time: 97.2 us; the launch traced here: 96.3 us
  starting transfers between devices  36.4 us (37%)
  waiting for transfers between devices  21.1 us (22%)
  Pallas kernels  20.4 us (21%)
  blocking collectives  17.8 us (18%)
    ppermute x14, starting transfers between devices, swap(): return lax.ppermute(value, axis, [(i, i ^ flip) for i in range(count)])  15.7 us
    ppermute x8, starting transfers between devices, shift(): lax.ppermute(value, axis, [(i, (i + offset) % count) for i in range(count)])  13 us
    ppermute x8, waiting for transfers between devices, shift(): lax.ppermute(value, axis, [(i, (i + offset) % count) for i in range(count)])  12.7 us
    all_gather x1, blocking collectives, per_device(): whole_rows = lax.all_gather(frames, TP, axis=1, tiled=True)  9.18 us
    all_gather x1, blocking collectives, per_device(): context = lax.all_gather(context, TP, axis=0, tiled=False)  8.65 us
    ppermute x14, waiting for transfers between devices, swap(): return lax.ppermute(value, axis, [(i, i ^ flip) for i in range(count)])  6.57 us
    pallas_call x3, Pallas kernels, first_attention(): pl.pallas_call(functools.partial(first_attention_kernel, places, len(bloc...  6.3 us
    ppermute x1, starting transfers between devices, per_device(): before = lax.ppermute(end, CTX, [(i, i + 1) for i in range(31)])  5.79 us
  transfers between devices with their start and end apart: 24, of which 8 were waited for; matrix products, arithmetic and copies ran while one was open for 0% of the time, Pallas kernels for 20%

profile of v7, /device:TPU:56, one launch (start us, length us, event | category | flops | bytes accessed | tf_op | source)
XLA Modules:
  0.0 96.3 jit_solution(12280379940749719180)
XLA Ops:
  0.9 9.2 %all_gather.9.rows_ref = bf16[192,1536]{1,0:T(8,128)(2,1)S(1)} all-gather(bf16[192,384]{1,0:T(8,128)(2,1)S(1)} %copy-done.8), channel_id=1, replica_groups=mesh['batch'=2,'z'=8,'y'=4,'xh'=2,'core'=2] {'xh','core'}, dimensions={1}, use_global_device_ids=true | all-gather | bytes 737280 | tf_op jit(solution)/shard_map/all_gather | solution.py:462
  10.1 1.5 %project.1 = (bf16[192,768]{1,0:T(8,128)(2,1)S(1)}, bf16[192,384]{1,0:T(8,128)(2,1)S(1)}) custom-call(f32[8,128]{1,0:T(8,128)S(1)} %epsilon.1.eps_ref, bf16[192,1536]{1,0:T(8,128)(2,1)S(1)} %all_gather.9.rows_ref, f32[1536]{0:T(1024)S(1)} %copy-done.3, bf16[3,1536,384]{2,1,0:T(8,128)(2,1)S(1)} %copy-done.1), custom_call_target="tpu_custom_call" | custom-call | tf_op jit(solution)/shard_map/project/pallas_call | solution.py:342
  12.4 1.9 %collective-permute-start = (bf16[192,768]{1,0:T(8,128)(2,1)S(1)}, bf16[192,768]{1,0:T(8,128)(2,1)S(1)}, u32[]{:S(2)}, u32[]{:S(2)}) collective-permute-start(bf16[192,768]{1,0:T(8,128)(2,1)S(1)} %get-tuple-element.27.refs_1_.refs_2_), channel_id=1, source_target_pairs={{0,16},{16,32},{32,48},{48,64},{64,80},{80,96},{96,112},{112,0},{1... | collective-permute-start | bytes 884744 | tf_op jit(solution)/shard_map/ppermute | solution.py:445
  14.5 3.3 %collective-permute-done.9.b_ref.refs_0_ = bf16[192,384]{1,0:T(8,128)(2,1)S(1)} collective-permute-done((bf16[192,384]{1,0:T(8,128)(2,1)S(1)}, bf16[192,384]{1,0:T(8,128)(2,1)S(1)}, u32[]{:S(2)}, u32[]{:S(2)}) %collective-permute-start.9) | collective-permute-done | bytes 147488 | tf_op jit(solution)/shard_map/ppermute | solution.py:441
  17.8 2.6 %collective-permute-start.17 = (bf16[384,1536]{1,0:T(8,128)(2,1)S(1)}, bf16[384,1536]{1,0:T(8,128)(2,1)S(1)}, u32[]{:S(2)}, u32[]{:S(2)}) collective-permute-start(bf16[384,1536]{1,0:T(8,128)(2,1)S(1)} %copy-done.6), channel_id=1, source_target_pairs={{0,2},{2,0},{1,3},{3,1},{4,6},{6,4},{5,7},{7,5},{8,10},{10,8},{9,1... | collective-permute-start | bytes 3538952 | tf_op jit(solution)/shard_map/ppermute | solution.py:441
  21.4 1.9 %collective-permute-start.1 = (bf16[192,768]{1,0:T(8,128)(2,1)S(1)}, bf16[192,768]{1,0:T(8,128)(2,1)S(1)}, u32[]{:S(2)}, u32[]{:S(2)}) collective-permute-start(bf16[192,768]{1,0:T(8,128)(2,1)S(1)} %collective-permute-done.refs_2_.refs_3_), channel_id=1, source_target_pairs={{0,16},{16,32},{32,48},{48,64},{64,80},{80,96},{96,112},{112,0},{1... | collective-permute-start | bytes 884744 | tf_op jit(solution)/shard_map/ppermute | solution.py:445
  23.4 2.3 %collective-permute-start.4 = (bf16[192,768]{1,0:T(8,128)(2,1)S(1)}, bf16[192,768]{1,0:T(8,128)(2,1)S(1)}, u32[]{:S(2)}, u32[]{:S(2)}) collective-permute-start(bf16[192,768]{1,0:T(8,128)(2,1)S(1)} %collective-permute-done.3.refs_3_.refs_4_), channel_id=1, source_target_pairs={{0,112},{16,0},{32,16},{48,32},{64,48},{80,64},{96,80},{112,96},{1... | collective-permute-start | bytes 884744 | tf_op jit(solution)/shard_map/ppermute | solution.py:445
  26.7 5.6 %collective-permute-done.1.a_ref.refs_4_.refs_5_ = bf16[192,768]{1,0:T(8,128)(2,1)S(1)} collective-permute-done((bf16[192,768]{1,0:T(8,128)(2,1)S(1)}, bf16[192,768]{1,0:T(8,128)(2,1)S(1)}, u32[]{:S(2)}, u32[]{:S(2)}) %collective-permute-start.1) | collective-permute-done | bytes 294944 | tf_op jit(solution)/shard_map/ppermute | solution.py:445
  32.8 2.5 %collective-permute-start.5 = (bf16[192,768]{1,0:T(8,128)(2,1)S(1)}, bf16[192,768]{1,0:T(8,128)(2,1)S(1)}, u32[]{:S(2)}, u32[]{:S(2)}) collective-permute-start(bf16[192,768]{1,0:T(8,128)(2,1)S(1)} %collective-permute-done.4.b_ref.refs_5_.refs_6_), channel_id=1, source_target_pairs={{0,112},{16,0},{32,16},{48,32},{64,48},{80,64},{96,80},{112,96},{1... | collective-permute-start | bytes 884744 | tf_op jit(solution)/shard_map/ppermute | solution.py:445
  35.4 3.2 %collective-permute-start.7 = (bf16[96,768]{1,0:T(8,128)(2,1)S(1)}, bf16[96,768]{1,0:T(8,128)(2,1)S(1)}, u32[]{:S(2)}, u32[]{:S(2)}) collective-permute-start(bf16[96,768]{1,0:T(8,128)(2,1)S(1)} %get-tuple-element.28), channel_id=1, source_target_pairs={{0,32},{16,48},{32,64},{48,80},{64,96},{80,112},{96,0},{112,16},{1... | collective-permute-start | bytes 442376 | tf_op jit(solution)/shard_map/ppermute | solution.py:445
  39.6 1.7 %first_attention.5 = (f32[192,384]{1,0:T(8,128)S(1)}, f32[192,128]{1,0:T(8,128)S(1)}, f32[192,128]{1,0:T(8,128)S(1)}) custom-call(bf16[384,384]{1,0:T(8,128)(2,1)S(1)} %collective-permute-done.11.refs_1_.refs_0_, bf16[192,768]{1,0:T(8,128)(2,1)S(1)} %get-tuple-element.27.refs_1_.refs_2_, bf16[192,768]{1,0:T(8,128)(2,1)S(1)} %collective-permute-done.refs_2_.refs_3_, ...), custom_call_target="tpu_custom_call" | custom-call | flops 754974720 | bytes 4194304 | tf_op jit(solution)/shard_map/first_attention/pallas_call | solution.py:156
  41.3 2.9 %first_attention.4 = (f32[384,384]{1,0:T(8,128)S(1)}, f32[384,128]{1,0:T(8,128)S(1)}, f32[384,128]{1,0:T(8,128)S(1)}) custom-call(bf16[192,384]{1,0:T(8,128)(2,1)S(1)} %collective-permute-done.9.b_ref.refs_0_, bf16[384,384]{1,0:T(8,128)(2,1)S(1)} %collective-permute-done.11.refs_1_.refs_0_, bf16[192,768]{1,0:T(8,128)(2,1)S(1)} %get-tuple-element.27.refs_1_.refs_2_, ...), custom_call_target="tpu_custom_call" | custom-call | flops 1509949440 | bytes 4194304 | tf_op jit(solution)/shard_map/first_attention/pallas_call | solution.py:156
  44.2 5.6 %collective-permute-done.7.refs_3_.refs_4_ = bf16[96,768]{1,0:T(8,128)(2,1)S(1)} collective-permute-done((bf16[96,768]{1,0:T(8,128)(2,1)S(1)}, bf16[96,768]{1,0:T(8,128)(2,1)S(1)}, u32[]{:S(2)}, u32[]{:S(2)}) %collective-permute-start.7) | collective-permute-done | bytes 147488 | tf_op jit(solution)/shard_map/ppermute | solution.py:445
  49.8 2.5 %last_attention.4 = (bf16[208,384]{1,0:T(8,128)(2,1)S(1)}, bf16[208,384]{1,0:T(8,128)(2,1)S(1)}) custom-call(bf16[192,384]{1,0:T(8,128)(2,1)S(1)} %collective-permute-done.9.b_ref.refs_0_, bf16[384,384]{1,0:T(8,128)(2,1)S(1)} %collective-permute-done.11.refs_1_.refs_0_, bf16[192,768]{1,0:T(8,128)(2,1)S(1)} %collective-permute-done.2.refs_1_.refs_2_, ...), custom_call_target="tpu_custom_call" | custom-call | flops 1207959552 | bytes 4194304 | tf_op jit(solution)/shard_map/last_attention/pallas_call | solution.py:172
  56.3 2.2 %collective-permute-start.14 = (bf16[208,384]{1,0:T(8,128)(2,1)S(1)}, bf16[208,384]{1,0:T(8,128)(2,1)S(1)}, u32[]{:S(2)}, u32[]{:S(2)}) collective-permute-start(bf16[208,384]{1,0:T(8,128)(2,1)S(1)} %get-tuple-element.40), channel_id=1, source_target_pairs={{0,12},{4,8},{8,4},{12,0},{1,13},{5,9},{9,5},{13,1},{2,14},{6,10},... | collective-permute-start | bytes 479240 | tf_op jit(solution)/shard_map/ppermute | solution.py:441
  58.4 1.7 %first_attention.3 = (f32[192,384]{1,0:T(8,128)S(1)}, f32[192,128]{1,0:T(8,128)S(1)}, f32[192,128]{1,0:T(8,128)S(1)}) custom-call(bf16[192,384]{1,0:T(8,128)(2,1)S(1)} %get-tuple-element.26.refs_0_.a_ref, bf16[192,768]{1,0:T(8,128)(2,1)S(1)} %get-tuple-element.27.refs_1_.refs_2_, bf16[192,768]{1,0:T(8,128)(2,1)S(1)} %collective-permute-done.refs_2_.refs_3_, ...), custom_call_target="tpu_custom_call" | custom-call | flops 754974720 | bytes 4194304 | tf_op jit(solution)/shard_map/first_attention/pallas_call | solution.py:156
  64.2 8.7 %all-gather = bf16[768,384]{1,0:T(8,128)(2,1)S(1)} all-gather(bf16[192,384]{1,0:T(8,128)(2,1)S(1)} %combine.1), channel_id=2, replica_groups=mesh['batch'=2,'z'=8,'y'=4,'xh'=2,'core'=2] {'xh','core'}, dimensions={0}, use_global_device_ids=true | all-gather | bytes 737280 | tf_op jit(solution)/shard_map/all_gather | solution.py:489
  72.8 3.2 %middle.1 = (bf16[192,384]{1,0:T(8,128)(2,1)S(1)}, bf16[192,768]{1,0:T(8,128)(2,1)S(1)}, bf16[16,768]{1,0:T(8,128)(2,1)S(1)}, bf16[16,768]{1,0:T(8,128)(2,1)S(1)}) custom-call(bf16[192,1536]{1,0:T(8,128)(2,1)S(1)} %all_gather.9.rows_ref, bf16[4,192,384]{2,1,0:T(8,128)(2,1)S(1)} %bitcast.1, bf16[384,1536]{1,0:T(8,128)(2,1)S(1)} %copy-done.6, ...), custom_call_target="tpu_custom_call" | custom-call | flops 20000000000 | bytes 1048576 | tf_op jit(solution)/shard_map/middle/pallas_call | solution.py:248
  76.0 5.8 %collective-permute-start.20 = (bf16[16,768]{1,0:T(8,128)(2,1)S(1)}, bf16[16,768]{1,0:T(8,128)(2,1)S(1)}, u32[]{:S(2)}, u32[]{:S(2)}) collective-permute-start(bf16[16,768]{1,0:T(8,128)(2,1)S(1)} %get-tuple-element.43), channel_id=1, source_target_pairs={{0,4},{4,8},{8,12},{12,16},{16,20},{20,24},{24,28},{28,32},{32,36}... | collective-permute-start | bytes 73736 | tf_op jit(solution)/shard_map/ppermute | solution.py:493
  81.8 1.9 %collective-permute-start.21 = (bf16[16,768]{1,0:T(8,128)(2,1)S(1)}, bf16[16,768]{1,0:T(8,128)(2,1)S(1)}, u32[]{:S(2)}, u32[]{:S(2)}) collective-permute-start(bf16[16,768]{1,0:T(8,128)(2,1)S(1)} %get-tuple-element.44), channel_id=1, source_target_pairs={{4,0},{8,4},{12,8},{16,12},{20,16},{24,20},{28,24},{32,28},{36,32}... | collective-permute-start | bytes 73736 | tf_op jit(solution)/shard_map/ppermute | solution.py:494
  85.6 2.2 %collective-permute-start.22 = (bf16[160,384]{1,0:T(8,128)(2,1)S(1)}, bf16[160,384]{1,0:T(8,128)(2,1)S(1)}, u32[]{:S(2)}, u32[]{:S(2)}) collective-permute-start(bf16[160,384]{1,0:T(8,128)(2,1)S(1)} %part_sum.5), channel_id=1, source_target_pairs={{0,2},{2,0},{1,3},{3,1},{4,6},{6,4},{5,7},{7,5},{8,10},{10,8},{9,1... | collective-permute-start | bytes 368648 | tf_op jit(solution)/shard_map/ppermute | solution.py:441
  87.8 1.8 %collective-permute-done.21.after_ref = bf16[16,768]{1,0:T(8,128)(2,1)S(1)} collective-permute-done((bf16[16,768]{1,0:T(8,128)(2,1)S(1)}, bf16[16,768]{1,0:T(8,128)(2,1)S(1)}, u32[]{:S(2)}, u32[]{:S(2)}) %collective-permute-start.21) | collective-permute-done | bytes 24608 | tf_op jit(solution)/shard_map/ppermute | solution.py:494
  90.2 2.2 %collective-permute-start.23 = (bf16[32,384]{1,0:T(8,128)(2,1)S(1)}, bf16[32,384]{1,0:T(8,128)(2,1)S(1)}, u32[]{:S(2)}, u32[]{:S(2)}) collective-permute-start(bf16[32,384]{1,0:T(8,128)(2,1)S(1)} %get-tuple-element.46), channel_id=1, source_target_pairs={{0,2},{2,0},{1,3},{3,1},{4,6},{6,4},{5,7},{7,5},{8,10},{10,8},{9,1... | collective-permute-start | bytes 73736 | tf_op jit(solution)/shard_map/ppermute | solution.py:441
  92.9 2.7 %collective-permute-done.23.edges_ref = bf16[32,384]{1,0:T(8,128)(2,1)S(1)} collective-permute-done((bf16[32,384]{1,0:T(8,128)(2,1)S(1)}, bf16[32,384]{1,0:T(8,128)(2,1)S(1)}, u32[]{:S(2)}, u32[]{:S(2)}) %collective-permute-start.23) | collective-permute-done | bytes 24608 | tf_op jit(solution)/shard_map/ppermute | solution.py:441
  (62 shorter events, 17.0 us)
Async XLA Ops:
  0.0 35.3 %collective-permute-start.6 = (bf16[2,1536,384]{2,1,0:T(8,128)(2,1)}, bf16[2,1536,384]{2,1,0:T(8,128)(2,1)S(1)}, u32[]{:S(2)}, u32[]{:S(2)}) collective-permute-start(bf16[2,1536,384]{2,1,0:T(8,128)(2,1)} %glu_ref.1), channel_id=1, source_target_pairs={{0,1},{1,0},{2,3},{3,2},{4,5},{5,4},{6,7},{7,6},{8,9},{9,8},{10,11... | collective-permute-start | bytes 7077896 | tf_op jit(solution)/shard_map/ppermute | solution.py:441
  0.0 25.6 %collective-permute-start.10 = (bf16[384,1536]{1,0:T(8,128)(2,1)}, bf16[384,1536]{1,0:T(8,128)(2,1)S(1)}, u32[]{:S(2)}, u32[]{:S(2)}) collective-permute-start(bf16[384,1536]{1,0:T(8,128)(2,1)} %w0.1), channel_id=1, source_target_pairs={{0,1},{1,0},{2,3},{3,2},{4,5},{5,4},{6,7},{7,6},{8,9},{9,8},{10,11... | collective-permute-start | bytes 3538952 | tf_op jit(solution)/shard_map/ppermute | solution.py:441
  11.6 6.2 %collective-permute-start.9 = (bf16[192,384]{1,0:T(8,128)(2,1)S(1)}, bf16[192,384]{1,0:T(8,128)(2,1)S(1)}, u32[]{:S(2)}, u32[]{:S(2)}) collective-permute-start(bf16[192,384]{1,0:T(8,128)(2,1)S(1)} %get-tuple-element.26.refs_0_.a_ref), channel_id=1, source_target_pairs={{0,4},{4,0},{8,12},{12,8},{1,5},{5,1},{9,13},{13,9},{2,6},{6,2},{1... | collective-permute-start | bytes 442376 | tf_op jit(solution)/shard_map/ppermute | solution.py:441
  12.4 9.0 %collective-permute-start = (bf16[192,768]{1,0:T(8,128)(2,1)S(1)}, bf16[192,768]{1,0:T(8,128)(2,1)S(1)}, u32[]{:S(2)}, u32[]{:S(2)}) collective-permute-start(bf16[192,768]{1,0:T(8,128)(2,1)S(1)} %get-tuple-element.27.refs_1_.refs_2_), channel_id=1, source_target_pairs={{0,16},{16,32},{32,48},{48,64},{64,80},{80,96},{96,112},{112,0},{1... | collective-permute-start | bytes 884744 | tf_op jit(solution)/shard_map/ppermute | solution.py:445
  14.4 9.0 %collective-permute-start.3 = (bf16[192,768]{1,0:T(8,128)(2,1)S(1)}, bf16[192,768]{1,0:T(8,128)(2,1)S(1)}, u32[]{:S(2)}, u32[]{:S(2)}) collective-permute-start(bf16[192,768]{1,0:T(8,128)(2,1)S(1)} %get-tuple-element.27.refs_1_.refs_2_), channel_id=1, source_target_pairs={{0,112},{16,0},{32,16},{48,32},{64,48},{80,64},{96,80},{112,96},{1... | collective-permute-start | bytes 884744 | tf_op jit(solution)/shard_map/ppermute | solution.py:445
  17.8 44.7 %collective-permute-start.17 = (bf16[384,1536]{1,0:T(8,128)(2,1)S(1)}, bf16[384,1536]{1,0:T(8,128)(2,1)S(1)}, u32[]{:S(2)}, u32[]{:S(2)}) collective-permute-start(bf16[384,1536]{1,0:T(8,128)(2,1)S(1)} %copy-done.6), channel_id=1, source_target_pairs={{0,2},{2,0},{1,3},{3,1},{4,6},{6,4},{5,7},{7,5},{8,10},{10,8},{9,1... | collective-permute-start | bytes 3538952 | tf_op jit(solution)/shard_map/ppermute | solution.py:441
  21.4 10.9 %collective-permute-start.1 = (bf16[192,768]{1,0:T(8,128)(2,1)S(1)}, bf16[192,768]{1,0:T(8,128)(2,1)S(1)}, u32[]{:S(2)}, u32[]{:S(2)}) collective-permute-start(bf16[192,768]{1,0:T(8,128)(2,1)S(1)} %collective-permute-done.refs_2_.refs_3_), channel_id=1, source_target_pairs={{0,16},{16,32},{32,48},{48,64},{64,80},{80,96},{96,112},{112,0},{1... | collective-permute-start | bytes 884744 | tf_op jit(solution)/shard_map/ppermute | solution.py:445
  23.4 9.4 %collective-permute-start.4 = (bf16[192,768]{1,0:T(8,128)(2,1)S(1)}, bf16[192,768]{1,0:T(8,128)(2,1)S(1)}, u32[]{:S(2)}, u32[]{:S(2)}) collective-permute-start(bf16[192,768]{1,0:T(8,128)(2,1)S(1)} %collective-permute-done.3.refs_3_.refs_4_), channel_id=1, source_target_pairs={{0,112},{16,0},{32,16},{48,32},{64,48},{80,64},{96,80},{112,96},{1... | collective-permute-start | bytes 884744 | tf_op jit(solution)/shard_map/ppermute | solution.py:445
  25.7 12.8 %collective-permute-start.11 = (bf16[384,384]{1,0:T(8,128)(2,1)S(1)}, bf16[384,384]{1,0:T(8,128)(2,1)S(1)}, u32[]{:S(2)}, u32[]{:S(2)}) collective-permute-start(bf16[384,384]{1,0:T(8,128)(2,1)S(1)} %join.1), channel_id=1, source_target_pairs={{0,8},{4,12},{8,0},{12,4},{1,9},{5,13},{9,1},{13,5},{2,10},{6,14},... | collective-permute-start | bytes 884744 | tf_op jit(solution)/shard_map/ppermute | solution.py:441
  32.4 11.8 %collective-permute-start.2 = (bf16[192,768]{1,0:T(8,128)(2,1)S(1)}, bf16[192,768]{1,0:T(8,128)(2,1)S(1)}, u32[]{:S(2)}, u32[]{:S(2)}) collective-permute-start(bf16[192,768]{1,0:T(8,128)(2,1)S(1)} %collective-permute-done.1.a_ref.refs_4_.refs_5_), channel_id=1, source_target_pairs={{0,16},{16,32},{32,48},{48,64},{64,80},{80,96},{96,112},{112,0},{1... | collective-permute-start | bytes 884744 | tf_op jit(solution)/shard_map/ppermute | solution.py:445
  32.8 11.4 %collective-permute-start.5 = (bf16[192,768]{1,0:T(8,128)(2,1)S(1)}, bf16[192,768]{1,0:T(8,128)(2,1)S(1)}, u32[]{:S(2)}, u32[]{:S(2)}) collective-permute-start(bf16[192,768]{1,0:T(8,128)(2,1)S(1)} %collective-permute-done.4.b_ref.refs_5_.refs_6_), channel_id=1, source_target_pairs={{0,112},{16,0},{32,16},{48,32},{64,48},{80,64},{96,80},{112,96},{1... | collective-permute-start | bytes 884744 | tf_op jit(solution)/shard_map/ppermute | solution.py:445
  35.4 14.5 %collective-permute-start.7 = (bf16[96,768]{1,0:T(8,128)(2,1)S(1)}, bf16[96,768]{1,0:T(8,128)(2,1)S(1)}, u32[]{:S(2)}, u32[]{:S(2)}) collective-permute-start(bf16[96,768]{1,0:T(8,128)(2,1)S(1)} %get-tuple-element.28), channel_id=1, source_target_pairs={{0,32},{16,48},{32,64},{48,80},{64,96},{80,112},{96,0},{112,16},{1... | collective-permute-start | bytes 442376 | tf_op jit(solution)/shard_map/ppermute | solution.py:445
  38.5 11.3 %collective-permute-start.8 = (bf16[96,768]{1,0:T(8,128)(2,1)S(1)}, bf16[96,768]{1,0:T(8,128)(2,1)S(1)}, u32[]{:S(2)}, u32[]{:S(2)}) collective-permute-start(bf16[96,768]{1,0:T(8,128)(2,1)S(1)} %get-tuple-element.29), channel_id=1, source_target_pairs={{0,96},{16,112},{32,0},{48,16},{64,32},{80,48},{96,64},{112,80},{1... | collective-permute-start | bytes 442376 | tf_op jit(solution)/shard_map/ppermute | solution.py:445
  52.3 10.7 %collective-permute-start.12 = (bf16[208,384]{1,0:T(8,128)(2,1)S(1)}, bf16[208,384]{1,0:T(8,128)(2,1)S(1)}, u32[]{:S(2)}, u32[]{:S(2)}) collective-permute-start(bf16[208,384]{1,0:T(8,128)(2,1)S(1)} %get-tuple-element.36), channel_id=1, source_target_pairs={{0,4},{4,0},{8,12},{12,8},{1,5},{5,1},{9,13},{13,9},{2,6},{6,2},{1... | collective-permute-start | bytes 479240 | tf_op jit(solution)/shard_map/ppermute | solution.py:441
  54.9 8.0 %collective-permute-start.13 = (bf16[208,384]{1,0:T(8,128)(2,1)S(1)}, bf16[208,384]{1,0:T(8,128)(2,1)S(1)}, u32[]{:S(2)}, u32[]{:S(2)}) collective-permute-start(bf16[208,384]{1,0:T(8,128)(2,1)S(1)} %last_attention.5), channel_id=1, source_target_pairs={{0,8},{4,12},{8,0},{12,4},{1,9},{5,13},{9,1},{13,5},{2,10},{6,14},... | collective-permute-start | bytes 479240 | tf_op jit(solution)/shard_map/ppermute | solution.py:441
  56.3 7.2 %collective-permute-start.14 = (bf16[208,384]{1,0:T(8,128)(2,1)S(1)}, bf16[208,384]{1,0:T(8,128)(2,1)S(1)}, u32[]{:S(2)}, u32[]{:S(2)}) collective-permute-start(bf16[208,384]{1,0:T(8,128)(2,1)S(1)} %get-tuple-element.40), channel_id=1, source_target_pairs={{0,12},{4,8},{8,4},{12,0},{1,13},{5,9},{9,5},{13,1},{2,14},{6,10},... | collective-permute-start | bytes 479240 | tf_op jit(solution)/shard_map/ppermute | solution.py:441
  58.4 1.7 %collective-permute-start.16 = (f32[384]{0:T(512)S(1)}, f32[384]{0:T(512)S(1)}, u32[]{:S(2)}, u32[]{:S(2)}) collective-permute-start(f32[384]{0:T(512)S(1)} %copy-done.4), channel_id=1, source_target_pairs={{0,1},{1,0},{2,3},{3,2},{4,5},{5,4},{6,7},{7,6},{8,9},{9,8},{10,11... | collective-permute-start | bytes 4616 | tf_op jit(solution)/shard_map/ppermute | solution.py:441
  60.2 2.2 %collective-permute-start.15 = (bf16[31,384]{1,0:T(8,128)(2,1)S(1)}, bf16[31,384]{1,0:T(8,128)(2,1)S(1)}, u32[]{:S(2)}, u32[]{:S(2)}) collective-permute-start(bf16[31,384]{1,0:T(8,128)(2,1)S(1)} %copy-done.2), channel_id=1, source_target_pairs={{0,1},{1,0},{2,3},{3,2},{4,5},{5,4},{6,7},{7,6},{8,9},{9,8},{10,11... | collective-permute-start | bytes 71432 | tf_op jit(solution)/shard_map/ppermute | solution.py:441
  62.4 22.9 %collective-permute-start.19 = (bf16[384,1536]{1,0:T(8,128)(2,1)S(1)}, bf16[384,1536]{1,0:T(8,128)(2,1)S(1)}, u32[]{:S(2)}, u32[]{:S(2)}) collective-permute-start(bf16[384,1536]{1,0:T(8,128)(2,1)S(1)} %copy-done), channel_id=1, source_target_pairs={{0,1},{1,0},{2,3},{3,2},{4,5},{5,4},{6,7},{7,6},{8,9},{9,8},{10,11... | collective-permute-start | bytes 3538952 | tf_op jit(solution)/shard_map/ppermute | solution.py:441
  62.5 10.4 %collective-permute-start.18 = (bf16[384,1536]{1,0:T(8,128)(2,1)S(1)}, bf16[384,1536]{1,0:T(8,128)(2,1)S(1)}, u32[]{:S(2)}, u32[]{:S(2)}) collective-permute-start(bf16[384,1536]{1,0:T(8,128)(2,1)S(1)} %collective-permute-done.17.w2), channel_id=1, source_target_pairs={{0,1},{1,0},{2,3},{3,2},{4,5},{5,4},{6,7},{7,6},{8,9},{9,8},{10,11... | collective-permute-start | bytes 3538952 | tf_op jit(solution)/shard_map/ppermute | solution.py:441
  76.0 11.8 %collective-permute-start.20 = (bf16[16,768]{1,0:T(8,128)(2,1)S(1)}, bf16[16,768]{1,0:T(8,128)(2,1)S(1)}, u32[]{:S(2)}, u32[]{:S(2)}) collective-permute-start(bf16[16,768]{1,0:T(8,128)(2,1)S(1)} %get-tuple-element.43), channel_id=1, source_target_pairs={{0,4},{4,8},{8,12},{12,16},{16,20},{20,24},{24,28},{28,32},{32,36}... | collective-permute-start | bytes 73736 | tf_op jit(solution)/shard_map/ppermute | solution.py:493
  81.8 7.8 %collective-permute-start.21 = (bf16[16,768]{1,0:T(8,128)(2,1)S(1)}, bf16[16,768]{1,0:T(8,128)(2,1)S(1)}, u32[]{:S(2)}, u32[]{:S(2)}) collective-permute-start(bf16[16,768]{1,0:T(8,128)(2,1)S(1)} %get-tuple-element.44), channel_id=1, source_target_pairs={{4,0},{8,4},{12,8},{16,12},{20,16},{24,20},{28,24},{32,28},{36,32}... | collective-permute-start | bytes 73736 | tf_op jit(solution)/shard_map/ppermute | solution.py:494
  85.6 10.0 %collective-permute-start.22 = (bf16[160,384]{1,0:T(8,128)(2,1)S(1)}, bf16[160,384]{1,0:T(8,128)(2,1)S(1)}, u32[]{:S(2)}, u32[]{:S(2)}) collective-permute-start(bf16[160,384]{1,0:T(8,128)(2,1)S(1)} %part_sum.5), channel_id=1, source_target_pairs={{0,2},{2,0},{1,3},{3,1},{4,6},{6,4},{5,7},{7,5},{8,10},{10,8},{9,1... | collective-permute-start | bytes 368648 | tf_op jit(solution)/shard_map/ppermute | solution.py:441
  90.2 5.4 %collective-permute-start.23 = (bf16[32,384]{1,0:T(8,128)(2,1)S(1)}, bf16[32,384]{1,0:T(8,128)(2,1)S(1)}, u32[]{:S(2)}, u32[]{:S(2)}) collective-permute-start(bf16[32,384]{1,0:T(8,128)(2,1)S(1)} %get-tuple-element.46), channel_id=1, source_target_pairs={{0,2},{2,0},{1,3},{3,1},{4,6},{6,4},{5,7},{7,5},{8,10},{10,8},{9,1... | collective-permute-start | bytes 73736 | tf_op jit(solution)/shard_map/ppermute | solution.py:441
  (9 other events, 61.6 us)
